TPU v7x, 512 devices: a whole 4x4x16 slice. The times are simulated.
512 devices in a mesh: pitch: 32 (over x_hi, z), chan: 16 (over x_lo, y, core).
Axes of the slice: x: 4 (x_hi: 2, x_lo: 2; x = x_hi * 2 + x_lo), y: 4, z: 16, core: 2. Of those that a mesh axis runs over, the one named last changes fastest.
Arguments:
- activation: bfloat16 [32, 1024, 4096], P(None, 'chan', 'pitch'), may hold values from -6 to 6
- cotangent: bfloat16 [32, 1024, 4096], P(None, 'chan', 'pitch'), may hold values from -6 to 6
- spectral_weight: bfloat16 [128, 2, 1024, 1024], P('pitch', None, 'chan'), may hold values from -0.5 to 0.5
- out_bias: float32 [1024], P('chan'), may hold values from -3 to 3
Outputs:
- grad_input: bfloat16 [32, 1024, 4096], P(None, 'chan', 'pitch')
- grad_weight: float32 [128, 2, 1024, 1024], P('pitch', None, 'chan')
- grad_bias: float32 [1024], P('chan')
All inputs are finite; a program needn't handle non-finite values.
Results may differ from a plain program's by a relative error of at most 0.025.
Values may be sent and summed in bfloat16 or wider, within the bound.
No kernel may reach another device: no remote copies, remote signals or barrier semaphores. Data moves between devices by JAX's collectives and lax.ppermute only.
A program may use at most 64 MiB of HBM per device.

v0:
```python
import math

import jax
import jax.numpy as jnp
from jax import lax
from jax.sharding import PartitionSpec as P

P_SIZE = 4096
M = 128


highest = lax.Precision.HIGHEST


def spectral_table(mode_count, point_count, doubled):
    mode_ids = jnp.arange(mode_count, dtype=jnp.int32)
    point_ids = jnp.arange(point_count, dtype=jnp.int32)
    product = mode_ids[:, None] * point_ids[None, :] % P_SIZE
    angles = product.astype(jnp.float32) * (2.0 * math.pi / P_SIZE)
    factor = jnp.full((mode_count,), 1.0 / math.sqrt(P_SIZE), jnp.float32)
    if doubled:
        factor = jnp.where(mode_ids == 0, factor, 2.0 * factor)
    stacked = jnp.stack([jnp.cos(angles), -jnp.sin(angles)], axis=1) * factor[:, None, None]
    return stacked.reshape(2 * mode_count, point_count)


def activate(values):
    return jax.nn.gelu(values, approximate=True)


def contract(form, left, right):
    return jnp.einsum(form, left, right, preferred_element_type=jnp.float32)


def to_modes(grid_field, doubled):
    chan_width = grid_field.shape[1]
    spanwise = lax.all_to_all(grid_field, "pitch", split_axis=0, concat_axis=2, tiled=True)
    span_part = spanwise.shape[0]
    basis = spectral_table(M, P_SIZE, doubled)
    result = jnp.einsum("scp,jp->jsc", spanwise.astype(jnp.float32), basis, precision=highest)
    packed = result.reshape(M, 2, span_part, chan_width).astype(jnp.bfloat16)
    return lax.all_to_all(packed, "pitch", split_axis=0, concat_axis=2, tiled=True)


def to_points(spectra, doubled):
    chan_width = spectra.shape[3]
    spanwise = lax.all_to_all(spectra, "pitch", split_axis=2, concat_axis=0, tiled=True)
    span_part = spanwise.shape[2]
    basis = spectral_table(M, P_SIZE, doubled)
    flattened = spanwise.astype(jnp.float32).reshape(2 * M, span_part, chan_width)
    result = jnp.einsum("jsc,jp->scp", flattened, basis, precision=highest)
    grid_field = result.astype(jnp.bfloat16)
    return lax.all_to_all(grid_field, "pitch", split_axis=2, concat_axis=0, tiled=True)


def body(activation, cotangent, spectral_weight, out_bias):
    spectra = to_modes(activation, False)
    gathered = lax.all_gather(spectra, "chan", axis=3, tiled=True)
    real_in = gathered[:, 0]
    imag_in = gathered[:, 1]
    weight_re = spectral_weight[:, 0]
    weight_im = spectral_weight[:, 1]
    mixed_re = contract("ksi,koi->kso", real_in, weight_re) - contract(
        "ksi,koi->kso", imag_in, weight_im
    )
    mixed_im = contract("ksi,koi->kso", real_in, weight_im) + contract(
        "ksi,koi->kso", imag_in, weight_re
    )
    mixed = jnp.stack([mixed_re, mixed_im], axis=1).astype(jnp.bfloat16)
    response = to_points(mixed, True)
    pre_act = lax.optimization_barrier(response).astype(jnp.float32) + out_bias[None, :, None]
    tangent = cotangent.astype(jnp.float32)
    unused_out, pullback = jax.vjp(activate, pre_act)
    grad_pre = pullback(tangent)[0]
    grad_bias = lax.psum(jnp.sum(grad_pre, axis=(0, 2)), "pitch")
    grad_modes = to_modes(grad_pre.astype(jnp.bfloat16), True)
    grad_re = grad_modes[:, 0]
    grad_im = grad_modes[:, 1]
    weight_grad_re = contract("ksi,kso->koi", real_in, grad_re) + contract(
        "ksi,kso->koi", imag_in, grad_im
    )
    weight_grad_im = contract("ksi,kso->koi", real_in, grad_im) - contract(
        "ksi,kso->koi", imag_in, grad_re
    )
    grad_weight = jnp.stack([weight_grad_re, weight_grad_im], axis=1)
    back_re = contract("koi,kso->ksi", weight_re, grad_re) + contract(
        "koi,kso->ksi", weight_im, grad_im
    )
    back_im = contract("koi,kso->ksi", weight_re, grad_im) - contract(
        "koi,kso->ksi", weight_im, grad_re
    )
    partial_back = jnp.stack([back_re, back_im], axis=1)
    input_modes = lax.psum_scatter(
        partial_back.astype(jnp.bfloat16), "chan", scatter_dimension=3, tiled=True
    )
    spatial = to_points(input_modes, False)
    grad_input = (tangent + lax.optimization_barrier(spatial).astype(jnp.float32)).astype(
        jnp.bfloat16
    )
    return (grad_input, grad_weight, grad_bias)


def solution(mesh):
    placed = (
        P(None, "chan", "pitch"),
        P(None, "chan", "pitch"),
        P("pitch", None, "chan", None),
        P("chan"),
    )
    return jax.shard_map(
        body,
        mesh=mesh,
        in_specs=placed,
        out_specs=(P(None, "chan", "pitch"), P("pitch", None, "chan", None), P("chan")),
        check_vma=False,
    )
```

profile of v0, /device:TPU:24, one launch (start us, length us, event | category | flops | bytes accessed | tf_op | source)
XLA Modules:
  0.0 545.1 jit_solution(567413910694297759)
XLA Ops:
  7.2 17.9 %all-to-all-start = ((bf16[32,64,128]{2,1,0:T(8,128)(2,1)}), bf16[32,64,128]{2,1,0:T(8,128)(2,1)S(1)}, u32[]{:S(2)}, u32[]{:S(2)}) async-start(bf16[32,64,128]{2,1,0:T(8,128)(2,1)} %param.4), calls=%async_computation | async-start | bytes 1048576 | tf_op jit(solution)/shard_map/all_to_all | solution.py:37
  25.1 9.1 %sine_negate_fusion = (f32[128,1,4096]{2,0,1:T(8,128)S(1)}, f32[128,1,4096]{2,0,1:T(8,128)}) fusion(), kind=kLoop, calls=%fused_computation.14 | loop fusion | flops 7864320 | bytes 4194304 | tf_op jit(solution)/shard_map/neg | solution.py:23
  34.2 23.6 %all-to-all-done = bf16[32,64,128]{2,1,0:T(8,128)(2,1)S(1)} async-done(((bf16[32,64,128]{2,1,0:T(8,128)(2,1)}), bf16[32,64,128]{2,1,0:T(8,128)(2,1)S(1)}, u32[]{:S(2)}, u32[]{:S(2)}) %all-to-all-start) | async-done | bytes 524320 | tf_op jit(solution)/shard_map/all_to_all | solution.py:37
  58.4 3.9 fusion.18
  62.5 0.7 reshape.192
  63.2 5.2 all-to-all-start.1
  68.4 15.2 %all-to-all-done.1 = bf16[32,2,256]{2,1,0:T(2,128)(2,1)S(1)} async-done(((bf16[32,2,256]{2,1,0:T(2,128)(2,1)}), bf16[32,2,256]{2,1,0:T(2,128)(2,1)S(1)}, u32[]{:S(2)}, u32[]{:S(2)}) %all-to-all-start.1) | async-done | bytes 32800 | tf_op jit(solution)/shard_map/all_to_all | solution.py:42
  83.9 22.2 %all-gather = bf16[4,2,32,1,1024]{2,0,3,1,4:T(4,128)(2,1)} all-gather(bf16[4,2,32,1,64]{2,0,3,1,4:T(4,128)(2,1)S(1)} %copy.80), channel_id=2, replica_groups=mesh['pitch'=32,'chan'=16] {'chan'}, dimensions={4}, use_global_device_ids=true | all-gather | bytes 557056 | tf_op jit(solution)/shard_map/all_gather | solution.py:58
  106.1 2.9 copy.81
  109.0 1.4 fusion.43
  110.4 1.3 fusion.35
  111.7 1.3 fusion.21
  114.1 3.9 all-to-all-start.2
  118.0 4.2 fusion.2
  122.2 2.0 copy-done
  124.1 5.2 copy.86
  129.3 6.3 %mul.168 = f32[256,4096]{1,0:T(8,128)} reshape(f32[128,2,4096]{2,1,0:T(2,128)} %copy.86) | data formatting | bytes 8388608 | tf_op jit(solution)/shard_map/mul | solution.py:23
  135.8 3.9 fusion
  139.8 2.8 copy.87
  143.1 23.4 %reduce = bf16[4096,64]{1,0:T(8,128)(2,1)} reduce(bf16[4096,1,64]{2,1,0:T(2,128)(2,1)S(1)} %bitcast.145, bf16[]{:T(256)} %broadcast.219), dimensions={1}, to_apply=%bitcast.118.reduce_sub_computation | reduce | bytes 1048578
  166.4 2.3 reshape.196
  168.8 47.3 %all_to_all.132 = bf16[32,2,4096]{2,1,0:T(2,128)(2,1)S(1)} all-to-all(bf16[32,2,4096]{2,1,0:T(2,128)(2,1)S(1)} %reshape.196), channel_id=1, replica_groups=mesh['pitch'=32,'chan'=16] {'pitch'}, dimensions={0} | all-to-all | bytes 1048576 | tf_op jit(solution)/shard_map/all_to_all | solution.py:53
  216.1 1.2 reshape.197
  217.3 2.3 copy.88
  219.8 0.9 copy-done.3
  220.6 1.4 fusion.56
  222.3 50.0 %all_to_all.133 = bf16[32,64,128]{2,1,0:T(8,128)(2,1)S(1)} all-to-all(bf16[32,64,128]{2,1,0:T(8,128)(2,1)S(1)} %copy.89), channel_id=1, replica_groups=mesh['pitch'=32,'chan'=16] {'pitch'}, dimensions={0} | all-to-all | bytes 1048576 | tf_op jit(solution)/shard_map/all_to_all | solution.py:37
  272.9 4.6 fusion.19
  277.7 20.2 %all_to_all.134 = bf16[32,2,256]{2,1,0:T(2,128)(2,1)S(1)} all-to-all(bf16[32,2,256]{2,1,0:T(2,128)(2,1)S(1)} %reshape.198), channel_id=1, replica_groups=mesh['pitch'=32,'chan'=16] {'pitch'}, dimensions={0} | all-to-all | bytes 65536 | tf_op jit(solution)/shard_map/all_to_all | solution.py:42
  299.0 1.4 copy.103
  300.4 2.2 reshape.190
  302.6 55.2 %reduce-scatter.4.cloned.1.call-done = bf16[64,256]{1,0:T(8,128)(2,1)} async-done(((bf16[1024,256]{1,0:T(8,128)(2,1)}), bf16[64,256]{1,0:T(8,128)(2,1)}) %reduce-scatter.4.cloned.1.call-update) | async-done | bytes 32784
  357.8 0.9 reshape.191
  358.8 0.7 reshape.200
  359.6 15.0 %all-to-all-start.6 = ((bf16[32,2,256]{2,1,0:T(2,128)(2,1)}), bf16[32,2,256]{2,1,0:T(2,128)(2,1)S(1)}, u32[]{:S(2)}, u32[]{:S(2)}) async-start(bf16[32,2,256]{2,1,0:T(2,128)(2,1)} %reshape.200), calls=%async_computation.6 | async-start | bytes 65536 | tf_op jit(solution)/shard_map/all_to_all | solution.py:47
  374.6 7.4 %copy.96 = f32[128,2,4096]{2,1,0:T(2,128)} copy(f32[128,2,4096]{2,0,1:T(8,128)} %get-tuple-element.20) | data formatting | bytes 8388608 | tf_op jit(solution)/shard_map/mul | solution.py:23
  382.0 6.1 %mul.183 = f32[256,4096]{1,0:T(8,128)} reshape(f32[128,2,4096]{2,1,0:T(2,128)} %copy.96) | data formatting | bytes 8388608 | tf_op jit(solution)/shard_map/mul | solution.py:23
  388.0 1.8 all-to-all-done.6
  390.0 3.9 fusion.1
  393.9 2.8 copy.97
  396.7 23.4 %reduce.1 = bf16[4096,64]{1,0:T(8,128)(2,1)} reduce(bf16[4096,1,64]{2,1,0:T(2,128)(2,1)S(1)} %bitcast.146, bf16[]{:T(256)} %broadcast.219), dimensions={1}, to_apply=%bitcast.124.reduce_sub_computation | reduce | bytes 1048578
  420.1 3.2 reshape.202
  423.3 12.9 %all-to-all-start.7 = ((bf16[32,2,4096]{2,1,0:T(2,128)(2,1)}), bf16[32,2,4096]{2,1,0:T(2,128)(2,1)S(1)}, u32[]{:S(2)}, u32[]{:S(2)}) async-start(bf16[32,2,4096]{2,1,0:T(2,128)(2,1)} %reshape.202), calls=%async_computation.7 | async-start | bytes 1048576 | tf_op jit(solution)/shard_map/all_to_all | solution.py:53
  436.2 93.7 %psum.7 = f32[64]{0:T(128)} all-reduce(f32[64]{0:T(128)S(1)} %get-tuple-element.18), channel_id=1, replica_groups=mesh['pitch'=32,'chan'=16] {'pitch'}, use_global_device_ids=true, to_apply=%region_2.3 | all-reduce | flops 64 | bytes 512 | tf_op jit(solution)/shard_map/psum | solution.py:75
  531.5 1.5 copy.100
  533.0 1.2 reshape.203
  534.2 2.3 copy.98
  537.0 1.0 copy.99
  (55 shorter events, 7.4 us)
Async XLA Ops:
  7.2 50.7 %all-to-all-start = ((bf16[32,64,128]{2,1,0:T(8,128)(2,1)}), bf16[32,64,128]{2,1,0:T(8,128)(2,1)S(1)}, u32[]{:S(2)}, u32[]{:S(2)}) async-start(bf16[32,64,128]{2,1,0:T(8,128)(2,1)} %param.4), calls=%async_computation | async-start | bytes 1048576 | tf_op jit(solution)/shard_map/all_to_all | solution.py:37
  63.2 20.4 %all-to-all-start.1 = ((bf16[32,2,256]{2,1,0:T(2,128)(2,1)}), bf16[32,2,256]{2,1,0:T(2,128)(2,1)S(1)}, u32[]{:S(2)}, u32[]{:S(2)}) async-start(bf16[32,2,256]{2,1,0:T(2,128)(2,1)} %reshape.192), calls=%async_computation.1 | async-start | bytes 65536 | tf_op jit(solution)/shard_map/all_to_all | solution.py:42
  109.0 4.0 copy-start.1
  114.1 21.5 %all-to-all-start.2 = ((bf16[32,2,256]{2,1,0:T(2,128)(2,1)}), bf16[32,2,256]{2,1,0:T(2,128)(2,1)S(1)}, u32[]{:S(2)}, u32[]{:S(2)}) async-start(bf16[32,2,256]{2,1,0:T(2,128)(2,1)} %reshape.194), calls=%async_computation.2 | async-start | bytes 65536 | tf_op jit(solution)/shard_map/all_to_all | solution.py:47
  117.9 239.8 %reduce-scatter.4.cloned.1.call-start = ((), (), s32[]{:S(2)}) async-start(), calls=%async_computation.9 | async-start | bytes 557056
  122.2 2.0 copy-start
  217.3 2.5 copy-start.5
  219.6 1.0 copy-start.3
  272.9 25.2 %copy-start.2 = (bf16[4,2,64,1024]{3,2,1,0:T(8,128)(2,1)S(1)}, bf16[4,2,64,1024]{3,2,1,0:T(8,128)(2,1)}, u32[]{:S(2)}) copy-start(bf16[4,2,64,1024]{3,2,1,0:T(8,128)(2,1)} %param.6) | copy-start | bytes 3145732
  359.6 30.2 %all-to-all-start.6 = ((bf16[32,2,256]{2,1,0:T(2,128)(2,1)}), bf16[32,2,256]{2,1,0:T(2,128)(2,1)S(1)}, u32[]{:S(2)}, u32[]{:S(2)}) async-start(bf16[32,2,256]{2,1,0:T(2,128)(2,1)} %reshape.200), calls=%async_computation.6 | async-start | bytes 65536 | tf_op jit(solution)/shard_map/all_to_all | solution.py:47
  423.3 109.7 %all-to-all-start.7 = ((bf16[32,2,4096]{2,1,0:T(2,128)(2,1)}), bf16[32,2,4096]{2,1,0:T(2,128)(2,1)S(1)}, u32[]{:S(2)}, u32[]{:S(2)}) async-start(bf16[32,2,4096]{2,1,0:T(2,128)(2,1)} %reshape.202), calls=%async_computation.7 | async-start | bytes 1048576 | tf_op jit(solution)/shard_map/all_to_all | solution.py:53
  534.2 2.4 copy-start.4
Sparse Core Ops, SparseCore 0:
  302.7 55.0 reduce-scatter.3
where the time goes:
time: 548 us; the launch traced here: 545 us
  blocking collectives  233 us (43%)
  waiting for transfers between devices  95.8 us (17%)
  other arithmetic  62.1 us (11%)
  local copies, waits for them, and re-layouts  61.3 us (11%)
  starting transfers between devices  54.9 us (10%)
  matrix products  22.9 us (4%)
  between operations  14.7 us (3%)
    psum x1, blocking collectives, body(): grad_bias = lax.psum(jnp.sum(grad_pre, axis=(0, 2)), 'pitch')  93.7 us
    unnamed x2, waiting for transfers between devices  55.2 us
    all_to_all x1, blocking collectives, to_modes(): lax.all_to_all(grid_field, 'pitch', split_axis=0, concat_axis=2, tiled=True)  50 us
    all_to_all x1, blocking collectives, to_points(): lax.all_to_all(grid_field, 'pitch', split_axis=2, concat_axis=0, tiled=True)  47.3 us
    unnamed x2, other arithmetic  46.8 us
    mul x4, local copies, waits for them, and re-layouts, spectral_table(): jnp.stack([jnp.cos(angles), -jnp.sin(angles)], axis=1)  24.9 us
    all_to_all x1, waiting for transfers between devices, to_modes(): lax.all_to_all(grid_field, 'pitch', split_axis=0, concat_axis=2, tiled=True)  23.6 us
    all_gather x1, blocking collectives, body(): gathered = lax.all_gather(spectra, 'chan', axis=3, tiled=True)  22.2 us
  transfers between devices with their start and end apart: 6, of which 4 were waited for; matrix products, arithmetic and copies ran while one was open for 8% of the time, Pallas kernels for 0%

commit v1 on v0

v1 whole, which is shorter than its diff:
```python
import functools
import math

import jax
import jax.numpy as jnp
import ml_dtypes
import numpy as np
from jax import lax
from jax.experimental import pallas as pl
from jax.experimental.pallas import tpu as pltpu
from jax.sharding import Mesh
from jax.sharding import PartitionSpec as P

P_SIZE = 4096
M = 128
R = 24
RB = 32
XH = 2
Z = 16
WIN = P_SIZE // (XH * Z)
f32 = jnp.float32
bf16 = jnp.bfloat16
NT = (((1,), (1,)), ((), ()))
NN = (((1,), (0,)), ((), ()))
TN = (((0,), (0,)), ((), ()))
VMEM_LIMIT = 24 * 1024 * 1024


def split_hi_lo(table):
    hi = table.astype(ml_dtypes.bfloat16)
    lo = (table - hi.astype(np.float64)).astype(ml_dtypes.bfloat16)
    return hi, lo


@functools.cache
def tables():
    modes = np.arange(M)
    points = np.arange(P_SIZE)
    angle = 2.0 * math.pi * (np.outer(modes, points) % P_SIZE) / P_SIZE
    forward = np.stack([np.cos(angle), -np.sin(angle)], axis=1).reshape(2 * M, P_SIZE) / math.sqrt(P_SIZE)
    scale = np.repeat(np.where(modes == 0, 1.0, 2.0), 2)[:, None]
    basis = np.linalg.svd(forward[:, :WIN])[2][:R]
    windows = forward.reshape(2 * M, XH * Z, WIN)
    coef = np.einsum("jwp,rp->wjr", windows, basis)
    out = {}
    hi, lo = split_hi_lo(basis)
    out["points"] = np.concatenate([hi, lo], axis=0)
    out["expand"] = np.concatenate([hi, lo, hi], axis=0)
    for name, factor, rows in (("plain", 1.0, R), ("doubled", scale, RB)):
        part = np.zeros((XH * Z, 2 * M, rows))
        part[:, :, :R] = coef * factor
        part = part.reshape(XH, Z, XH, 2 * M // XH, rows)
        gather = part.transpose(2, 1, 3, 0, 4).reshape(XH * Z, 2 * M // XH, XH * rows)
        out["to_" + name] = np.concatenate(split_hi_lo(gather), axis=1)
        inv = (coef * factor).reshape(XH, Z, XH, Z, 8, R)
        own = np.stack([np.stack([inv[a if q == 0 else 1 - a, :, a] for q in range(2)], axis=1) for a in range(XH)])
        wide = np.zeros((XH, Z, 2, 2, R, Z, 2, 8))
        for t2 in range(2):
            wide[:, :, :, t2, :, :, t2, :] = own.transpose(0, 1, 2, 5, 3, 4)
        wide = wide.reshape(XH * Z, 4 * R, 16 * Z)
        out["from_" + name] = np.concatenate(split_hi_lo(wide), axis=1)
    return out


def dot(left, right, dims):
    return lax.dot_general(left, right, dims, preferred_element_type=f32)


def call(kernel, out_shape, args, table=None, where=None, scratch=(), flops=0, name=None):
    def whole(shape):
        return pl.BlockSpec(shape, lambda i, w, n=len(shape): (0,) * n)

    outs = jax.tree.leaves(out_shape)
    in_specs = [whole(a.shape) for a in args]
    if table is not None:
        in_specs.append(pl.BlockSpec((1,) + table.shape[1:], lambda i, w: (w[0], 0, 0)))
        args = list(args) + [table]
    touched = sum(int(np.prod(a.shape)) * a.dtype.itemsize for a in list(args[: len(args)]) + outs)
    specs = jax.tree.map(lambda s: whole(s.shape), out_shape)
    return pl.pallas_call(
        kernel,
        out_shape=out_shape,
        grid_spec=pltpu.PrefetchScalarGridSpec(
            num_scalar_prefetch=1, grid=(1,), in_specs=in_specs, out_specs=specs, scratch_shapes=list(scratch)
        ),
        compiler_params=pltpu.CompilerParams(vmem_limit_bytes=VMEM_LIMIT),
        cost_estimate=pl.CostEstimate(flops=flops, bytes_accessed=touched, transcendentals=0),
        name=name,
    )(where, *args)


def points_kernel(w, x_ref, v_ref, y_ref):
    y = dot(v_ref[...], x_ref[...], NT)
    y_ref[...] = (y[:R] + y[R:]).astype(bf16)


def modes_kernel(w, y_ref, g_ref, out_ref):
    half = g_ref.shape[1] // 2
    for tt in range(8):
        part = dot(g_ref[0], y_ref[:, tt * 256 : (tt + 1) * 256], NN)
        part = part[:half] + part[half:]
        left = part[:, :128].reshape(Z, 8, 128)
        right = part[:, 128:].reshape(Z, 8, 128)
        out_ref[:, tt * 16 : (tt + 1) * 16, :] = jnp.concatenate([left, right], axis=1).astype(bf16)


def modes_bias_kernel(w, y_ref, g_ref, out_ref, bias_ref):
    modes_kernel(w, y_ref, g_ref, out_ref)
    first = y_ref[0:RB, 0:128].astype(f32)[R : R + 8]
    second = y_ref[RB : 2 * RB, 0:128].astype(f32)[R : R + 8]
    bias_ref[...] = first + second


def summed(ref):
    total = ref[0].astype(f32)
    for i in range(1, ref.shape[0]):
        total = total + ref[i].astype(f32)
    return total


def rows_of(scr, k, r):
    return scr[pl.ds(2 * k + r, 16, stride=8), :]


def gather_kernel(w, got_ref, out_ref, scr):
    scr[...] = summed(got_ref)
    blocks = []
    for k in range(4):
        re, im = rows_of(scr, k, 0), rows_of(scr, k, 1)
        blocks.append(jnp.concatenate([re[:, :64], im[:, :64]], axis=1))
        blocks.append(jnp.concatenate([re[:, 64:], im[:, 64:]], axis=1))
    send = jnp.concatenate(blocks, axis=0).astype(bf16)
    for i in range(out_ref.shape[0]):
        out_ref[i] = send


def put_rows(scr, k, r, block):
    scr[pl.ds(2 * k + r, 16, stride=8), :] = jnp.concatenate([block[:16], block[16:]], axis=1)


def mix_kernel(w, got_ref, weight_ref, out_ref, spec_ref, scr):
    for k in range(4):
        rows = slice(k * 32, (k + 1) * 32)
        re, im = [], []
        for q in range(8):
            one, two = got_ref[2 * q, rows, :], got_ref[2 * q + 1, rows, :]
            re.append(jnp.concatenate([one[:, :64], two[:, :64]], axis=1))
            im.append(jnp.concatenate([one[:, 64:], two[:, 64:]], axis=1))
        spec = jnp.concatenate([jnp.concatenate(re, axis=1), jnp.concatenate(im, axis=1)], axis=0)
        spec_ref[k] = spec
        out = dot(spec, weight_ref[k], NT)
        put_rows(scr, k, 0, out[:32, :64] - out[32:, 64:])
        put_rows(scr, k, 1, out[:32, 64:] + out[32:, :64])
    send = scr[...].astype(bf16)
    for i in range(out_ref.shape[0]):
        out_ref[i] = send


def window_sums(got, d_ref, own_ref, other_ref, tt):
    out = dot(d_ref[0], got, NN)
    out = out[: 4 * R] + out[4 * R :]
    lanes = slice(tt * 256, (tt + 1) * 256)
    own_ref[:, lanes] = jnp.concatenate([out[:R], out[R : 2 * R]], axis=1)
    return jnp.concatenate([out[2 * R : 3 * R], out[3 * R :]], axis=1)


def windows_kernel(w, got_ref, d_ref, own_ref, other_ref):
    for tt in range(8):
        got = got_ref[:, tt * 16 : (tt + 1) * 16, :].reshape(16 * Z, 128)
        other = window_sums(got, d_ref, own_ref, other_ref, tt)
        other_ref[:, tt * 256 : (tt + 1) * 256] = other.astype(bf16)


def hi_lo_rows(row):
    hi = row.astype(bf16).astype(f32)
    return jnp.concatenate([hi, (row - hi).astype(bf16).astype(f32)], axis=1)


def windows_bias_kernel(w, got_ref, d_ref, own_ref, other_ref, bias_ref):
    total = jnp.zeros((16, 128), f32)
    for i in range(Z):
        total = total + got_ref[i, 128:144, :].astype(f32)
    bias_ref[...] = total[:8]
    for tt in range(8):
        got = got_ref[:, tt * 16 : (tt + 1) * 16, :].reshape(16 * Z, 128)
        other = window_sums(got, d_ref, own_ref, other_ref, tt)
        other_ref[:, tt * 256 : (tt + 1) * 256] = other.astype(bf16)


def expanded(own_ref, other_ref, e_ref, tt):
    lanes = slice(tt * 256, (tt + 1) * 256)
    coef = own_ref[:, lanes] + other_ref[:, lanes].astype(f32)
    hi = coef.astype(bf16).astype(f32)
    stacked = jnp.concatenate([hi, hi, coef - hi], axis=0).astype(bf16)
    field = dot(stacked, e_ref[...], TN)
    return field.astype(bf16).astype(f32).reshape(4, 64, WIN)


def pointwise_kernel(w, own_ref, other_ref, cot_ref, bias_ref, e_ref, v_ref, y_ref):
    root = math.sqrt(2.0 / math.pi)
    bias = bias_ref[...][None]
    total = jnp.zeros((64, WIN), f32)
    for tt in range(8):
        v = expanded(own_ref, other_ref, e_ref, tt) + bias
        square = v * v
        th = jnp.tanh(root * (v + 0.044715 * (square * v)))
        slope = 0.5 * (1.0 + th) + (0.5 * root) * v * (1.0 - th * th) * (1.0 + (3.0 * 0.044715) * square)
        grad = slope * cot_ref[tt * 4 : (tt + 1) * 4].astype(f32)
        total = total + jnp.sum(grad, axis=0)
        y = dot(v_ref[...], grad.astype(bf16).reshape(256, WIN), NT)
        y = y[:R] + y[R:]
        y = jnp.concatenate([y, jnp.zeros((RB - R, 256), f32)], axis=0)
        y_ref[:, tt * 256 : (tt + 1) * 256] = y.astype(bf16)
    sums = lax.dot_general(
        jnp.ones((8, WIN), f32), total, NT, precision=lax.Precision.HIGHEST, preferred_element_type=f32
    )
    sums = hi_lo_rows(sums)
    y = y_ref[:, 0:128].astype(f32)
    y_ref[:, 0:128] = jnp.concatenate([y[:R], sums], axis=0).astype(bf16)


def back_kernel(w, got_ref, weight_ref, out_ref, grad_ref, scr):
    scr[...] = summed(got_ref).astype(bf16).astype(f32)
    for k in range(4):
        re, im = rows_of(scr, k, 0), rows_of(scr, k, 1)
        re = jnp.concatenate([re[:, :64], re[:, 64:]], axis=0)
        im = jnp.concatenate([im[:, :64], im[:, 64:]], axis=0)
        top = jnp.concatenate([re, im], axis=1)
        low = jnp.concatenate([im, -re], axis=1)
        grad = jnp.concatenate([top, low], axis=0).astype(bf16)
        grad_ref[k] = grad
        out = dot(grad, weight_ref[k], NN).astype(bf16)
        rows = slice(k * 32, (k + 1) * 32)
        for q in range(8):
            re, im = out[:32, q * 128 : (q + 1) * 128], out[32:, q * 128 : (q + 1) * 128]
            out_ref[2 * q, rows, :] = jnp.concatenate([re[:, :64], im[:, :64]], axis=1)
            out_ref[2 * q + 1, rows, :] = jnp.concatenate([re[:, 64:], im[:, 64:]], axis=1)


def weight_kernel(w, grad_ref, spec_ref, out_ref):
    for k in range(4):
        out_ref[k] = dot(grad_ref[k], spec_ref[k], TN)


def collect_kernel(w, got_ref, bias_ref, out_ref, scr):
    total = summed(got_ref)
    for k in range(4):
        block = total[k * 32 : (k + 1) * 32]
        put_rows(scr, k, 0, block[:, :64])
        put_rows(scr, k, 1, block[:, 64:])
    send = scr[...].astype(bf16)
    bias = bias_ref[...]
    bias = hi_lo_rows(bias[:, :64] + bias[:, 64:])
    tail = jnp.concatenate([bias, jnp.zeros((8, 128), f32)], axis=0).astype(bf16)
    for i in range(out_ref.shape[0]):
        out_ref[i, 0:128, :] = send
        out_ref[i, 128:144, :] = tail


def finish_kernel(w, own_ref, other_ref, cot_ref, e_ref, out_ref):
    for tt in range(8):
        field = expanded(own_ref, other_ref, e_ref, tt)
        rows = slice(tt * 4, (tt + 1) * 4)
        out_ref[rows] = (cot_ref[rows].astype(f32) + field).astype(bf16)


def exchange(blocks, axis):
    return lax.all_to_all(blocks, axis, split_axis=0, concat_axis=0, tiled=True)


def body(activation, cotangent, spectral_weight, out_bias):
    table = tables()
    where = jnp.reshape(lax.axis_index("xh") * Z + lax.axis_index("z"), (1,)).astype(jnp.int32)
    const = {name: jnp.asarray(value) for name, value in table.items()}
    shape = jax.ShapeDtypeStruct
    run = functools.partial(call, where=where)
    swap = [(0, 1), (1, 0)]
    chan = lax.axis_size("chan")
    span, width = activation.shape[0], activation.shape[1]
    lanes = span * width
    weight = spectral_weight.reshape(4, 2 * width, spectral_weight.shape[3])
    bias_wide = jnp.broadcast_to(out_bias[:, None], (width, WIN))
    square = pltpu.VMEM((128, 128), f32)
    block = shape((Z, 128, 128), bf16)

    coefs = run(points_kernel, shape((R, lanes), bf16), [activation.reshape(lanes, WIN), const["points"]], name="points")
    coefs = lax.all_gather(coefs, "xh", axis=0, tiled=True)
    parts = run(modes_kernel, block, [coefs], const["to_plain"], flops=2 * 256 * 64 * lanes, name="modes")
    parts = exchange(parts, "z")
    spectra = run(gather_kernel, shape((chan, 128, 128), bf16), [parts], scratch=[square], name="gather")
    spectra = exchange(spectra, "chan")
    mixed, spec = run(
        mix_kernel,
        (block, shape((4, 64, weight.shape[2]), bf16)),
        [spectra, weight],
        scratch=[square],
        flops=2 * 4 * 64 * 128 * weight.shape[2],
        name="mix",
    )
    mixed = exchange(mixed, "z")
    pair = (shape((R, lanes), f32), shape((R, lanes), bf16))
    own, other = run(windows_kernel, pair, [mixed], const["from_doubled"], name="windows")
    other = lax.ppermute(other, "xh", swap)
    coefs = run(
        pointwise_kernel,
        shape((RB, lanes), bf16),
        [own, other, cotangent, bias_wide, const["expand"], const["points"]],
        name="pointwise",
    )
    coefs = lax.all_gather(coefs, "xh", axis=0, tiled=True)
    parts, bias_pair = run(modes_bias_kernel, (block, shape((8, 128), f32)), [coefs], const["to_doubled"], name="modes_back")
    parts = exchange(parts, "z")
    back, grad = run(
        back_kernel,
        (shape((chan, 128, 128), bf16), shape((4, 64, 128), bf16)),
        [parts, weight],
        scratch=[square],
        name="back",
    )
    back = exchange(back, "chan")
    grad_weight = run(
        weight_kernel,
        shape((4, 2 * width, weight.shape[2]), f32),
        [grad, spec],
        flops=2 * 4 * 64 * 128 * weight.shape[2],
        name="weight",
    )
    sums = run(collect_kernel, shape((Z, 144, 128), bf16), [back, bias_pair], scratch=[square], name="collect")
    sums = exchange(sums, "z")
    own, other, bias_sum = run(
        windows_bias_kernel, pair + (shape((8, 128), f32),), [sums], const["from_plain"], name="windows_back"
    )
    other = lax.ppermute(other, "xh", swap)
    grad_input = run(
        finish_kernel, shape(activation.shape, bf16), [own, other, cotangent, const["expand"]], name="finish"
    )
    grad_bias = bias_sum[0, :width] + bias_sum[0, width:]
    return grad_input, grad_weight.reshape(spectral_weight.shape), grad_bias


def solution(mesh):
    fine = Mesh(mesh.devices.reshape(XH, Z, -1), ("xh", "z", "chan"))
    pitch = ("xh", "z")
    field = P(None, "chan", pitch)
    modes = P(pitch, None, "chan", None)
    return jax.shard_map(
        body,
        mesh=fine,
        in_specs=(field, field, modes, P("chan")),
        out_specs=(field, modes, P("chan")),
        check_vma=False,
    )
```

time: 548 us -> 223 us (0.41)
  blocking collectives: 233 us -> 152 us
  other arithmetic: 62.1 us -> 0.58 us
  waiting for transfers between devices: 95.8 us -> 35.6 us
  local copies, waits for them, and re-layouts: 61.3 us -> 6.11 us
  starting transfers between devices: 54.9 us -> 16.8 us
  matrix products: 22.9 us -> 0 us
  between operations: 14.7 us -> 0.82 us
  Pallas kernels: 0 us -> 8.77 us
    psum x1 -> x0, blocking collectives: 93.7 us -> none  [body(): grad_bias = lax.psum(jnp.sum(grad_pre, axis=(0, 2)), 'pitch')]
    unnamed x2 -> x0, waiting for transfers between devices: 55.2 us -> none
    all_to_all x5 -> x1, starting transfers between devices: 54.8 us -> 7.39 us  [exchange(): return lax.all_to_all(blocks, axis, split_axis=0, concat_axis=0, tiled=True)]
    unnamed x2 -> x0, other arithmetic: 46.8 us -> none
    mul x4 -> x0, local copies, waits for them, and re-layouts: 24.9 us -> none  [spectral_table(): jnp.stack([jnp.cos(angles), -jnp.sin(angles)], axis=1)]
    dot_general x16 -> x0, matrix products: 22.9 us -> none  [the longest x2 8.5 us: to_modes(): jnp.einsum('scp,jp->jsc', spanwise.astype(jnp.float32), basis, precision=...]
    all_to_all x3 -> x5, blocking collectives: 118 us -> 138 us  [exchange(): return lax.all_to_all(blocks, axis, split_axis=0, concat_axis=0, tiled=True)]
    unnamed x32 -> x30, local copies, waits for them, and re-layouts: 21.2 us -> 6.04 us
  transfers between devices with their start and end apart: 6 -> 3, of which waited for: 4 -> 3; matrix products, arithmetic and copies ran while one was open for 8% -> 0% of each run, Pallas kernels for 0% -> 1%
where the time goes in v1:
time: 223 us; the launch traced here: 221 us
  blocking collectives  152 us (68%)
  waiting for transfers between devices  35.6 us (16%)
  starting transfers between devices  16.8 us (8%)
  Pallas kernels  8.77 us (4%)
  local copies, waits for them, and re-layouts  6.11 us (3%)
    all_to_all x5, blocking collectives, exchange(): return lax.all_to_all(blocks, axis, split_axis=0, concat_axis=0, tiled=True)  138 us
    all_to_all x1, waiting for transfers between devices, exchange(): return lax.all_to_all(blocks, axis, split_axis=0, concat_axis=0, tiled=True)  28.5 us
    all_gather x2, blocking collectives, body(): coefs = lax.all_gather(coefs, 'xh', axis=0, tiled=True)  14 us
    ppermute x2, starting transfers between devices, body(): other = lax.ppermute(other, 'xh', swap)  9.4 us
    pallas_call x12, Pallas kernels, call(): pl.pallas_call(kernel, out_shape=out_shape, grid_spec=pltpu.PrefetchScala...  8.77 us
    all_to_all x1, starting transfers between devices, exchange(): return lax.all_to_all(blocks, axis, split_axis=0, concat_axis=0, tiled=True)  7.39 us
    ppermute x2, waiting for transfers between devices, body(): other = lax.ppermute(other, 'xh', swap)  7.13 us
    unnamed x30, local copies, waits for them, and re-layouts  6.04 us
  transfers between devices with their start and end apart: 3, of which 3 were waited for; matrix products, arithmetic and copies ran while one was open for 0% of the time, Pallas kernels for 1%

profile of v1, /device:TPU:24, one launch (start us, length us, event | category | flops | bytes accessed | tf_op | source)
XLA Modules:
  0.0 220.7 jit_solution(11327444803555609086)
XLA Ops:
  0.6 0.0 copy-start.8
  0.6 1.0 copy-done.8
  1.7 0.7 copy-done.12
  2.4 0.3 points.1
  2.7 6.8 %all_gather.6.y_ref = bf16[48,2048]{1,0:T(8,128)(2,1)S(1)} all-gather(bf16[24,2048]{1,0:T(8,128)(2,1)S(1)} %points.1), channel_id=1, replica_groups=mesh['xh'=2,'z'=16,'chan'=16] {'xh'}, dimensions={0}, use_global_device_ids=true | all-gather | bytes 294912 | tf_op jit(solution)/shard_map/all_gather | solution.py:287
  9.5 1.6 copy-done.7
  11.1 0.4 modes.1
  11.5 0.0 copy-start
  11.5 42.5 %all_to_all.30.got_ref = bf16[16,128,128]{2,1,0:T(8,128)(2,1)S(1)} all-to-all(bf16[16,128,128]{2,1,0:T(8,128)(2,1)S(1)} %modes.1), channel_id=1, replica_groups=mesh['xh'=2,'z'=16,'chan'=16] {'z'}, dimensions={0} | all-to-all | bytes 1048576 | tf_op jit(solution)/shard_map/all_to_all | solution.py:268
  54.0 0.2 gather.1
  54.2 0.0 copy-start.2
  54.2 14.4 %all_to_all.31.got_ref = bf16[16,128,128]{2,1,0:T(8,128)(2,1)S(1)} all-to-all(bf16[16,128,128]{2,1,0:T(8,128)(2,1)S(1)} %gather.1), channel_id=1, replica_groups=mesh['xh'=2,'z'=16,'chan'=16] {'chan'}, dimensions={0} | all-to-all | bytes 1048576 | tf_op jit(solution)/shard_map/all_to_all | solution.py:268
  68.6 0.0 copy-done
  68.6 0.7 mix.1
  69.3 0.0 copy-start.9
  69.3 0.8 copy-done.9
  70.1 36.0 %all_to_all.32.got_ref = bf16[16,128,128]{2,1,0:T(8,128)(2,1)S(1)} all-to-all(bf16[16,128,128]{2,1,0:T(8,128)(2,1)S(1)} %get-tuple-element.14), channel_id=1, replica_groups=mesh['xh'=2,'z'=16,'chan'=16] {'z'}, dimensions={0} | all-to-all | bytes 1048576 | tf_op jit(solution)/shard_map/all_to_all | solution.py:268
  106.1 0.0 copy-done.2
  106.1 0.0 copy-start.13
  106.1 0.0 copy-start.4
  106.1 0.3 windows.1
  106.5 4.8 %collective-permute-start = (bf16[24,2048]{1,0:T(8,128)(2,1)S(1)}, bf16[24,2048]{1,0:T(8,128)(2,1)S(1)}, u32[]{:S(2)}, u32[]{:S(2)}) collective-permute-start(bf16[24,2048]{1,0:T(8,128)(2,1)S(1)} %get-tuple-element.16), channel_id=1, source_target_pairs={{0,256},{256,0},{1,257},{257,1},{2,258},{258,2},{3,259},{259,3},{4... | collective-permute-start | bytes 294920 | tf_op jit(solution)/shard_map/ppermute | solution.py:303
  111.2 4.3 %collective-permute-done.other_ref = bf16[24,2048]{1,0:T(8,128)(2,1)S(1)} collective-permute-done((bf16[24,2048]{1,0:T(8,128)(2,1)S(1)}, bf16[24,2048]{1,0:T(8,128)(2,1)S(1)}, u32[]{:S(2)}, u32[]{:S(2)}) %collective-permute-start) | collective-permute-done | bytes 98336 | tf_op jit(solution)/shard_map/ppermute | solution.py:303
  115.6 0.0 copy-done.14
  115.6 0.1 broadcast_in_dim.2.bias_ref
  115.6 0.0 copy-done.5
  115.7 0.0 copy-done.11
  115.7 0.0 copy-done.13
  115.7 1.3 pointwise.1
  117.0 7.2 %all_gather.7.y_ref = bf16[64,2048]{1,0:T(8,128)(2,1)S(1)} all-gather(bf16[32,2048]{1,0:T(8,128)(2,1)S(1)} %pointwise.1), channel_id=1, replica_groups=mesh['xh'=2,'z'=16,'chan'=16] {'xh'}, dimensions={0}, use_global_device_ids=true | all-gather | bytes 393216 | tf_op jit(solution)/shard_map/all_gather | solution.py:310
  124.1 0.0 copy-done.4
  124.1 0.4 modes_back.1
  124.5 32.0 %all_to_all.33.got_ref = bf16[16,128,128]{2,1,0:T(8,128)(2,1)S(1)} all-to-all(bf16[16,128,128]{2,1,0:T(8,128)(2,1)S(1)} %get-tuple-element.17), channel_id=1, replica_groups=mesh['xh'=2,'z'=16,'chan'=16] {'z'}, dimensions={0} | all-to-all | bytes 1048576 | tf_op jit(solution)/shard_map/all_to_all | solution.py:268
  156.5 0.6 back.1
  157.1 13.2 %all_to_all.34.got_ref = bf16[16,128,128]{2,1,0:T(8,128)(2,1)S(1)} all-to-all(bf16[16,128,128]{2,1,0:T(8,128)(2,1)S(1)} %get-tuple-element.18), channel_id=1, replica_groups=mesh['xh'=2,'z'=16,'chan'=16] {'chan'}, dimensions={0} | all-to-all | bytes 1048576 | tf_op jit(solution)/shard_map/all_to_all | solution.py:268
  170.3 0.2 collect.1
  170.5 0.0 copy-start.3
  170.5 0.8 copy-done.3
  171.4 7.4 %all-to-all-start.5 = ((bf16[16,144,128]{2,1,0:T(8,128)(2,1)}), bf16[16,144,128]{2,1,0:T(8,128)(2,1)}, u32[]{:S(2)}, u32[]{:S(2)}) async-start(bf16[16,144,128]{2,1,0:T(8,128)(2,1)} %copy-done.3), calls=%async_computation.5 | async-start | bytes 1179648 | tf_op jit(solution)/shard_map/all_to_all | solution.py:268
  178.8 0.0 copy-start.10
  178.8 1.0 copy-done.10
  179.8 1.8 weight.1
  181.6 28.5 %all-to-all-done.5.got_ref = bf16[16,144,128]{2,1,0:T(8,128)(2,1)} async-done(((bf16[16,144,128]{2,1,0:T(8,128)(2,1)}), bf16[16,144,128]{2,1,0:T(8,128)(2,1)}, u32[]{:S(2)}, u32[]{:S(2)}) %all-to-all-start.5) | async-done | bytes 589856 | tf_op jit(solution)/shard_map/all_to_all | solution.py:268
  210.1 1.5 windows_back.1
  211.5 4.6 %collective-permute-start.1 = (bf16[24,2048]{1,0:T(8,128)(2,1)S(1)}, bf16[24,2048]{1,0:T(8,128)(2,1)S(1)}, u32[]{:S(2)}, u32[]{:S(2)}) collective-permute-start(bf16[24,2048]{1,0:T(8,128)(2,1)S(1)} %get-tuple-element.21), channel_id=1, source_target_pairs={{0,256},{256,0},{1,257},{257,1},{2,258},{258,2},{3,259},{259,3},{4... | collective-permute-start | bytes 294920 | tf_op jit(solution)/shard_map/ppermute | solution.py:333
  216.2 0.6 add_bitcast_fusion
  216.8 2.8 %collective-permute-done.1.other_ref = bf16[24,2048]{1,0:T(8,128)(2,1)S(1)} collective-permute-done((bf16[24,2048]{1,0:T(8,128)(2,1)S(1)}, bf16[24,2048]{1,0:T(8,128)(2,1)S(1)}, u32[]{:S(2)}, u32[]{:S(2)}) %collective-permute-start.1) | collective-permute-done | bytes 98336 | tf_op jit(solution)/shard_map/ppermute | solution.py:333
  219.6 1.1 finish.1
  (9 shorter events, 0.0 us)
Async XLA Ops:
  0.6 1.0 copy-start.8
  1.7 0.7 copy-start.12
  9.5 1.6 copy-start.7
  11.5 57.1 %copy-start = (bf16[4,2,64,1024]{3,2,1,0:T(8,128)(2,1)S(1)}, bf16[4,2,64,1024]{3,2,1,0:T(8,128)(2,1)}, u32[]{:S(2)}) copy-start(bf16[4,2,64,1024]{3,2,1,0:T(8,128)(2,1)} %param.12) | copy-start | bytes 3145732
  54.2 51.8 %copy-start.2 = (bf16[32,192,256]{2,1,0:T(8,128)(2,1)S(1)}, bf16[32,192,256]{2,1,0:T(8,128)(2,1)}, u32[]{:S(2)}) copy-start(bf16[32,192,256]{2,1,0:T(8,128)(2,1)} %constant.30.clone.d_ref) | copy-start | bytes 9437188
  69.3 0.8 copy-start.9
  106.1 9.5 %copy-start.14 = (f32[64]{0:T(128)S(1)}, f32[64]{0:T(128)}, u32[]{:S(2)}) copy-start(f32[64]{0:T(128)} %param.13) | copy-start | bytes 772
  106.1 9.6 %copy-start.5 = (bf16[32,64,128]{2,1,0:T(8,128)(2,1)S(1)}, bf16[32,64,128]{2,1,0:T(8,128)(2,1)}, u32[]{:S(2)}) copy-start(bf16[32,64,128]{2,1,0:T(8,128)(2,1)} %cot_ref.3) | copy-start | bytes 1572868
  106.1 9.6 %copy-start.11 = (bf16[72,128]{1,0:T(8,128)(2,1)S(1)}, bf16[72,128]{1,0:T(8,128)(2,1)}, u32[]{:S(2)}) copy-start(bf16[72,128]{1,0:T(8,128)(2,1)} %constant.26.clone.e_ref) | copy-start | bytes 55300
  106.1 9.6 %copy-start.13 = (bf16[48,128]{1,0:T(8,128)(2,1)S(1)}, bf16[48,128]{1,0:T(8,128)(2,1)}, u32[]{:S(2)}) copy-start(bf16[48,128]{1,0:T(8,128)(2,1)} %constant.25.clone.v_ref) | copy-start | bytes 36868
  106.1 18.0 %copy-start.4 = (bf16[32,256,64]{2,1,0:T(8,128)(2,1)S(1)}, bf16[32,256,64]{2,1,0:T(8,128)(2,1)}, u32[]{:S(2)}) copy-start(bf16[32,256,64]{2,1,0:T(8,128)(2,1)} %constant.29.clone.g_ref) | copy-start | bytes 3145732
  106.5 9.1 %collective-permute-start = (bf16[24,2048]{1,0:T(8,128)(2,1)S(1)}, bf16[24,2048]{1,0:T(8,128)(2,1)S(1)}, u32[]{:S(2)}, u32[]{:S(2)}) collective-permute-start(bf16[24,2048]{1,0:T(8,128)(2,1)S(1)} %get-tuple-element.16), channel_id=1, source_target_pairs={{0,256},{256,0},{1,257},{257,1},{2,258},{258,2},{3,259},{259,3},{4... | collective-permute-start | bytes 294920 | tf_op jit(solution)/shard_map/ppermute | solution.py:303
  170.5 0.8 copy-start.3
  171.4 38.7 %copy-start.1 = (bf16[32,192,256]{2,1,0:T(8,128)(2,1)S(1)}, bf16[32,192,256]{2,1,0:T(8,128)(2,1)}, u32[]{:S(2)}) copy-start(bf16[32,192,256]{2,1,0:T(8,128)(2,1)} %constant.28.clone.d_ref) | copy-start | bytes 9437188
  171.4 38.7 %all-to-all-start.5 = ((bf16[16,144,128]{2,1,0:T(8,128)(2,1)}), bf16[16,144,128]{2,1,0:T(8,128)(2,1)}, u32[]{:S(2)}, u32[]{:S(2)}) async-start(bf16[16,144,128]{2,1,0:T(8,128)(2,1)} %copy-done.3), calls=%async_computation.5 | async-start | bytes 1179648 | tf_op jit(solution)/shard_map/all_to_all | solution.py:268
  178.8 1.0 copy-start.10
  210.1 9.5 %copy-start.6 = (bf16[32,64,128]{2,1,0:T(8,128)(2,1)S(1)}, bf16[32,64,128]{2,1,0:T(8,128)(2,1)}, u32[]{:S(2)}) copy-start(bf16[32,64,128]{2,1,0:T(8,128)(2,1)} %cot_ref.3) | copy-start | bytes 1572868
  211.5 8.0 %collective-permute-start.1 = (bf16[24,2048]{1,0:T(8,128)(2,1)S(1)}, bf16[24,2048]{1,0:T(8,128)(2,1)S(1)}, u32[]{:S(2)}, u32[]{:S(2)}) collective-permute-start(bf16[24,2048]{1,0:T(8,128)(2,1)S(1)} %get-tuple-element.21), channel_id=1, source_target_pairs={{0,256},{256,0},{1,257},{257,1},{2,258},{258,2},{3,259},{259,3},{4... | collective-permute-start | bytes 294920 | tf_op jit(solution)/shard_map/ppermute | solution.py:333

commit v2 on v0

v2 whole, which is shorter than its diff:
```python
import functools
import math

import jax
import jax.numpy as jnp
import ml_dtypes
import numpy as np
from jax import lax
from jax.experimental import pallas as pl
from jax.experimental.pallas import tpu as pltpu
from jax.sharding import PartitionSpec as P

P_SIZE = 4096
M = 128
PITCH = 32
WIN = P_SIZE // PITCH
KEPT = M // PITCH
R = 32
f32 = jnp.float32
bf16 = jnp.bfloat16
NT = (((1,), (1,)), ((), ()))
NN = (((1,), (0,)), ((), ()))
TN = (((0,), (0,)), ((), ()))
VMEM_LIMIT = 32 * 1024 * 1024


def split_hi_lo(table):
    hi = table.astype(ml_dtypes.bfloat16)
    lo = (table - hi.astype(np.float64)).astype(ml_dtypes.bfloat16)
    return hi, lo


@functools.cache
def tables():
    modes = np.arange(M)
    angle = 2.0 * math.pi * (np.outer(modes, np.arange(P_SIZE)) % P_SIZE) / P_SIZE
    forward = np.stack([np.cos(angle), -np.sin(angle)]) / math.sqrt(P_SIZE)
    doubled = forward * np.where(modes == 0, 1.0, 2.0)[:, None]
    basis = np.linalg.svd(forward[:, :, :WIN].reshape(2 * M, WIN))[2][:R]
    coef = np.einsum("akwp,xp->akwx", forward.reshape(2, M, PITCH, WIN), basis)
    coef = coef.reshape(2 * M, PITCH, 2, R // 2)
    out = {}
    hi, lo = split_hi_lo(basis)
    out["points"] = np.concatenate([hi, lo], axis=0)
    gather = coef.transpose(2, 0, 1, 3).reshape(2, 2 * M, PITCH * R // 2)
    out["modes"] = np.stack(split_hi_lo(gather), axis=1).reshape(8 * M, PITCH * R // 2)
    spread = coef.transpose(2, 1, 3, 0).reshape(PITCH * R, 2 * M)
    out["windows"] = np.concatenate(split_hi_lo(spread), axis=0)
    whole = doubled.reshape(2, PITCH, KEPT, P_SIZE).transpose(0, 2, 1, 3).reshape(2 * M, P_SIZE)
    out["doubled"] = np.stack(split_hi_lo(whole))
    return out


def dot(left, right, dims):
    return lax.dot_general(left, right, dims, preferred_element_type=f32)


def run(kernel, out_shape, *args, scratch=(), flops=0, name=None):
    touched = sum(int(np.prod(a.shape)) * a.dtype.itemsize for a in list(args) + jax.tree.leaves(out_shape))
    return pl.pallas_call(
        kernel,
        out_shape=out_shape,
        scratch_shapes=list(scratch),
        compiler_params=pltpu.CompilerParams(vmem_limit_bytes=VMEM_LIMIT),
        cost_estimate=pl.CostEstimate(flops=flops, bytes_accessed=touched, transcendentals=0),
        name=name,
    )(*args)


def halves(left, right):
    return (
        jnp.concatenate([left[:, :64], right[:, :64]], axis=1),
        jnp.concatenate([left[:, 64:], right[:, 64:]], axis=1),
    )


def points_kernel(x_ref, v_ref, out_ref):
    for t in range(16):
        field = x_ref[2 * t : 2 * t + 2].reshape(128, WIN)
        y = dot(v_ref[...], field, NT)
        y = y[:R] + y[R:]
        first, second = halves(y[:16], y[16:])
        out_ref[t * 32 : (t + 1) * 32, :] = jnp.concatenate([first, second], axis=0).astype(bf16)


def modes_kernel(got_ref, g_ref, out_ref):
    part = dot(g_ref[...], got_ref[...], NN)
    part = part[: 4 * M, :64] + part[4 * M :, 64:]
    part = part[: 2 * M] + part[2 * M :]
    out_ref[...] = jnp.concatenate([part[:M], part[M:]], axis=1).astype(bf16)


def by_mode(scr, value, count):
    scr[...] = value
    return [scr[pl.ds(k, PITCH, stride=count), :] for k in range(KEPT)]


def gather_kernel(got_ref, out_ref, scr):
    send = jnp.concatenate(by_mode(scr, got_ref[...].astype(f32), KEPT), axis=0).astype(bf16)
    for i in range(out_ref.shape[0]):
        out_ref[i] = send


def mix_kernel(got_ref, weight_ref, out_ref, spec_ref, scr):
    for k in range(KEPT):
        rows = slice(k * PITCH, (k + 1) * PITCH)
        re, im = [], []
        for q in range(got_ref.shape[0] // 2):
            first, second = halves(got_ref[2 * q, rows, :], got_ref[2 * q + 1, rows, :])
            re.append(first)
            im.append(second)
        spec = jnp.concatenate([jnp.concatenate(re, axis=1), jnp.concatenate(im, axis=1)], axis=0)
        spec_ref[k] = spec
        out = dot(spec, weight_ref[k], NT)
        real = out[:32, :64] - out[32:, 64:]
        imag = out[:32, 64:] + out[32:, :64]
        scr[pl.ds(k, PITCH, stride=KEPT), :] = jnp.concatenate([real, imag], axis=1)
    out_ref[...] = scr[...].astype(bf16)


def pointwise_kernel(got_ref, cot_ref, bias_ref, table_ref, out_ref, scr, send):
    root = math.sqrt(2.0 / math.pi)
    mixed = jnp.concatenate(by_mode(scr, got_ref[...].astype(f32), KEPT), axis=0)
    mixed = mixed.T
    mixed = jnp.concatenate([mixed[:64], mixed[64:]], axis=1).astype(bf16)
    bias = bias_ref[...]
    total = jnp.zeros((64, WIN), f32)
    modes = jnp.zeros((2 * M, 64), f32)
    for chunk in range(8):
        lanes = slice(chunk * 512, (chunk + 1) * 512)
        high, low = table_ref[0, :, lanes], table_ref[1, :, lanes]
        response = (dot(mixed, high, NN) + dot(mixed, low, NN)).astype(bf16).astype(f32)
        grads = []
        for i in range(4):
            v = response[:, i * WIN : (i + 1) * WIN] + bias
            square = v * v
            th = jnp.tanh(root * (v + 0.044715 * (square * v)))
            slope = 0.5 * (1.0 + th) + (0.5 * root) * v * (1.0 - th * th) * (1.0 + (3.0 * 0.044715) * square)
            grad = slope * cot_ref[chunk * 4 + i].astype(f32)
            total = total + grad
            grads.append(grad.astype(bf16))
        grads = jnp.concatenate(grads, axis=1)
        modes = modes + dot(high, grads, NT) + dot(low, grads, NT)
    sums = lax.dot_general(
        jnp.ones((8, WIN), f32), total, NT, precision=lax.Precision.HIGHEST, preferred_element_type=f32
    )
    high = sums.astype(bf16).astype(f32)
    sums = jnp.concatenate([high, sums - high], axis=1)
    modes = jnp.concatenate([modes[:M], modes[M:]], axis=1)
    for k in range(KEPT):
        send[pl.ds(k, PITCH, stride=8), :] = modes[k * PITCH : (k + 1) * PITCH]
    send[pl.ds(KEPT, PITCH, stride=8), :] = jnp.concatenate([sums] * (PITCH // 8), axis=0)
    for k in range(KEPT + 1, 8):
        send[pl.ds(k, PITCH, stride=8), :] = jnp.zeros((PITCH, 128), f32)
    out_ref[...] = send[...].astype(bf16)


def back_kernel(got_ref, weight_ref, out_ref, grad_ref, bias_ref, scr):
    blocks = by_mode(scr, got_ref[...].astype(f32), 8)
    sums = jnp.sum(scr[pl.ds(KEPT, PITCH, stride=8), :], axis=0, keepdims=True)
    bias_ref[...] = jnp.broadcast_to(sums[:, :64] + sums[:, 64:], (8, 64))
    for k in range(KEPT):
        top = blocks[k]
        low = jnp.concatenate([top[:, 64:], -top[:, :64]], axis=1)
        grad = jnp.concatenate([top, low], axis=0).astype(bf16)
        grad_ref[k] = grad
        out = dot(grad, weight_ref[k], NN)
        rows = slice(k * PITCH, (k + 1) * PITCH)
        for q in range(out_ref.shape[0] // 2):
            lanes = slice(q * 128, (q + 1) * 128)
            first, second = halves(out[:32, lanes], out[32:, lanes])
            out_ref[2 * q, rows, :] = first.astype(bf16)
            out_ref[2 * q + 1, rows, :] = second.astype(bf16)


def weight_kernel(grad_ref, spec_ref, out_ref):
    for k in range(KEPT):
        out_ref[k] = dot(grad_ref[k], spec_ref[k], TN)


def collect_kernel(got_ref, out_ref, scr):
    total = got_ref[0].astype(f32)
    for i in range(1, got_ref.shape[0]):
        total = total + got_ref[i].astype(f32)
    for k in range(KEPT):
        scr[pl.ds(k, PITCH, stride=KEPT), :] = total[k * PITCH : (k + 1) * PITCH]
    out_ref[...] = scr[...].astype(bf16)


def windows_kernel(got_ref, u_ref, out_ref):
    got = jnp.concatenate([got_ref[:, :64], got_ref[:, 64:]], axis=0)
    out = dot(u_ref[...], got, NN)
    half = PITCH * R
    out = out[:half] + out[half:]
    out_ref[...] = jnp.concatenate([out[: half // 2], out[half // 2 :]], axis=1).astype(bf16)


def finish_kernel(got_ref, cot_ref, v_ref, out_ref):
    for t in range(16):
        low, high = halves(got_ref[t * 32 : t * 32 + 16, :], got_ref[t * 32 + 16 : t * 32 + 32, :])
        coef = jnp.concatenate([low, high, low, high], axis=0)
        field = dot(coef, v_ref[...], TN).astype(bf16).astype(f32).reshape(2, 64, WIN)
        rows = slice(2 * t, 2 * t + 2)
        out_ref[rows] = (cot_ref[rows].astype(f32) + field).astype(bf16)


def exchange(blocks, axis):
    return lax.all_to_all(blocks, axis, split_axis=0, concat_axis=0, tiled=True)


def body(activation, cotangent, spectral_weight, out_bias):
    const = {name: jnp.asarray(value) for name, value in tables().items()}
    shape = jax.ShapeDtypeStruct
    chan = lax.axis_size("chan")
    width = activation.shape[1]
    inputs = spectral_weight.shape[3]
    weight = spectral_weight.reshape(KEPT, 2 * width, inputs)
    bias_wide = jnp.broadcast_to(out_bias[:, None], (width, WIN))
    square = pltpu.VMEM((M, 128), f32)
    tall = pltpu.VMEM((2 * M, 128), f32)
    small = shape((M, 128), bf16)
    coefs_shape = shape((PITCH * R // 2, 128), bf16)
    across = shape((chan, M, 128), bf16)
    mix_flops = 2 * KEPT * 64 * 128 * inputs

    coefs = run(points_kernel, coefs_shape, activation, const["points"], name="points")
    coefs = exchange(coefs, "pitch")
    span_cotangent = exchange(cotangent, "pitch")
    spectra = run(modes_kernel, small, coefs, const["modes"], name="modes")
    spectra = exchange(spectra, "pitch")
    spectra = run(gather_kernel, across, spectra, scratch=[square], name="gather")
    spectra = exchange(spectra, "chan")
    mixed, spec = run(
        mix_kernel,
        (small, shape((KEPT, 64, inputs), bf16)),
        spectra,
        weight,
        scratch=[square],
        flops=mix_flops,
        name="mix",
    )
    mixed = exchange(mixed, "pitch")
    grads = run(
        pointwise_kernel,
        shape((2 * M, 128), bf16),
        mixed,
        span_cotangent,
        bias_wide,
        const["doubled"],
        scratch=[square, tall],
        name="pointwise",
    )
    grads = exchange(grads, "pitch")
    back, grad, bias = run(
        back_kernel,
        (across, shape((KEPT, 64, 128), bf16), shape((8, 64), f32)),
        grads,
        weight,
        scratch=[tall],
        flops=mix_flops,
        name="back",
    )
    back = exchange(back, "chan")
    grad_weight = run(
        weight_kernel, shape((KEPT, 2 * width, inputs), f32), grad, spec, flops=mix_flops, name="weight"
    )
    back = run(collect_kernel, small, back, scratch=[square], name="collect")
    back = exchange(back, "pitch")
    coefs = run(windows_kernel, coefs_shape, back, const["windows"], name="windows")
    coefs = exchange(coefs, "pitch")
    grad_input = run(
        finish_kernel, shape(activation.shape, bf16), coefs, cotangent, const["points"], name="finish"
    )
    return grad_input, grad_weight.reshape(spectral_weight.shape), bias[0]


def solution(mesh):
    field = P(None, "chan", "pitch")
    modes = P("pitch", None, "chan", None)
    return jax.shard_map(
        body,
        mesh=mesh,
        in_specs=(field, field, modes, P("chan")),
        out_specs=(field, modes, P("chan")),
        check_vma=False,
    )
```

time: 548 us -> 212 us (0.39)
  waiting for transfers between devices: 95.8 us -> 15.6 us
  other arithmetic: 62.1 us -> 0 us
  blocking collectives: 233 us -> 174 us
  local copies, waits for them, and re-layouts: 61.3 us -> 5.83 us
  starting transfers between devices: 54.9 us -> 3.86 us
  matrix products: 22.9 us -> 0 us
  between operations: 14.7 us -> 0.72 us
  Pallas kernels: 0 us -> 9.93 us
    psum x1 -> x0, blocking collectives: 93.7 us -> none  [body(): grad_bias = lax.psum(jnp.sum(grad_pre, axis=(0, 2)), 'pitch')]
    all_to_all x3 -> x8, blocking collectives: 118 us -> 174 us  [exchange(): return lax.all_to_all(blocks, axis, split_axis=0, concat_axis=0, tiled=True)]
    unnamed x2 -> x0, waiting for transfers between devices: 55.2 us -> none
    all_to_all x5 -> x1, starting transfers between devices: 54.8 us -> 3.86 us  [exchange(): return lax.all_to_all(blocks, axis, split_axis=0, concat_axis=0, tiled=True)]
    unnamed x2 -> x0, other arithmetic: 46.8 us -> none
    all_to_all x5 -> x1, waiting for transfers between devices: 40.6 us -> 15.6 us  [exchange(): return lax.all_to_all(blocks, axis, split_axis=0, concat_axis=0, tiled=True)]
    mul x4 -> x0, local copies, waits for them, and re-layouts: 24.9 us -> none  [spectral_table(): jnp.stack([jnp.cos(angles), -jnp.sin(angles)], axis=1)]
    dot_general x16 -> x0, matrix products: 22.9 us -> none  [the longest x2 8.5 us: to_modes(): jnp.einsum('scp,jp->jsc', spanwise.astype(jnp.float32), basis, precision=...]
  transfers between devices with their start and end apart: 6 -> 1, of which waited for: 4 -> 1; matrix products, arithmetic and copies ran while one was open for 8% -> 0% of each run, Pallas kernels for 0% -> 1%
where the time goes in v2:
time: 212 us; the launch traced here: 210 us
  blocking collectives  174 us (82%)
  waiting for transfers between devices  15.6 us (7%)
  Pallas kernels  9.93 us (5%)
  local copies, waits for them, and re-layouts  5.83 us (3%)
  starting transfers between devices  3.86 us (2%)
    all_to_all x8, blocking collectives, exchange(): return lax.all_to_all(blocks, axis, split_axis=0, concat_axis=0, tiled=True)  174 us
    all_to_all x1, waiting for transfers between devices, exchange(): return lax.all_to_all(blocks, axis, split_axis=0, concat_axis=0, tiled=True)  15.6 us
    pallas_call x10, Pallas kernels, run(): pl.pallas_call(kernel, out_shape=out_shape, scratch_shapes=list(scratch),...  9.93 us
    unnamed x18, local copies, waits for them, and re-layouts  4.59 us
  transfers between devices with their start and end apart: 1, of which 1 were waited for; matrix products, arithmetic and copies ran while one was open for 0% of the time, Pallas kernels for 1%

profile of v2, /device:TPU:24, one launch (start us, length us, event | category | flops | bytes accessed | tf_op | source)
XLA Modules:
  0.0 210.3 jit_solution(2121114755818172335)
XLA Ops:
  0.6 0.0 copy-start
  0.6 0.0 copy-start.6
  0.7 1.2 copy-done.6
  1.8 0.0 copy-start.7
  1.8 0.9 copy-done.7
  2.8 0.5 points.1
  3.3 36.1 %all_to_all.81 = bf16[32,16,128]{2,1,0:T(8,128)(2,1)S(1)} all-to-all(bf16[32,16,128]{2,1,0:T(8,128)(2,1)S(1)} %bitcast.20), channel_id=1, replica_groups=mesh['pitch'=32,'chan'=16] {'pitch'}, dimensions={0} | all-to-all | bytes 262144 | tf_op jit(solution)/shard_map/all_to_all | solution.py:208
  39.4 0.0 copy-start.5
  39.4 1.2 copy-done.5
  40.6 0.6 modes.1
  41.2 18.1 %all_to_all.82 = bf16[32,4,128]{2,1,0:T(4,128)(2,1)S(1)} all-to-all(bf16[32,4,128]{2,1,0:T(4,128)(2,1)S(1)} %bitcast.24), channel_id=1, replica_groups=mesh['pitch'=32,'chan'=16] {'pitch'}, dimensions={0} | all-to-all | bytes 65536 | tf_op jit(solution)/shard_map/all_to_all | solution.py:208
  59.3 0.1 gather.1
  59.3 13.2 %all_to_all.83.got_ref = bf16[16,128,128]{2,1,0:T(8,128)(2,1)S(1)} all-to-all(bf16[16,128,128]{2,1,0:T(8,128)(2,1)S(1)} %gather.1), channel_id=1, replica_groups=mesh['pitch'=32,'chan'=16] {'chan'}, dimensions={0} | all-to-all | bytes 1048576 | tf_op jit(solution)/shard_map/all_to_all | solution.py:208
  72.6 0.0 copy-start.1
  72.6 1.2 copy-done.1
  73.8 0.0 copy-start.2
  73.8 0.6 mix.1
  74.4 18.2 %all_to_all.84 = bf16[32,4,128]{2,1,0:T(4,128)(2,1)S(1)} all-to-all(bf16[32,4,128]{2,1,0:T(4,128)(2,1)S(1)} %bitcast.28), channel_id=1, replica_groups=mesh['pitch'=32,'chan'=16] {'pitch'}, dimensions={0} | all-to-all | bytes 65536 | tf_op jit(solution)/shard_map/all_to_all | solution.py:208
  92.6 0.0 copy-start.4
  92.6 37.3 %all_to_all.85.cot_ref = bf16[32,64,128]{2,1,0:T(8,128)(2,1)S(1)} all-to-all(bf16[32,64,128]{2,1,0:T(8,128)(2,1)} %cot_ref.1), channel_id=1, replica_groups=mesh['pitch'=32,'chan'=16] {'pitch'}, dimensions={0} | all-to-all | bytes 1048576 | tf_op jit(solution)/shard_map/all_to_all | solution.py:208
  129.8 0.7 broadcast_in_dim.2.bias_ref
  130.6 0.0 copy-done
  130.6 3.4 %pointwise.1 = bf16[256,128]{1,0:T(8,128)(2,1)S(1)} custom-call(bf16[128,128]{1,0:T(8,128)(2,1)S(1)} %bitcast.23, bf16[32,64,128]{2,1,0:T(8,128)(2,1)S(1)} %all_to_all.85.cot_ref, f32[64,128]{1,0:T(8,128)S(1)} %broadcast_in_dim.2.bias_ref, bf16[2,256,4096]{2,1,0:T(8,128)(2,1)S(1)} %copy-done), custom_call_target="tpu_custom_call" | custom-call | bytes 4849664 | tf_op jit(solution)/shard_map/pointwise/pallas_call | solution.py:60
  133.9 0.0 copy-start.3
  133.9 0.0 copy-start.8
  134.0 20.0 %all_to_all.86 = bf16[32,8,128]{2,1,0:T(8,128)(2,1)S(1)} all-to-all(bf16[32,8,128]{2,1,0:T(8,128)(2,1)S(1)} %bitcast.21), channel_id=1, replica_groups=mesh['pitch'=32,'chan'=16] {'pitch'}, dimensions={0} | all-to-all | bytes 131072 | tf_op jit(solution)/shard_map/all_to_all | solution.py:208
  153.9 0.0 copy-done.2
  153.9 0.6 back.1
  154.5 13.4 %all_to_all.87.got_ref = bf16[16,128,128]{2,1,0:T(8,128)(2,1)S(1)} all-to-all(bf16[16,128,128]{2,1,0:T(8,128)(2,1)S(1)} %get-tuple-element.9), channel_id=1, replica_groups=mesh['pitch'=32,'chan'=16] {'chan'}, dimensions={0} | all-to-all | bytes 1048576 | tf_op jit(solution)/shard_map/all_to_all | solution.py:208
  167.8 0.1 collect.1
  167.9 18.2 %all_to_all.88 = bf16[32,4,128]{2,1,0:T(4,128)(2,1)S(1)} all-to-all(bf16[32,4,128]{2,1,0:T(4,128)(2,1)S(1)} %bitcast.27), channel_id=1, replica_groups=mesh['pitch'=32,'chan'=16] {'pitch'}, dimensions={0} | all-to-all | bytes 65536 | tf_op jit(solution)/shard_map/all_to_all | solution.py:208
  186.1 0.0 copy-done.4
  186.1 1.2 windows.1
  187.3 3.9 %all-to-all-start.8 = ((bf16[32,16,128]{2,1,0:T(8,128)(2,1)}), bf16[32,16,128]{2,1,0:T(8,128)(2,1)S(1)}, u32[]{:S(2)}, u32[]{:S(2)}) async-start(bf16[32,16,128]{2,1,0:T(8,128)(2,1)} %bitcast.11), calls=%async_computation.8 | async-start | bytes 262144 | tf_op jit(solution)/shard_map/all_to_all | solution.py:208
  191.2 1.8 weight.1
  192.9 0.5 slice_bitcast_fusion
  193.5 15.6 %all-to-all-done.8 = bf16[32,16,128]{2,1,0:T(8,128)(2,1)S(1)} async-done(((bf16[32,16,128]{2,1,0:T(8,128)(2,1)}), bf16[32,16,128]{2,1,0:T(8,128)(2,1)S(1)}, u32[]{:S(2)}, u32[]{:S(2)}) %all-to-all-start.8) | async-done | bytes 131104 | tf_op jit(solution)/shard_map/all_to_all | solution.py:208
  209.0 0.0 copy-done.3
  209.0 0.0 copy-done.8
  209.0 1.3 finish.1
Async XLA Ops:
  0.6 129.9 %copy-start = (bf16[2,256,4096]{2,1,0:T(8,128)(2,1)S(1)}, bf16[2,256,4096]{2,1,0:T(8,128)(2,1)}, u32[]{:S(2)}) copy-start(bf16[2,256,4096]{2,1,0:T(8,128)(2,1)} %constant.11.clone.table_ref) | copy-start | bytes 12582916
  0.6 1.2 copy-start.6
  1.8 0.9 copy-start.7
  39.4 1.2 copy-start.5
  72.6 1.2 copy-start.1
  73.8 80.1 %copy-start.2 = (bf16[4,2,64,1024]{3,2,1,0:T(8,128)(2,1)S(1)}, bf16[4,2,64,1024]{3,2,1,0:T(8,128)(2,1)}, u32[]{:S(2)}) copy-start(bf16[4,2,64,1024]{3,2,1,0:T(8,128)(2,1)} %param.10) | copy-start | bytes 3145732
  92.6 93.5 %copy-start.4 = (bf16[2048,256]{1,0:T(8,128)(2,1)S(1)}, bf16[2048,256]{1,0:T(8,128)(2,1)}, u32[]{:S(2)}) copy-start(bf16[2048,256]{1,0:T(8,128)(2,1)} %constant.10.clone.u_ref) | copy-start | bytes 3145732
  133.9 75.1 %copy-start.3 = (bf16[32,64,128]{2,1,0:T(8,128)(2,1)S(1)}, bf16[32,64,128]{2,1,0:T(8,128)(2,1)}, u32[]{:S(2)}) copy-start(bf16[32,64,128]{2,1,0:T(8,128)(2,1)} %cot_ref.1) | copy-start | bytes 1572868
  133.9 75.1 %copy-start.8 = (bf16[64,128]{1,0:T(8,128)(2,1)S(1)}, bf16[64,128]{1,0:T(8,128)(2,1)}, u32[]{:S(2)}) copy-start(bf16[64,128]{1,0:T(8,128)(2,1)} %constant.8.clone.v_ref) | copy-start | bytes 49156
  187.3 21.7 %all-to-all-start.8 = ((bf16[32,16,128]{2,1,0:T(8,128)(2,1)}), bf16[32,16,128]{2,1,0:T(8,128)(2,1)S(1)}, u32[]{:S(2)}, u32[]{:S(2)}) async-start(bf16[32,16,128]{2,1,0:T(8,128)(2,1)} %bitcast.11), calls=%async_computation.8 | async-start | bytes 262144 | tf_op jit(solution)/shard_map/all_to_all | solution.py:208

commit v3 on v2

--- a/solution.py
+++ b/solution.py
@@ -22,6 +22,7 @@
 NN = (((1,), (0,)), ((), ()))
 TN = (((0,), (0,)), ((), ()))
 VMEM_LIMIT = 32 * 1024 * 1024
+FIRST_LIMIT = 60 * 1024 * 1024
 
 
 def split_hi_lo(table):
@@ -35,7 +36,6 @@
     modes = np.arange(M)
     angle = 2.0 * math.pi * (np.outer(modes, np.arange(P_SIZE)) % P_SIZE) / P_SIZE
     forward = np.stack([np.cos(angle), -np.sin(angle)]) / math.sqrt(P_SIZE)
-    doubled = forward * np.where(modes == 0, 1.0, 2.0)[:, None]
     basis = np.linalg.svd(forward[:, :, :WIN].reshape(2 * M, WIN))[2][:R]
     coef = np.einsum("akwp,xp->akwx", forward.reshape(2, M, PITCH, WIN), basis)
     coef = coef.reshape(2 * M, PITCH, 2, R // 2)
@@ -46,8 +46,11 @@
     out["modes"] = np.stack(split_hi_lo(gather), axis=1).reshape(8 * M, PITCH * R // 2)
     spread = coef.transpose(2, 1, 3, 0).reshape(PITCH * R, 2 * M)
     out["windows"] = np.concatenate(split_hi_lo(spread), axis=0)
-    whole = doubled.reshape(2, PITCH, KEPT, P_SIZE).transpose(0, 2, 1, 3).reshape(2 * M, P_SIZE)
-    out["doubled"] = np.stack(split_hi_lo(whole))
+    scale = np.where(modes == 0, 1.0, 2.0).reshape(1, PITCH, KEPT, 1)
+    scaled = coef.reshape(2, PITCH, KEPT, PITCH * R) * scale
+    out["doubled"] = np.stack(split_hi_lo(scaled.transpose(0, 2, 1, 3).reshape(2 * M, PITCH * R)))
+    high, low = split_hi_lo(np.kron(np.eye(4), basis))
+    out["expand"] = np.concatenate([high, high, low], axis=0)
     return out
 
 
@@ -55,13 +58,15 @@
     return lax.dot_general(left, right, dims, preferred_element_type=f32)
 
 
-def run(kernel, out_shape, *args, scratch=(), flops=0, name=None):
+def run(kernel, out_shape, *args, scratch=(), flops=0, name=None, far=0, vmem=VMEM_LIMIT):
+    near = [pl.BlockSpec(memory_space=pltpu.VMEM)] * (len(args) - far)
     touched = sum(int(np.prod(a.shape)) * a.dtype.itemsize for a in list(args) + jax.tree.leaves(out_shape))
     return pl.pallas_call(
         kernel,
         out_shape=out_shape,
+        in_specs=near + [pl.BlockSpec(memory_space=pltpu.HBM)] * far,
         scratch_shapes=list(scratch),
-        compiler_params=pltpu.CompilerParams(vmem_limit_bytes=VMEM_LIMIT),
+        compiler_params=pltpu.CompilerParams(vmem_limit_bytes=vmem),
         cost_estimate=pl.CostEstimate(flops=flops, bytes_accessed=touched, transcendentals=0),
         name=name,
     )(*args)
@@ -74,17 +79,28 @@
     )
 
 
-def points_kernel(x_ref, v_ref, out_ref):
+def points_kernel(v_ref, x_ref, cot_ref, out_ref, field, sems):
+    cot_copy = pltpu.make_async_copy(cot_ref, out_ref.at[:, R // 2 :, :], sems.at[4])
+    copies = [
+        pltpu.make_async_copy(x_ref.at[8 * i : 8 * i + 8], field.at[8 * i : 8 * i + 8], sems.at[i]) for i in range(4)
+    ]
+    for copy in copies:
+        copy.start()
+    cot_copy.start()
     for t in range(16):
-        field = x_ref[2 * t : 2 * t + 2].reshape(128, WIN)
-        y = dot(v_ref[...], field, NT)
+        if t % 4 == 0:
+            copies[t // 4].wait()
+        y = dot(v_ref[...], field[2 * t : 2 * t + 2].reshape(128, WIN), NT)
         y = y[:R] + y[R:]
         first, second = halves(y[:16], y[16:])
-        out_ref[t * 32 : (t + 1) * 32, :] = jnp.concatenate([first, second], axis=0).astype(bf16)
+        out_ref[2 * t, 0:16, :] = first.astype(bf16)
+        out_ref[2 * t + 1, 0:16, :] = second.astype(bf16)
+    cot_copy.wait()
 
 
 def modes_kernel(got_ref, g_ref, out_ref):
-    part = dot(g_ref[...], got_ref[...], NN)
+    got = got_ref[:, 0 : R // 2, :].reshape(PITCH * R // 2, 128)
+    part = dot(g_ref[...], got, NN)
     part = part[: 4 * M, :64] + part[4 * M :, 64:]
     part = part[: 2 * M] + part[2 * M :]
     out_ref[...] = jnp.concatenate([part[:M], part[M:]], axis=1).astype(bf16)
@@ -118,34 +134,48 @@
     out_ref[...] = scr[...].astype(bf16)
 
 
-def pointwise_kernel(got_ref, cot_ref, bias_ref, table_ref, out_ref, scr, send):
+def pointwise_kernel(got_ref, cot_ref, bias_ref, table_ref, e_ref, out_ref, scr, send):
     root = math.sqrt(2.0 / math.pi)
     mixed = jnp.concatenate(by_mode(scr, got_ref[...].astype(f32), KEPT), axis=0)
     mixed = mixed.T
     mixed = jnp.concatenate([mixed[:64], mixed[64:]], axis=1).astype(bf16)
     bias = bias_ref[...]
     total = jnp.zeros((64, WIN), f32)
-    modes = jnp.zeros((2 * M, 64), f32)
-    for chunk in range(8):
-        lanes = slice(chunk * 512, (chunk + 1) * 512)
-        high, low = table_ref[0, :, lanes], table_ref[1, :, lanes]
-        response = (dot(mixed, high, NN) + dot(mixed, low, NN)).astype(bf16).astype(f32)
-        grads = []
-        for i in range(4):
-            v = response[:, i * WIN : (i + 1) * WIN] + bias
-            square = v * v
-            th = jnp.tanh(root * (v + 0.044715 * (square * v)))
-            slope = 0.5 * (1.0 + th) + (0.5 * root) * v * (1.0 - th * th) * (1.0 + (3.0 * 0.044715) * square)
-            grad = slope * cot_ref[chunk * 4 + i].astype(f32)
-            total = total + grad
-            grads.append(grad.astype(bf16))
-        grads = jnp.concatenate(grads, axis=1)
-        modes = modes + dot(high, grads, NT) + dot(low, grads, NT)
+    high, low = table_ref[0], table_ref[1]
+    coef = dot(mixed, high, NN) + dot(mixed, low, NN)
+    ys = []
+    for half in range(2):
+        groups = range(4 * half, 4 * half + 4)
+        part = jnp.concatenate([coef[:, g * 128 : (g + 1) * 128] for g in groups], axis=0)
+        part_high = part.astype(bf16)
+        part_low = (part - part_high.astype(f32)).astype(bf16)
+        response = dot(jnp.concatenate([part_high, part_low, part_high], axis=1), e_ref[...], NN)
+        response = response.astype(bf16).astype(f32)
+        blocks = []
+        for j, g in enumerate(groups):
+            grads = []
+            for i in range(4):
+                v = response[j * 64 : (j + 1) * 64, i * WIN : (i + 1) * WIN] + bias
+                square = v * v
+                th = jnp.tanh(root * (v + 0.044715 * (square * v)))
+                slope = 0.5 * (1.0 + th) + (0.5 * root) * v * (1.0 - th * th) * (1.0 + (3.0 * 0.044715) * square)
+                grad = slope * cot_ref[4 * g + i, R // 2 :, :].astype(f32)
+                total = total + grad
+                grads.append(grad.astype(bf16))
+            blocks.append(jnp.concatenate(grads, axis=1))
+        y = dot(jnp.concatenate(blocks, axis=0), e_ref[128:, :], NT)
+        y = y[:, :128] + y[:, 128:]
+        ys += [y[j * 64 : (j + 1) * 64] for j in range(4)]
+    y = jnp.concatenate(ys, axis=1)
+    y_high = y.astype(bf16)
+    y_low = (y - y_high.astype(f32)).astype(bf16)
+    modes = dot(high, jnp.concatenate([y_high, y_low], axis=0), NT)
+    modes = modes[:, :64] + modes[:, 64:] + dot(low, y_high, NT)
     sums = lax.dot_general(
         jnp.ones((8, WIN), f32), total, NT, precision=lax.Precision.HIGHEST, preferred_element_type=f32
     )
-    high = sums.astype(bf16).astype(f32)
-    sums = jnp.concatenate([high, sums - high], axis=1)
+    rounded = sums.astype(bf16).astype(f32)
+    sums = jnp.concatenate([rounded, sums - rounded], axis=1)
     modes = jnp.concatenate([modes[:M], modes[M:]], axis=1)
     for k in range(KEPT):
         send[pl.ds(k, PITCH, stride=8), :] = modes[k * PITCH : (k + 1) * PITCH]
@@ -223,10 +253,19 @@
     across = shape((chan, M, 128), bf16)
     mix_flops = 2 * KEPT * 64 * 128 * inputs
 
-    coefs = run(points_kernel, coefs_shape, activation, const["points"], name="points")
-    coefs = exchange(coefs, "pitch")
-    span_cotangent = exchange(cotangent, "pitch")
-    spectra = run(modes_kernel, small, coefs, const["modes"], name="modes")
+    first = run(
+        points_kernel,
+        shape((PITCH, R // 2 + width, 128), bf16),
+        const["points"],
+        activation,
+        cotangent,
+        scratch=[pltpu.VMEM(activation.shape, bf16), pltpu.SemaphoreType.DMA((5,))],
+        far=2,
+        vmem=FIRST_LIMIT,
+        name="points",
+    )
+    first = exchange(first, "pitch")
+    spectra = run(modes_kernel, small, first, const["modes"], name="modes")
     spectra = exchange(spectra, "pitch")
     spectra = run(gather_kernel, across, spectra, scratch=[square], name="gather")
     spectra = exchange(spectra, "chan")
@@ -244,9 +283,10 @@
         pointwise_kernel,
         shape((2 * M, 128), bf16),
         mixed,
-        span_cotangent,
+        first,
         bias_wide,
         const["doubled"],
+        const["expand"],
         scratch=[square, tall],
         name="pointwise",
     )

time: 212 us -> 192 us (0.906)
  blocking collectives: 174 us -> 159 us
  local copies, waits for them, and re-layouts: 5.83 us -> 0.62 us
    all_to_all x8 -> x7, blocking collectives: 174 us -> 159 us  [exchange(): return lax.all_to_all(blocks, axis, split_axis=0, concat_axis=0, tiled=True)]
    unnamed x18 -> x16, local copies, waits for them, and re-layouts: 4.59 us -> 0.04 us
where the time goes in v3:
time: 192 us; the launch traced here: 191 us
  blocking collectives  159 us (83%)
  waiting for transfers between devices  15.6 us (8%)
  Pallas kernels  11.5 us (6%)
  starting transfers between devices  3.86 us (2%)
    all_to_all x7, blocking collectives, exchange(): return lax.all_to_all(blocks, axis, split_axis=0, concat_axis=0, tiled=True)  159 us
    all_to_all x1, waiting for transfers between devices, exchange(): return lax.all_to_all(blocks, axis, split_axis=0, concat_axis=0, tiled=True)  15.6 us
    pallas_call x10, Pallas kernels, run(): pl.pallas_call(kernel, out_shape=out_shape, in_specs=near + [pl.BlockSpec...  11.5 us
    all_to_all x1, starting transfers between devices, exchange(): return lax.all_to_all(blocks, axis, split_axis=0, concat_axis=0, tiled=True)  3.86 us
  transfers between devices with their start and end apart: 1, of which 1 were waited for; matrix products, arithmetic and copies ran while one was open for 0% of the time, Pallas kernels for 1%

profile of v3, /device:TPU:24, one launch (start us, length us, event | category | flops | bytes accessed | tf_op | source)
XLA Modules:
  0.0 190.8 jit_solution(8531208382811603405)
XLA Ops:
  0.6 0.0 copy-start.4
  0.6 3.7 %points.1 = bf16[32,80,128]{2,1,0:T(8,128)(2,1)} custom-call(bf16[64,128]{1,0:T(8,128)(2,1)} %constant.10.clone.v_ref, bf16[32,64,128]{2,1,0:T(8,128)(2,1)} %x_ref.1, bf16[32,64,128]{2,1,0:T(8,128)(2,1)} %cot_ref.3), custom_call_target="tpu_custom_call" | custom-call | bytes 1720320 | tf_op jit(solution)/shard_map/points/pallas_call | solution.py:64
  4.3 0.0 copy-start
  4.3 55.6 %all_to_all.70.got_ref.cot_ref = bf16[32,80,128]{2,1,0:T(8,128)(2,1)S(1)} all-to-all(bf16[32,80,128]{2,1,0:T(8,128)(2,1)} %points.1), channel_id=1, replica_groups=mesh['pitch'=32,'chan'=16] {'pitch'}, dimensions={0} | all-to-all | bytes 1310720 | tf_op jit(solution)/shard_map/all_to_all | solution.py:238
  59.9 0.0 copy-done.4
  59.9 0.0 copy-start.7
  59.9 0.6 modes.1
  60.5 0.0 copy-start.3
  60.5 0.0 copy-start.5
  60.5 21.2 %all_to_all.71 = bf16[32,4,128]{2,1,0:T(4,128)(2,1)S(1)} all-to-all(bf16[32,4,128]{2,1,0:T(4,128)(2,1)S(1)} %bitcast.21), channel_id=1, replica_groups=mesh['pitch'=32,'chan'=16] {'pitch'}, dimensions={0} | all-to-all | bytes 65536 | tf_op jit(solution)/shard_map/all_to_all | solution.py:238
  81.7 0.1 gather.1
  81.7 13.2 %all_to_all.72.got_ref = bf16[16,128,128]{2,1,0:T(8,128)(2,1)S(1)} all-to-all(bf16[16,128,128]{2,1,0:T(8,128)(2,1)S(1)} %gather.1), channel_id=1, replica_groups=mesh['pitch'=32,'chan'=16] {'chan'}, dimensions={0} | all-to-all | bytes 1048576 | tf_op jit(solution)/shard_map/all_to_all | solution.py:238
  95.0 0.0 copy-done
  95.0 0.6 mix.1
  95.6 18.2 %all_to_all.73 = bf16[32,4,128]{2,1,0:T(4,128)(2,1)S(1)} all-to-all(bf16[32,4,128]{2,1,0:T(4,128)(2,1)S(1)} %bitcast.24), channel_id=1, replica_groups=mesh['pitch'=32,'chan'=16] {'pitch'}, dimensions={0} | all-to-all | bytes 65536 | tf_op jit(solution)/shard_map/all_to_all | solution.py:238
  113.7 0.0 copy-done.7
  113.7 0.1 broadcast_in_dim.2.bias_ref
  113.8 0.0 copy-done.3
  113.8 0.0 copy-done.5
  113.8 0.0 copy-start.2
  113.8 1.8 pointwise.1
  115.6 18.7 %all_to_all.74 = bf16[32,8,128]{2,1,0:T(8,128)(2,1)S(1)} all-to-all(bf16[32,8,128]{2,1,0:T(8,128)(2,1)S(1)} %bitcast.17), channel_id=1, replica_groups=mesh['pitch'=32,'chan'=16] {'pitch'}, dimensions={0} | all-to-all | bytes 131072 | tf_op jit(solution)/shard_map/all_to_all | solution.py:238
  134.3 0.6 back.1
  134.9 13.5 %all_to_all.75.got_ref = bf16[16,128,128]{2,1,0:T(8,128)(2,1)S(1)} all-to-all(bf16[16,128,128]{2,1,0:T(8,128)(2,1)S(1)} %get-tuple-element.9), channel_id=1, replica_groups=mesh['pitch'=32,'chan'=16] {'chan'}, dimensions={0} | all-to-all | bytes 1048576 | tf_op jit(solution)/shard_map/all_to_all | solution.py:238
  148.4 0.1 collect.1
  148.4 18.2 %all_to_all.76 = bf16[32,4,128]{2,1,0:T(4,128)(2,1)S(1)} all-to-all(bf16[32,4,128]{2,1,0:T(4,128)(2,1)S(1)} %bitcast.23), channel_id=1, replica_groups=mesh['pitch'=32,'chan'=16] {'pitch'}, dimensions={0} | all-to-all | bytes 65536 | tf_op jit(solution)/shard_map/all_to_all | solution.py:238
  166.6 0.0 copy-start.1
  166.6 0.0 copy-start.6
  166.6 0.0 copy-done.2
  166.6 1.2 windows.1
  167.8 3.9 %all-to-all-start.7 = ((bf16[32,16,128]{2,1,0:T(8,128)(2,1)}), bf16[32,16,128]{2,1,0:T(8,128)(2,1)S(1)}, u32[]{:S(2)}, u32[]{:S(2)}) async-start(bf16[32,16,128]{2,1,0:T(8,128)(2,1)} %bitcast.9), calls=%async_computation.7 | async-start | bytes 262144 | tf_op jit(solution)/shard_map/all_to_all | solution.py:238
  171.7 1.8 weight.1
  173.5 0.5 slice_bitcast_fusion
  174.0 15.6 %all-to-all-done.7 = bf16[32,16,128]{2,1,0:T(8,128)(2,1)S(1)} async-done(((bf16[32,16,128]{2,1,0:T(8,128)(2,1)}), bf16[32,16,128]{2,1,0:T(8,128)(2,1)S(1)}, u32[]{:S(2)}, u32[]{:S(2)}) %all-to-all-start.7) | async-done | bytes 131104 | tf_op jit(solution)/shard_map/all_to_all | solution.py:238
  189.6 0.0 copy-done.1
  189.6 0.0 copy-done.6
  189.6 1.3 finish.1
Async XLA Ops:
  0.6 59.3 %copy-start.4 = (bf16[1024,512]{1,0:T(8,128)(2,1)S(1)}, bf16[1024,512]{1,0:T(8,128)(2,1)}, u32[]{:S(2)}) copy-start(bf16[1024,512]{1,0:T(8,128)(2,1)} %constant.11.clone.g_ref) | copy-start | bytes 3145732
  4.3 90.6 %copy-start = (bf16[4,2,64,1024]{3,2,1,0:T(8,128)(2,1)S(1)}, bf16[4,2,64,1024]{3,2,1,0:T(8,128)(2,1)}, u32[]{:S(2)}) copy-start(bf16[4,2,64,1024]{3,2,1,0:T(8,128)(2,1)} %param.11) | copy-start | bytes 3145732
  59.9 53.8 %copy-start.7 = (f32[64]{0:T(128)S(1)}, f32[64]{0:T(128)}, u32[]{:S(2)}) copy-start(f32[64]{0:T(128)} %param.12) | copy-start | bytes 772
  60.5 53.3 %copy-start.3 = (bf16[2,256,1024]{2,1,0:T(8,128)(2,1)S(1)}, bf16[2,256,1024]{2,1,0:T(8,128)(2,1)}, u32[]{:S(2)}) copy-start(bf16[2,256,1024]{2,1,0:T(8,128)(2,1)} %constant.13.clone.table_ref) | copy-start | bytes 3145732
  60.5 53.3 %copy-start.5 = (bf16[384,512]{1,0:T(8,128)(2,1)S(1)}, bf16[384,512]{1,0:T(8,128)(2,1)}, u32[]{:S(2)}) copy-start(bf16[384,512]{1,0:T(8,128)(2,1)} %constant.14.clone.e_ref) | copy-start | bytes 1179652
  113.8 52.8 %copy-start.2 = (bf16[2048,256]{1,0:T(8,128)(2,1)S(1)}, bf16[2048,256]{1,0:T(8,128)(2,1)}, u32[]{:S(2)}) copy-start(bf16[2048,256]{1,0:T(8,128)(2,1)} %constant.12.clone.u_ref) | copy-start | bytes 3145732
  166.6 23.0 %copy-start.1 = (bf16[32,64,128]{2,1,0:T(8,128)(2,1)S(1)}, bf16[32,64,128]{2,1,0:T(8,128)(2,1)}, u32[]{:S(2)}) copy-start(bf16[32,64,128]{2,1,0:T(8,128)(2,1)} %cot_ref.3) | copy-start | bytes 1572868
  166.6 23.0 %copy-start.6 = (bf16[64,128]{1,0:T(8,128)(2,1)S(1)}, bf16[64,128]{1,0:T(8,128)(2,1)}, u32[]{:S(2)}) copy-start(bf16[64,128]{1,0:T(8,128)(2,1)} %constant.10.clone.v_ref) | copy-start | bytes 49156
  167.8 21.7 %all-to-all-start.7 = ((bf16[32,16,128]{2,1,0:T(8,128)(2,1)}), bf16[32,16,128]{2,1,0:T(8,128)(2,1)S(1)}, u32[]{:S(2)}, u32[]{:S(2)}) async-start(bf16[32,16,128]{2,1,0:T(8,128)(2,1)} %bitcast.9), calls=%async_computation.7 | async-start | bytes 262144 | tf_op jit(solution)/shard_map/all_to_all | solution.py:238

commit v4 on v3

--- a/solution.py
+++ b/solution.py
@@ -8,14 +8,18 @@
 from jax import lax
 from jax.experimental import pallas as pl
 from jax.experimental.pallas import tpu as pltpu
+from jax.sharding import Mesh
 from jax.sharding import PartitionSpec as P
 
 P_SIZE = 4096
 M = 128
-PITCH = 32
+XH = 2
+Z = 16
+PITCH = XH * Z
 WIN = P_SIZE // PITCH
 KEPT = M // PITCH
 R = 32
+PITCH_AXES = ("xh", "z")
 f32 = jnp.float32
 bf16 = jnp.bfloat16
 NT = (((1,), (1,)), ((), ()))
@@ -42,9 +46,10 @@
     out = {}
     hi, lo = split_hi_lo(basis)
     out["points"] = np.concatenate([hi, lo], axis=0)
-    gather = coef.transpose(2, 0, 1, 3).reshape(2, 2 * M, PITCH * R // 2)
+    by_z = coef.reshape(2, XH, Z, KEPT, PITCH, 2, R // 2).transpose(5, 0, 2, 1, 3, 4, 6)
+    gather = by_z.reshape(2, 2 * M, PITCH * R // 2)
     out["modes"] = np.stack(split_hi_lo(gather), axis=1).reshape(8 * M, PITCH * R // 2)
-    spread = coef.transpose(2, 1, 3, 0).reshape(PITCH * R, 2 * M)
+    spread = coef.transpose(1, 3, 2, 0).reshape(PITCH * R // 2, 4 * M)
     out["windows"] = np.concatenate(split_hi_lo(spread), axis=0)
     scale = np.where(modes == 0, 1.0, 2.0).reshape(1, PITCH, KEPT, 1)
     scaled = coef.reshape(2, PITCH, KEPT, PITCH * R) * scale
@@ -58,13 +63,15 @@
     return lax.dot_general(left, right, dims, preferred_element_type=f32)
 
 
-def run(kernel, out_shape, *args, scratch=(), flops=0, name=None, far=0, vmem=VMEM_LIMIT):
+def run(kernel, out_shape, *args, scratch=(), flops=0, name=None, far=0, far_out=False, vmem=VMEM_LIMIT):
+    out_space = pltpu.HBM if far_out else pltpu.VMEM
     near = [pl.BlockSpec(memory_space=pltpu.VMEM)] * (len(args) - far)
     touched = sum(int(np.prod(a.shape)) * a.dtype.itemsize for a in list(args) + jax.tree.leaves(out_shape))
     return pl.pallas_call(
         kernel,
         out_shape=out_shape,
         in_specs=near + [pl.BlockSpec(memory_space=pltpu.HBM)] * far,
+        out_specs=jax.tree.map(lambda _: pl.BlockSpec(memory_space=out_space), out_shape),
         scratch_shapes=list(scratch),
         compiler_params=pltpu.CompilerParams(vmem_limit_bytes=vmem),
         cost_estimate=pl.CostEstimate(flops=flops, bytes_accessed=touched, transcendentals=0),
@@ -79,23 +86,31 @@
     )
 
 
-def points_kernel(v_ref, x_ref, cot_ref, out_ref, field, sems):
-    cot_copy = pltpu.make_async_copy(cot_ref, out_ref.at[:, R // 2 :, :], sems.at[4])
-    copies = [
-        pltpu.make_async_copy(x_ref.at[8 * i : 8 * i + 8], field.at[8 * i : 8 * i + 8], sems.at[i]) for i in range(4)
-    ]
+def points_kernel(v_ref, x_ref, cot_ref, out_ref, basis, field, coefs, sems):
+    copies = [pltpu.make_async_copy(v_ref, basis, sems.at[12])]
+    for i in range(4):
+        part = slice(8 * i, 8 * i + 8)
+        copies.append(pltpu.make_async_copy(x_ref.at[part], field.at[part], sems.at[i]))
+    for i in range(4):
+        part = slice(8 * i, 8 * i + 8)
+        copies.append(pltpu.make_async_copy(cot_ref.at[part], out_ref.at[part, R // 2 :, :], sems.at[4 + i]))
     for copy in copies:
         copy.start()
-    cot_copy.start()
-    for t in range(16):
-        if t % 4 == 0:
-            copies[t // 4].wait()
-        y = dot(v_ref[...], field[2 * t : 2 * t + 2].reshape(128, WIN), NT)
-        y = y[:R] + y[R:]
-        first, second = halves(y[:16], y[16:])
-        out_ref[2 * t, 0:16, :] = first.astype(bf16)
-        out_ref[2 * t + 1, 0:16, :] = second.astype(bf16)
-    cot_copy.wait()
+    copies[0].wait()
+    sends = []
+    for i in range(4):
+        copies[1 + i].wait()
+        for t in range(4 * i, 4 * i + 4):
+            y = dot(basis[...], field[2 * t : 2 * t + 2].reshape(128, WIN), NT)
+            y = y[:R] + y[R:]
+            first, second = halves(y[:16], y[16:])
+            coefs[2 * t] = first.astype(bf16)
+            coefs[2 * t + 1] = second.astype(bf16)
+        part = slice(8 * i, 8 * i + 8)
+        sends.append(pltpu.make_async_copy(coefs.at[part], out_ref.at[part, 0 : R // 2, :], sems.at[8 + i]))
+        sends[i].start()
+    for copy in sends + copies[5:]:
+        copy.wait()
 
 
 def modes_kernel(got_ref, g_ref, out_ref):
@@ -112,17 +127,25 @@
 
 
 def gather_kernel(got_ref, out_ref, scr):
-    send = jnp.concatenate(by_mode(scr, got_ref[...].astype(f32), KEPT), axis=0).astype(bf16)
-    for i in range(out_ref.shape[0]):
-        out_ref[i] = send
+    scr[...] = got_ref[...].astype(f32)
+    each = out_ref.shape[0] // XH
+    for a in range(XH):
+        rows = [scr[pl.ds(a * KEPT + k, Z, stride=XH * KEPT), :] for k in range(KEPT)]
+        send = jnp.concatenate(rows, axis=0).astype(bf16)
+        for i in range(each):
+            out_ref[a * each + i] = send
 
 
 def mix_kernel(got_ref, weight_ref, out_ref, spec_ref, scr):
     for k in range(KEPT):
-        rows = slice(k * PITCH, (k + 1) * PITCH)
+        rows = slice(k * Z, (k + 1) * Z)
+        chan = got_ref.shape[0] // XH
         re, im = [], []
-        for q in range(got_ref.shape[0] // 2):
-            first, second = halves(got_ref[2 * q, rows, :], got_ref[2 * q + 1, rows, :])
+        for q in range(chan // 2):
+            left, right = [
+                jnp.concatenate([got_ref[c, rows, :], got_ref[chan + c, rows, :]], axis=0) for c in (2 * q, 2 * q + 1)
+            ]
+            first, second = halves(left, right)
             re.append(first)
             im.append(second)
         spec = jnp.concatenate([jnp.concatenate(re, axis=1), jnp.concatenate(im, axis=1)], axis=0)
@@ -218,20 +241,35 @@
 
 
 def windows_kernel(got_ref, u_ref, out_ref):
-    got = jnp.concatenate([got_ref[:, :64], got_ref[:, 64:]], axis=0)
-    out = dot(u_ref[...], got, NN)
-    half = PITCH * R
-    out = out[:half] + out[half:]
-    out_ref[...] = jnp.concatenate([out[: half // 2], out[half // 2 :]], axis=1).astype(bf16)
-
-
-def finish_kernel(got_ref, cot_ref, v_ref, out_ref):
+    got = got_ref[...]
+    turned = jnp.concatenate([got[:, 64:], got[:, :64]], axis=1)
+    low = lax.broadcasted_iota(jnp.int32, got.shape, 1) < 64
+    none = jnp.zeros_like(got)
+    parts = [
+        jnp.where(low, got, none),
+        jnp.where(low, turned, none),
+        jnp.where(low, none, turned),
+        jnp.where(low, none, got),
+    ]
+    out = dot(u_ref[...], jnp.concatenate(parts, axis=0), NN)
+    half = out.shape[0] // 2
+    out_ref[...] = (out[:half] + out[half:]).astype(bf16)
+
+
+def finish_kernel(got_ref, cot_ref, v_ref, out_ref, field, sems):
+    sends = []
     for t in range(16):
         low, high = halves(got_ref[t * 32 : t * 32 + 16, :], got_ref[t * 32 + 16 : t * 32 + 32, :])
         coef = jnp.concatenate([low, high, low, high], axis=0)
-        field = dot(coef, v_ref[...], TN).astype(bf16).astype(f32).reshape(2, 64, WIN)
+        part = dot(coef, v_ref[...], TN).astype(bf16).astype(f32).reshape(2, 64, WIN)
         rows = slice(2 * t, 2 * t + 2)
-        out_ref[rows] = (cot_ref[rows].astype(f32) + field).astype(bf16)
+        field[rows] = (cot_ref[rows].astype(f32) + part).astype(bf16)
+        if t % 4 == 3:
+            done = slice(2 * t - 6, 2 * t + 2)
+            sends.append(pltpu.make_async_copy(field.at[done], out_ref.at[done], sems.at[t // 4]))
+            sends[-1].start()
+    for send in sends:
+        send.wait()
 
 
 def exchange(blocks, axis):
@@ -259,16 +297,22 @@
         const["points"],
         activation,
         cotangent,
-        scratch=[pltpu.VMEM(activation.shape, bf16), pltpu.SemaphoreType.DMA((5,))],
-        far=2,
+        scratch=[
+            pltpu.VMEM((2 * R, WIN), bf16),
+            pltpu.VMEM(activation.shape, bf16),
+            pltpu.VMEM((PITCH, R // 2, 128), bf16),
+            pltpu.SemaphoreType.DMA((13,)),
+        ],
+        far=3,
+        far_out=True,
         vmem=FIRST_LIMIT,
         name="points",
     )
-    first = exchange(first, "pitch")
+    first = exchange(first, PITCH_AXES)
     spectra = run(modes_kernel, small, first, const["modes"], name="modes")
-    spectra = exchange(spectra, "pitch")
-    spectra = run(gather_kernel, across, spectra, scratch=[square], name="gather")
-    spectra = exchange(spectra, "chan")
+    spectra = exchange(spectra, "z")
+    spectra = run(gather_kernel, shape((XH * chan, M // XH, 128), bf16), spectra, scratch=[square], name="gather")
+    spectra = exchange(spectra, ("xh", "chan"))
     mixed, spec = run(
         mix_kernel,
         (small, shape((KEPT, 64, inputs), bf16)),
@@ -278,7 +322,7 @@
         flops=mix_flops,
         name="mix",
     )
-    mixed = exchange(mixed, "pitch")
+    mixed = exchange(mixed, PITCH_AXES)
     grads = run(
         pointwise_kernel,
         shape((2 * M, 128), bf16),
@@ -290,7 +334,7 @@
         scratch=[square, tall],
         name="pointwise",
     )
-    grads = exchange(grads, "pitch")
+    grads = exchange(grads, PITCH_AXES)
     back, grad, bias = run(
         back_kernel,
         (across, shape((KEPT, 64, 128), bf16), shape((8, 64), f32)),
@@ -305,21 +349,29 @@
         weight_kernel, shape((KEPT, 2 * width, inputs), f32), grad, spec, flops=mix_flops, name="weight"
     )
     back = run(collect_kernel, small, back, scratch=[square], name="collect")
-    back = exchange(back, "pitch")
+    back = exchange(back, PITCH_AXES)
     coefs = run(windows_kernel, coefs_shape, back, const["windows"], name="windows")
-    coefs = exchange(coefs, "pitch")
+    coefs = exchange(coefs, PITCH_AXES)
     grad_input = run(
-        finish_kernel, shape(activation.shape, bf16), coefs, cotangent, const["points"], name="finish"
+        finish_kernel,
+        shape(activation.shape, bf16),
+        coefs,
+        cotangent,
+        const["points"],
+        scratch=[pltpu.VMEM(activation.shape, bf16), pltpu.SemaphoreType.DMA((4,))],
+        far_out=True,
+        name="finish",
     )
     return grad_input, grad_weight.reshape(spectral_weight.shape), bias[0]
 
 
 def solution(mesh):
-    field = P(None, "chan", "pitch")
-    modes = P("pitch", None, "chan", None)
+    fine = Mesh(mesh.devices.reshape(XH, Z, -1), ("xh", "z", "chan"))
+    field = P(None, "chan", ("xh", "z"))
+    modes = P(("xh", "z"), None, "chan", None)
     return jax.shard_map(
         body,
-        mesh=mesh,
+        mesh=fine,
         in_specs=(field, field, modes, P("chan")),
         out_specs=(field, modes, P("chan")),
         check_vma=False,

time: 192 us -> 204 us (1.062)
  Pallas kernels: 11.5 us -> 24.8 us
    pallas_call x10, Pallas kernels: 11.5 us -> 24.8 us  [run(): pl.pallas_call(kernel, out_shape=out_shape, in_specs=near + [pl.BlockSpec...]
where the time goes in v4:
time: 204 us; the launch traced here: 203 us
  blocking collectives  157 us (77%)
  Pallas kernels  24.8 us (12%)
  waiting for transfers between devices  15.6 us (8%)
  starting transfers between devices  3.86 us (2%)
    all_to_all x7, blocking collectives, exchange(): return lax.all_to_all(blocks, axis, split_axis=0, concat_axis=0, tiled=True)  157 us
    pallas_call x10, Pallas kernels, run(): pl.pallas_call(kernel, out_shape=out_shape, in_specs=near + [pl.BlockSpec...  24.8 us
    all_to_all x1, waiting for transfers between devices, exchange(): return lax.all_to_all(blocks, axis, split_axis=0, concat_axis=0, tiled=True)  15.6 us
  transfers between devices with their start and end apart: 1, of which 1 were waited for; matrix products, arithmetic and copies ran while one was open for 0% of the time, Pallas kernels for 1%

profile of v4, /device:TPU:24, one launch (start us, length us, event | category | flops | bytes accessed | tf_op | source)
XLA Modules:
  0.0 202.7 jit_solution(17119785403789030329)
XLA Ops:
  0.6 0.0 copy-start.4
  0.6 17.1 %points.1 = bf16[32,80,128]{2,1,0:T(8,128)(2,1)} custom-call(bf16[64,128]{1,0:T(8,128)(2,1)} %constant.10.clone.v_ref, bf16[32,64,128]{2,1,0:T(8,128)(2,1)} %x_ref.1, bf16[32,64,128]{2,1,0:T(8,128)(2,1)} %cot_ref.3), custom_call_target="tpu_custom_call" | custom-call | bytes 1720320 | tf_op jit(solution)/shard_map/points/pallas_call | solution.py:70
  17.8 0.0 copy-start
  17.8 55.6 %all_to_all.70.got_ref.cot_ref = bf16[32,80,128]{2,1,0:T(8,128)(2,1)S(1)} all-to-all(bf16[32,80,128]{2,1,0:T(8,128)(2,1)} %points.1), channel_id=1, replica_groups=mesh['xh'=2,'z'=16,'chan'=16] {'xh','z'}, dimensions={0} | all-to-all | bytes 1310720 | tf_op jit(solution)/shard_map/all_to_all | solution.py:276
  73.3 0.0 copy-done.4
  73.3 0.0 copy-start.7
  73.3 0.6 modes.1
  73.9 0.0 copy-start.3
  73.9 0.0 copy-start.5
  73.9 18.3 %all_to_all.71 = bf16[16,8,128]{2,1,0:T(8,128)(2,1)S(1)} all-to-all(bf16[16,8,128]{2,1,0:T(8,128)(2,1)S(1)} %bitcast.21), channel_id=1, replica_groups=mesh['xh'=2,'z'=16,'chan'=16] {'z'}, dimensions={0} | all-to-all | bytes 65536 | tf_op jit(solution)/shard_map/all_to_all | solution.py:276
  92.2 0.1 gather.1
  92.3 14.4 %all_to_all.72.got_ref = bf16[32,64,128]{2,1,0:T(8,128)(2,1)S(1)} all-to-all(bf16[32,64,128]{2,1,0:T(8,128)(2,1)S(1)} %gather.1), channel_id=1, replica_groups=mesh['xh'=2,'z'=16,'chan'=16] {'xh','chan'}, dimensions={0} | all-to-all | bytes 1048576 | tf_op jit(solution)/shard_map/all_to_all | solution.py:276
  106.7 0.0 copy-done
  106.7 0.6 mix.1
  107.3 18.4 %all_to_all.73 = bf16[32,4,128]{2,1,0:T(4,128)(2,1)S(1)} all-to-all(bf16[32,4,128]{2,1,0:T(4,128)(2,1)S(1)} %bitcast.24), channel_id=1, replica_groups=mesh['xh'=2,'z'=16,'chan'=16] {'xh','z'}, dimensions={0} | all-to-all | bytes 65536 | tf_op jit(solution)/shard_map/all_to_all | solution.py:276
  125.7 0.0 copy-done.7
  125.7 0.1 broadcast_in_dim.2.bias_ref
  125.8 0.0 copy-done.3
  125.8 0.0 copy-done.5
  125.8 0.0 copy-start.2
  125.8 1.8 pointwise.1
  127.6 18.7 %all_to_all.74 = bf16[32,8,128]{2,1,0:T(8,128)(2,1)S(1)} all-to-all(bf16[32,8,128]{2,1,0:T(8,128)(2,1)S(1)} %bitcast.17), channel_id=1, replica_groups=mesh['xh'=2,'z'=16,'chan'=16] {'xh','z'}, dimensions={0} | all-to-all | bytes 131072 | tf_op jit(solution)/shard_map/all_to_all | solution.py:276
  146.3 0.6 back.1
  146.9 13.5 %all_to_all.75.got_ref = bf16[16,128,128]{2,1,0:T(8,128)(2,1)S(1)} all-to-all(bf16[16,128,128]{2,1,0:T(8,128)(2,1)S(1)} %get-tuple-element.9), channel_id=1, replica_groups=mesh['xh'=2,'z'=16,'chan'=16] {'chan'}, dimensions={0} | all-to-all | bytes 1048576 | tf_op jit(solution)/shard_map/all_to_all | solution.py:276
  160.4 0.1 collect.1
  160.4 18.2 %all_to_all.76 = bf16[32,4,128]{2,1,0:T(4,128)(2,1)S(1)} all-to-all(bf16[32,4,128]{2,1,0:T(4,128)(2,1)S(1)} %bitcast.23), channel_id=1, replica_groups=mesh['xh'=2,'z'=16,'chan'=16] {'xh','z'}, dimensions={0} | all-to-all | bytes 65536 | tf_op jit(solution)/shard_map/all_to_all | solution.py:276
  178.6 0.0 copy-start.1
  178.6 0.0 copy-start.6
  178.6 0.0 copy-done.2
  178.6 1.2 windows.1
  179.8 3.9 %all-to-all-start.7 = ((bf16[32,16,128]{2,1,0:T(8,128)(2,1)}), bf16[32,16,128]{2,1,0:T(8,128)(2,1)S(1)}, u32[]{:S(2)}, u32[]{:S(2)}) async-start(bf16[32,16,128]{2,1,0:T(8,128)(2,1)} %bitcast.9), calls=%async_computation.7 | async-start | bytes 262144 | tf_op jit(solution)/shard_map/all_to_all | solution.py:276
  183.6 1.8 weight.1
  185.4 0.5 slice_bitcast_fusion
  185.9 15.6 %all-to-all-done.7 = bf16[32,16,128]{2,1,0:T(8,128)(2,1)S(1)} async-done(((bf16[32,16,128]{2,1,0:T(8,128)(2,1)}), bf16[32,16,128]{2,1,0:T(8,128)(2,1)S(1)}, u32[]{:S(2)}, u32[]{:S(2)}) %all-to-all-start.7) | async-done | bytes 131104 | tf_op jit(solution)/shard_map/all_to_all | solution.py:276
  201.5 0.0 copy-done.1
  201.5 0.0 copy-done.6
  201.5 1.2 finish.1
Async XLA Ops:
  0.6 72.7 %copy-start.4 = (bf16[1024,512]{1,0:T(8,128)(2,1)S(1)}, bf16[1024,512]{1,0:T(8,128)(2,1)}, u32[]{:S(2)}) copy-start(bf16[1024,512]{1,0:T(8,128)(2,1)} %constant.11.clone.g_ref) | copy-start | bytes 3145732
  17.8 89.0 %copy-start = (bf16[4,2,64,1024]{3,2,1,0:T(8,128)(2,1)S(1)}, bf16[4,2,64,1024]{3,2,1,0:T(8,128)(2,1)}, u32[]{:S(2)}) copy-start(bf16[4,2,64,1024]{3,2,1,0:T(8,128)(2,1)} %param.11) | copy-start | bytes 3145732
  73.3 52.4 %copy-start.7 = (f32[64]{0:T(128)S(1)}, f32[64]{0:T(128)}, u32[]{:S(2)}) copy-start(f32[64]{0:T(128)} %param.12) | copy-start | bytes 772
  73.9 51.9 %copy-start.3 = (bf16[2,256,1024]{2,1,0:T(8,128)(2,1)S(1)}, bf16[2,256,1024]{2,1,0:T(8,128)(2,1)}, u32[]{:S(2)}) copy-start(bf16[2,256,1024]{2,1,0:T(8,128)(2,1)} %constant.13.clone.table_ref) | copy-start | bytes 3145732
  73.9 51.9 %copy-start.5 = (bf16[384,512]{1,0:T(8,128)(2,1)S(1)}, bf16[384,512]{1,0:T(8,128)(2,1)}, u32[]{:S(2)}) copy-start(bf16[384,512]{1,0:T(8,128)(2,1)} %constant.14.clone.e_ref) | copy-start | bytes 1179652
  125.8 52.8 %copy-start.2 = (bf16[1024,512]{1,0:T(8,128)(2,1)S(1)}, bf16[1024,512]{1,0:T(8,128)(2,1)}, u32[]{:S(2)}) copy-start(bf16[1024,512]{1,0:T(8,128)(2,1)} %constant.12.clone.u_ref) | copy-start | bytes 3145732
  178.6 22.9 %copy-start.1 = (bf16[32,64,128]{2,1,0:T(8,128)(2,1)S(1)}, bf16[32,64,128]{2,1,0:T(8,128)(2,1)}, u32[]{:S(2)}) copy-start(bf16[32,64,128]{2,1,0:T(8,128)(2,1)} %cot_ref.3) | copy-start | bytes 1572868
  178.6 22.9 %copy-start.6 = (bf16[64,128]{1,0:T(8,128)(2,1)S(1)}, bf16[64,128]{1,0:T(8,128)(2,1)}, u32[]{:S(2)}) copy-start(bf16[64,128]{1,0:T(8,128)(2,1)} %constant.10.clone.v_ref) | copy-start | bytes 49156
  179.8 21.7 %all-to-all-start.7 = ((bf16[32,16,128]{2,1,0:T(8,128)(2,1)}), bf16[32,16,128]{2,1,0:T(8,128)(2,1)S(1)}, u32[]{:S(2)}, u32[]{:S(2)}) async-start(bf16[32,16,128]{2,1,0:T(8,128)(2,1)} %bitcast.9), calls=%async_computation.7 | async-start | bytes 262144 | tf_op jit(solution)/shard_map/all_to_all | solution.py:276

commit v5 on v4

--- a/solution.py
+++ b/solution.py
@@ -18,6 +18,7 @@
 PITCH = XH * Z
 WIN = P_SIZE // PITCH
 KEPT = M // PITCH
+EARLY = 32
 R = 32
 PITCH_AXES = ("xh", "z")
 f32 = jnp.float32
@@ -86,31 +87,33 @@
     )
 
 
-def points_kernel(v_ref, x_ref, cot_ref, out_ref, basis, field, coefs, sems):
-    copies = [pltpu.make_async_copy(v_ref, basis, sems.at[12])]
+def points_kernel(v_ref, x_ref, cot_ref, out_ref, basis, field, message, sems):
+    table = pltpu.make_async_copy(v_ref, basis, sems.at[12])
+    fields, cots, sends = [], [], []
     for i in range(4):
         part = slice(8 * i, 8 * i + 8)
-        copies.append(pltpu.make_async_copy(x_ref.at[part], field.at[part], sems.at[i]))
+        fields.append(pltpu.make_async_copy(x_ref.at[part], field.at[part], sems.at[i]))
+        cots.append(
+            pltpu.make_async_copy(cot_ref.at[part, 0:EARLY, :], message.at[part, R // 2 :, :], sems.at[4 + i])
+        )
+        sends.append(pltpu.make_async_copy(message.at[part], out_ref.at[part], sems.at[8 + i]))
+    table.start()
     for i in range(4):
-        part = slice(8 * i, 8 * i + 8)
-        copies.append(pltpu.make_async_copy(cot_ref.at[part], out_ref.at[part, R // 2 :, :], sems.at[4 + i]))
-    for copy in copies:
-        copy.start()
-    copies[0].wait()
-    sends = []
+        fields[i].start()
+        cots[i].start()
+    table.wait()
     for i in range(4):
-        copies[1 + i].wait()
+        fields[i].wait()
         for t in range(4 * i, 4 * i + 4):
             y = dot(basis[...], field[2 * t : 2 * t + 2].reshape(128, WIN), NT)
             y = y[:R] + y[R:]
             first, second = halves(y[:16], y[16:])
-            coefs[2 * t] = first.astype(bf16)
-            coefs[2 * t + 1] = second.astype(bf16)
-        part = slice(8 * i, 8 * i + 8)
-        sends.append(pltpu.make_async_copy(coefs.at[part], out_ref.at[part, 0 : R // 2, :], sems.at[8 + i]))
+            message[2 * t, 0:16, :] = first.astype(bf16)
+            message[2 * t + 1, 0:16, :] = second.astype(bf16)
+        cots[i].wait()
         sends[i].start()
-    for copy in sends + copies[5:]:
-        copy.wait()
+    for i in range(4):
+        sends[i].wait()
 
 
 def modes_kernel(got_ref, g_ref, out_ref):
@@ -136,7 +139,10 @@
             out_ref[a * each + i] = send
 
 
-def mix_kernel(got_ref, weight_ref, out_ref, spec_ref, scr):
+def mix_kernel(got_ref, weight_ref, cot_ref, out_ref, spec_ref, scr):
+    late = cot_ref.shape[1] - EARLY
+    scr[...] = jnp.zeros(scr.shape, f32)
+    out_ref[:, 0:late, :] = cot_ref[:, EARLY:, :]
     for k in range(KEPT):
         rows = slice(k * Z, (k + 1) * Z)
         chan = got_ref.shape[0] // XH
@@ -153,13 +159,15 @@
         out = dot(spec, weight_ref[k], NT)
         real = out[:32, :64] - out[32:, 64:]
         imag = out[:32, 64:] + out[32:, :64]
-        scr[pl.ds(k, PITCH, stride=KEPT), :] = jnp.concatenate([real, imag], axis=1)
-    out_ref[...] = scr[...].astype(bf16)
-
-
-def pointwise_kernel(got_ref, cot_ref, bias_ref, table_ref, e_ref, out_ref, scr, send):
+        scr[pl.ds(k, PITCH, stride=8), :] = jnp.concatenate([real, imag], axis=1)
+    out_ref[:, late:, :] = scr[...].reshape(PITCH, 8, 128).astype(bf16)
+
+
+def pointwise_kernel(got_ref, early_ref, bias_ref, table_ref, e_ref, out_ref, scr, send):
     root = math.sqrt(2.0 / math.pi)
-    mixed = jnp.concatenate(by_mode(scr, got_ref[...].astype(f32), KEPT), axis=0)
+    late = got_ref.shape[1] - 8
+    modes = got_ref[:, late:, :].astype(f32).reshape(8 * PITCH, 128)
+    mixed = jnp.concatenate(by_mode(scr, modes, 8), axis=0)
     mixed = mixed.T
     mixed = jnp.concatenate([mixed[:64], mixed[64:]], axis=1).astype(bf16)
     bias = bias_ref[...]
@@ -182,7 +190,8 @@
                 square = v * v
                 th = jnp.tanh(root * (v + 0.044715 * (square * v)))
                 slope = 0.5 * (1.0 + th) + (0.5 * root) * v * (1.0 - th * th) * (1.0 + (3.0 * 0.044715) * square)
-                grad = slope * cot_ref[4 * g + i, R // 2 :, :].astype(f32)
+                cot = [early_ref[4 * g + i, R // 2 :, :], got_ref[4 * g + i, 0:late, :]]
+                grad = slope * jnp.concatenate(cot, axis=0).astype(f32)
                 total = total + grad
                 grads.append(grad.astype(bf16))
             blocks.append(jnp.concatenate(grads, axis=1))
@@ -293,14 +302,14 @@
 
     first = run(
         points_kernel,
-        shape((PITCH, R // 2 + width, 128), bf16),
+        shape((PITCH, R // 2 + EARLY, 128), bf16),
         const["points"],
         activation,
         cotangent,
         scratch=[
             pltpu.VMEM((2 * R, WIN), bf16),
             pltpu.VMEM(activation.shape, bf16),
-            pltpu.VMEM((PITCH, R // 2, 128), bf16),
+            pltpu.VMEM((PITCH, R // 2 + EARLY, 128), bf16),
             pltpu.SemaphoreType.DMA((13,)),
         ],
         far=3,
@@ -315,10 +324,11 @@
     spectra = exchange(spectra, ("xh", "chan"))
     mixed, spec = run(
         mix_kernel,
-        (small, shape((KEPT, 64, inputs), bf16)),
+        (shape((PITCH, width - EARLY + 8, 128), bf16), shape((KEPT, 64, inputs), bf16)),
         spectra,
         weight,
-        scratch=[square],
+        cotangent,
+        scratch=[tall],
         flops=mix_flops,
         name="mix",
     )
@@ -331,7 +341,7 @@
         bias_wide,
         const["doubled"],
         const["expand"],
-        scratch=[square, tall],
+        scratch=[tall, tall],
         name="pointwise",
     )
     grads = exchange(grads, PITCH_AXES)

time: 204 us -> 190 us (0.931)
  Pallas kernels: 24.8 us -> 10.6 us
    pallas_call x10, Pallas kernels: 24.8 us -> 10.6 us  [run(): pl.pallas_call(kernel, out_shape=out_shape, in_specs=near + [pl.BlockSpec...]
where the time goes in v5:
time: 190 us; the launch traced here: 189 us
  blocking collectives  157 us (83%)
  waiting for transfers between devices  15.6 us (8%)
  Pallas kernels  10.6 us (6%)
  starting transfers between devices  3.86 us (2%)
    all_to_all x7, blocking collectives, exchange(): return lax.all_to_all(blocks, axis, split_axis=0, concat_axis=0, tiled=True)  157 us
    all_to_all x1, waiting for transfers between devices, exchange(): return lax.all_to_all(blocks, axis, split_axis=0, concat_axis=0, tiled=True)  15.6 us
    pallas_call x10, Pallas kernels, run(): pl.pallas_call(kernel, out_shape=out_shape, in_specs=near + [pl.BlockSpec...  10.6 us
    all_to_all x1, starting transfers between devices, exchange(): return lax.all_to_all(blocks, axis, split_axis=0, concat_axis=0, tiled=True)  3.86 us
  transfers between devices with their start and end apart: 1, of which 1 were waited for; matrix products, arithmetic and copies ran while one was open for 0% of the time, Pallas kernels for 1%

profile of v5, /device:TPU:24, one launch (start us, length us, event | category | flops | bytes accessed | tf_op | source)
XLA Modules:
  0.0 188.8 jit_solution(4161857295926387869)
XLA Ops:
  0.6 0.0 copy-start.4
  0.6 2.9 %points.1 = bf16[32,48,128]{2,1,0:T(8,128)(2,1)} custom-call(bf16[64,128]{1,0:T(8,128)(2,1)} %constant.10.clone.v_ref, bf16[32,64,128]{2,1,0:T(8,128)(2,1)} %x_ref.1, bf16[32,64,128]{2,1,0:T(8,128)(2,1)} %cot_ref.5), custom_call_target="tpu_custom_call" | custom-call | bytes 1458176 | tf_op jit(solution)/shard_map/points/pallas_call | solution.py:71
  3.5 0.0 copy-start
  3.5 0.0 copy-start.1
  3.5 46.7 %all_to_all.64.got_ref.early_ref = bf16[32,48,128]{2,1,0:T(8,128)(2,1)S(1)} all-to-all(bf16[32,48,128]{2,1,0:T(8,128)(2,1)} %points.1), channel_id=1, replica_groups=mesh['xh'=2,'z'=16,'chan'=16] {'xh','z'}, dimensions={0} | all-to-all | bytes 786432 | tf_op jit(solution)/shard_map/all_to_all | solution.py:285
  50.3 0.0 copy-done.4
  50.3 0.6 modes.1
  50.8 15.8 %all_to_all.65 = bf16[16,8,128]{2,1,0:T(8,128)(2,1)S(1)} all-to-all(bf16[16,8,128]{2,1,0:T(8,128)(2,1)S(1)} %bitcast.18), channel_id=1, replica_groups=mesh['xh'=2,'z'=16,'chan'=16] {'z'}, dimensions={0} | all-to-all | bytes 65536 | tf_op jit(solution)/shard_map/all_to_all | solution.py:285
  66.6 0.0 copy-start.7
  66.6 0.0 copy-start.3
  66.6 0.0 copy-start.5
  66.6 0.1 gather.1
  66.7 14.5 %all_to_all.66.got_ref = bf16[32,64,128]{2,1,0:T(8,128)(2,1)S(1)} all-to-all(bf16[32,64,128]{2,1,0:T(8,128)(2,1)S(1)} %gather.1), channel_id=1, replica_groups=mesh['xh'=2,'z'=16,'chan'=16] {'xh','chan'}, dimensions={0} | all-to-all | bytes 1048576 | tf_op jit(solution)/shard_map/all_to_all | solution.py:285
  81.2 0.0 copy-done
  81.2 0.0 copy-done.1
  81.2 0.6 mix.1
  81.8 29.8 %all_to_all.67.got_ref = bf16[32,40,128]{2,1,0:T(8,128)(2,1)S(1)} all-to-all(bf16[32,40,128]{2,1,0:T(8,128)(2,1)S(1)} %get-tuple-element.8), channel_id=1, replica_groups=mesh['xh'=2,'z'=16,'chan'=16] {'xh','z'}, dimensions={0} | all-to-all | bytes 655360 | tf_op jit(solution)/shard_map/all_to_all | solution.py:285
  111.6 0.0 copy-done.7
  111.6 0.1 broadcast_in_dim.2.bias_ref
  111.7 0.0 copy-done.3
  111.7 0.0 copy-done.5
  111.7 0.0 copy-start.2
  111.7 1.8 pointwise.1
  113.5 19.4 %all_to_all.68 = bf16[32,8,128]{2,1,0:T(8,128)(2,1)S(1)} all-to-all(bf16[32,8,128]{2,1,0:T(8,128)(2,1)S(1)} %bitcast.15), channel_id=1, replica_groups=mesh['xh'=2,'z'=16,'chan'=16] {'xh','z'}, dimensions={0} | all-to-all | bytes 131072 | tf_op jit(solution)/shard_map/all_to_all | solution.py:285
  132.9 0.6 back.1
  133.5 13.0 %all_to_all.69.got_ref = bf16[16,128,128]{2,1,0:T(8,128)(2,1)S(1)} all-to-all(bf16[16,128,128]{2,1,0:T(8,128)(2,1)S(1)} %get-tuple-element.9), channel_id=1, replica_groups=mesh['xh'=2,'z'=16,'chan'=16] {'chan'}, dimensions={0} | all-to-all | bytes 1048576 | tf_op jit(solution)/shard_map/all_to_all | solution.py:285
  146.5 0.1 collect.1
  146.6 18.2 %all_to_all.70 = bf16[32,4,128]{2,1,0:T(4,128)(2,1)S(1)} all-to-all(bf16[32,4,128]{2,1,0:T(4,128)(2,1)S(1)} %bitcast.20), channel_id=1, replica_groups=mesh['xh'=2,'z'=16,'chan'=16] {'xh','z'}, dimensions={0} | all-to-all | bytes 65536 | tf_op jit(solution)/shard_map/all_to_all | solution.py:285
  164.7 0.0 copy-start.6
  164.7 0.0 copy-done.2
  164.7 1.2 windows.1
  165.9 3.9 %all-to-all-start.7 = ((bf16[32,16,128]{2,1,0:T(8,128)(2,1)}), bf16[32,16,128]{2,1,0:T(8,128)(2,1)S(1)}, u32[]{:S(2)}, u32[]{:S(2)}) async-start(bf16[32,16,128]{2,1,0:T(8,128)(2,1)} %bitcast.7), calls=%async_computation.7 | async-start | bytes 262144 | tf_op jit(solution)/shard_map/all_to_all | solution.py:285
  169.8 1.8 weight.1
  171.5 0.5 slice_bitcast_fusion
  172.0 15.6 %all-to-all-done.7 = bf16[32,16,128]{2,1,0:T(8,128)(2,1)S(1)} async-done(((bf16[32,16,128]{2,1,0:T(8,128)(2,1)}), bf16[32,16,128]{2,1,0:T(8,128)(2,1)S(1)}, u32[]{:S(2)}, u32[]{:S(2)}) %all-to-all-start.7) | async-done | bytes 131104 | tf_op jit(solution)/shard_map/all_to_all | solution.py:285
  187.6 0.0 copy-done.6
  187.6 1.2 finish.1
Async XLA Ops:
  0.6 49.6 %copy-start.4 = (bf16[1024,512]{1,0:T(8,128)(2,1)S(1)}, bf16[1024,512]{1,0:T(8,128)(2,1)}, u32[]{:S(2)}) copy-start(bf16[1024,512]{1,0:T(8,128)(2,1)} %constant.11.clone.g_ref) | copy-start | bytes 3145732
  3.5 77.7 %copy-start = (bf16[32,64,128]{2,1,0:T(8,128)(2,1)S(1)}, bf16[32,64,128]{2,1,0:T(8,128)(2,1)}, u32[]{:S(2)}) copy-start(bf16[32,64,128]{2,1,0:T(8,128)(2,1)} %cot_ref.5) | copy-start | bytes 1572868
  3.5 77.7 %copy-start.1 = (bf16[4,2,64,1024]{3,2,1,0:T(8,128)(2,1)S(1)}, bf16[4,2,64,1024]{3,2,1,0:T(8,128)(2,1)}, u32[]{:S(2)}) copy-start(bf16[4,2,64,1024]{3,2,1,0:T(8,128)(2,1)} %param.11) | copy-start | bytes 3145732
  66.6 45.0 %copy-start.7 = (f32[64]{0:T(128)S(1)}, f32[64]{0:T(128)}, u32[]{:S(2)}) copy-start(f32[64]{0:T(128)} %param.12) | copy-start | bytes 772
  66.6 45.1 %copy-start.3 = (bf16[2,256,1024]{2,1,0:T(8,128)(2,1)S(1)}, bf16[2,256,1024]{2,1,0:T(8,128)(2,1)}, u32[]{:S(2)}) copy-start(bf16[2,256,1024]{2,1,0:T(8,128)(2,1)} %constant.13.clone.table_ref) | copy-start | bytes 3145732
  66.6 45.1 %copy-start.5 = (bf16[384,512]{1,0:T(8,128)(2,1)S(1)}, bf16[384,512]{1,0:T(8,128)(2,1)}, u32[]{:S(2)}) copy-start(bf16[384,512]{1,0:T(8,128)(2,1)} %constant.14.clone.e_ref) | copy-start | bytes 1179652
  111.7 53.0 %copy-start.2 = (bf16[1024,512]{1,0:T(8,128)(2,1)S(1)}, bf16[1024,512]{1,0:T(8,128)(2,1)}, u32[]{:S(2)}) copy-start(bf16[1024,512]{1,0:T(8,128)(2,1)} %constant.12.clone.u_ref) | copy-start | bytes 3145732
  164.7 22.9 %copy-start.6 = (bf16[64,128]{1,0:T(8,128)(2,1)S(1)}, bf16[64,128]{1,0:T(8,128)(2,1)}, u32[]{:S(2)}) copy-start(bf16[64,128]{1,0:T(8,128)(2,1)} %constant.10.clone.v_ref) | copy-start | bytes 49156
  165.9 21.7 %all-to-all-start.7 = ((bf16[32,16,128]{2,1,0:T(8,128)(2,1)}), bf16[32,16,128]{2,1,0:T(8,128)(2,1)S(1)}, u32[]{:S(2)}, u32[]{:S(2)}) async-start(bf16[32,16,128]{2,1,0:T(8,128)(2,1)} %bitcast.7), calls=%async_computation.7 | async-start | bytes 262144 | tf_op jit(solution)/shard_map/all_to_all | solution.py:285

commit v6 on v4

--- a/solution.py
+++ b/solution.py
@@ -46,8 +46,7 @@
     out = {}
     hi, lo = split_hi_lo(basis)
     out["points"] = np.concatenate([hi, lo], axis=0)
-    by_z = coef.reshape(2, XH, Z, KEPT, PITCH, 2, R // 2).transpose(5, 0, 2, 1, 3, 4, 6)
-    gather = by_z.reshape(2, 2 * M, PITCH * R // 2)
+    gather = coef.transpose(2, 0, 1, 3).reshape(2, 2 * M, PITCH * R // 2)
     out["modes"] = np.stack(split_hi_lo(gather), axis=1).reshape(8 * M, PITCH * R // 2)
     spread = coef.transpose(1, 3, 2, 0).reshape(PITCH * R // 2, 4 * M)
     out["windows"] = np.concatenate(split_hi_lo(spread), axis=0)
@@ -86,36 +85,25 @@
     )
 
 
-def points_kernel(v_ref, x_ref, cot_ref, out_ref, basis, field, coefs, sems):
-    copies = [pltpu.make_async_copy(v_ref, basis, sems.at[12])]
-    for i in range(4):
-        part = slice(8 * i, 8 * i + 8)
-        copies.append(pltpu.make_async_copy(x_ref.at[part], field.at[part], sems.at[i]))
-    for i in range(4):
-        part = slice(8 * i, 8 * i + 8)
-        copies.append(pltpu.make_async_copy(cot_ref.at[part], out_ref.at[part, R // 2 :, :], sems.at[4 + i]))
+def points_kernel(v_ref, x_ref, out_ref, basis, field, sems):
+    table = pltpu.make_async_copy(v_ref, basis, sems.at[4])
+    parts = [slice(8 * i, 8 * i + 8) for i in range(4)]
+    copies = [pltpu.make_async_copy(x_ref.at[part], field.at[part], sems.at[i]) for i, part in enumerate(parts)]
+    table.start()
     for copy in copies:
         copy.start()
-    copies[0].wait()
-    sends = []
-    for i in range(4):
-        copies[1 + i].wait()
-        for t in range(4 * i, 4 * i + 4):
-            y = dot(basis[...], field[2 * t : 2 * t + 2].reshape(128, WIN), NT)
-            y = y[:R] + y[R:]
-            first, second = halves(y[:16], y[16:])
-            coefs[2 * t] = first.astype(bf16)
-            coefs[2 * t + 1] = second.astype(bf16)
-        part = slice(8 * i, 8 * i + 8)
-        sends.append(pltpu.make_async_copy(coefs.at[part], out_ref.at[part, 0 : R // 2, :], sems.at[8 + i]))
-        sends[i].start()
-    for copy in sends + copies[5:]:
-        copy.wait()
+    table.wait()
+    for t in range(16):
+        if t % 4 == 0:
+            copies[t // 4].wait()
+        y = dot(basis[...], field[2 * t : 2 * t + 2].reshape(128, WIN), NT)
+        y = y[:R] + y[R:]
+        first, second = halves(y[:16], y[16:])
+        out_ref[t * 32 : (t + 1) * 32, :] = jnp.concatenate([first, second], axis=0).astype(bf16)
 
 
 def modes_kernel(got_ref, g_ref, out_ref):
-    got = got_ref[:, 0 : R // 2, :].reshape(PITCH * R // 2, 128)
-    part = dot(g_ref[...], got, NN)
+    part = dot(g_ref[...], got_ref[...], NN)
     part = part[: 4 * M, :64] + part[4 * M :, 64:]
     part = part[: 2 * M] + part[2 * M :]
     out_ref[...] = jnp.concatenate([part[:M], part[M:]], axis=1).astype(bf16)
@@ -127,25 +115,15 @@
 
 
 def gather_kernel(got_ref, out_ref, scr):
-    scr[...] = got_ref[...].astype(f32)
-    each = out_ref.shape[0] // XH
-    for a in range(XH):
-        rows = [scr[pl.ds(a * KEPT + k, Z, stride=XH * KEPT), :] for k in range(KEPT)]
-        send = jnp.concatenate(rows, axis=0).astype(bf16)
-        for i in range(each):
-            out_ref[a * each + i] = send
-
-
-def mix_kernel(got_ref, weight_ref, out_ref, spec_ref, scr):
-    for k in range(KEPT):
-        rows = slice(k * Z, (k + 1) * Z)
-        chan = got_ref.shape[0] // XH
+    out_ref[...] = jnp.concatenate(by_mode(scr, got_ref[...].astype(f32), KEPT), axis=0).astype(bf16)
+
+
+def mix_kernel(got_ref, weight_ref, moved_ref, out_ref, spec_ref, scr):
+    for k in range(KEPT):
+        rows = slice(k * PITCH, (k + 1) * PITCH)
         re, im = [], []
-        for q in range(chan // 2):
-            left, right = [
-                jnp.concatenate([got_ref[c, rows, :], got_ref[chan + c, rows, :]], axis=0) for c in (2 * q, 2 * q + 1)
-            ]
-            first, second = halves(left, right)
+        for q in range(got_ref.shape[0] // 2):
+            first, second = halves(got_ref[2 * q, rows, :], got_ref[2 * q + 1, rows, :])
             re.append(first)
             im.append(second)
         spec = jnp.concatenate([jnp.concatenate(re, axis=1), jnp.concatenate(im, axis=1)], axis=0)
@@ -182,7 +160,7 @@
                 square = v * v
                 th = jnp.tanh(root * (v + 0.044715 * (square * v)))
                 slope = 0.5 * (1.0 + th) + (0.5 * root) * v * (1.0 - th * th) * (1.0 + (3.0 * 0.044715) * square)
-                grad = slope * cot_ref[4 * g + i, R // 2 :, :].astype(f32)
+                grad = slope * cot_ref[4 * g + i].astype(f32)
                 total = total + grad
                 grads.append(grad.astype(bf16))
             blocks.append(jnp.concatenate(grads, axis=1))
@@ -291,34 +269,31 @@
     across = shape((chan, M, 128), bf16)
     mix_flops = 2 * KEPT * 64 * 128 * inputs
 
-    first = run(
+    coefs = run(
         points_kernel,
-        shape((PITCH, R // 2 + width, 128), bf16),
+        coefs_shape,
         const["points"],
         activation,
-        cotangent,
-        scratch=[
-            pltpu.VMEM((2 * R, WIN), bf16),
-            pltpu.VMEM(activation.shape, bf16),
-            pltpu.VMEM((PITCH, R // 2, 128), bf16),
-            pltpu.SemaphoreType.DMA((13,)),
-        ],
-        far=3,
-        far_out=True,
+        scratch=[pltpu.VMEM((2 * R, WIN), bf16), pltpu.VMEM(activation.shape, bf16), pltpu.SemaphoreType.DMA((5,))],
+        far=2,
         vmem=FIRST_LIMIT,
         name="points",
     )
-    first = exchange(first, PITCH_AXES)
-    spectra = run(modes_kernel, small, first, const["modes"], name="modes")
-    spectra = exchange(spectra, "z")
-    spectra = run(gather_kernel, shape((XH * chan, M // XH, 128), bf16), spectra, scratch=[square], name="gather")
-    spectra = exchange(spectra, ("xh", "chan"))
+    coefs = exchange(coefs, PITCH_AXES)
+    spectra = run(modes_kernel, small, coefs, const["modes"], name="modes")
+    spectra = exchange(spectra, PITCH_AXES)
+    spectra, moving = lax.optimization_barrier((spectra, cotangent))
+    moving = exchange(moving, PITCH_AXES)
+    spectra = run(gather_kernel, small, spectra, scratch=[square], name="gather")
+    spectra = lax.all_gather(spectra, "chan", axis=0, tiled=False)
     mixed, spec = run(
         mix_kernel,
         (small, shape((KEPT, 64, inputs), bf16)),
         spectra,
         weight,
+        moving,
         scratch=[square],
+        far=1,
         flops=mix_flops,
         name="mix",
     )
@@ -327,7 +302,7 @@
         pointwise_kernel,
         shape((2 * M, 128), bf16),
         mixed,
-        first,
+        moving,
         bias_wide,
         const["doubled"],
         const["expand"],

time: 204 us -> 195 us (0.956)
  blocking collectives: 157 us -> 141 us
  waiting for transfers between devices: 15.6 us -> 30.1 us
  Pallas kernels: 24.8 us -> 11.5 us
  starting transfers between devices: 3.86 us -> 7.74 us
    all_to_all x7 -> x6, blocking collectives: 157 us -> 125 us  [exchange(): return lax.all_to_all(blocks, axis, split_axis=0, concat_axis=0, tiled=True)]
    all_gather x0 -> x1, blocking collectives: none -> 16.9 us  [body(): spectra = lax.all_gather(spectra, 'chan', axis=0, tiled=False)]
    all_to_all x1 -> x2, waiting for transfers between devices: 15.6 us -> 30.1 us  [exchange(): return lax.all_to_all(blocks, axis, split_axis=0, concat_axis=0, tiled=True)]
    pallas_call x10, Pallas kernels: 24.8 us -> 11.5 us  [run(): pl.pallas_call(kernel, out_shape=out_shape, in_specs=near + [pl.BlockSpec...]
    all_to_all x1 -> x2, starting transfers between devices: 3.86 us -> 7.74 us  [exchange(): return lax.all_to_all(blocks, axis, split_axis=0, concat_axis=0, tiled=True)]
  transfers between devices with their start and end apart: 1 -> 2, of which waited for: 1 -> 2; matrix products, arithmetic and copies ran while one was open for 0% -> 0% of each run, Pallas kernels for 1% -> 1%
where the time goes in v6:
time: 195 us; the launch traced here: 193 us
  blocking collectives  141 us (72%)
  waiting for transfers between devices  30.1 us (15%)
  Pallas kernels  11.5 us (6%)
  starting transfers between devices  7.74 us (4%)
    all_to_all x6, blocking collectives, exchange(): return lax.all_to_all(blocks, axis, split_axis=0, concat_axis=0, tiled=True)  125 us
    all_to_all x2, waiting for transfers between devices, exchange(): return lax.all_to_all(blocks, axis, split_axis=0, concat_axis=0, tiled=True)  30.1 us
    all_gather x1, blocking collectives, body(): spectra = lax.all_gather(spectra, 'chan', axis=0, tiled=False)  16.9 us
    pallas_call x10, Pallas kernels, run(): pl.pallas_call(kernel, out_shape=out_shape, in_specs=near + [pl.BlockSpec...  11.5 us
    all_to_all x2, starting transfers between devices, exchange(): return lax.all_to_all(blocks, axis, split_axis=0, concat_axis=0, tiled=True)  7.74 us
  transfers between devices with their start and end apart: 2, of which 2 were waited for; matrix products, arithmetic and copies ran while one was open for 0% of the time, Pallas kernels for 1%

profile of v6, /device:TPU:24, one launch (start us, length us, event | category | flops | bytes accessed | tf_op | source)
XLA Modules:
  0.0 193.4 jit_solution(16640444936041614787)
XLA Ops:
  0.6 0.0 copy-start
  0.6 2.8 %points.1 = bf16[512,128]{1,0:T(8,128)(2,1)} custom-call(bf16[64,128]{1,0:T(8,128)(2,1)} %constant.10.clone.v_ref, bf16[32,64,128]{2,1,0:T(8,128)(2,1)} %x_ref.1), custom_call_target="tpu_custom_call" | custom-call | bytes 671744 | tf_op jit(solution)/shard_map/points/pallas_call | solution.py:69
  3.4 36.3 %all_to_all.77 = bf16[32,16,128]{2,1,0:T(8,128)(2,1)S(1)} all-to-all(bf16[32,16,128]{2,1,0:T(8,128)(2,1)} %bitcast.31), channel_id=1, replica_groups=mesh['xh'=2,'z'=16,'chan'=16] {'xh','z'}, dimensions={0} | all-to-all | bytes 262144 | tf_op jit(solution)/shard_map/all_to_all | solution.py:254
  39.7 0.0 copy-start.2
  39.7 1.2 copy-done.2
  41.0 0.6 modes.1
  41.5 0.0 copy-start.8
  41.5 0.0 copy-start.3
  41.6 0.0 copy-start.6
  41.6 18.2 %all_to_all.78 = bf16[32,4,128]{2,1,0:T(4,128)(2,1)S(1)} all-to-all(bf16[32,4,128]{2,1,0:T(4,128)(2,1)S(1)} %bitcast.25), channel_id=1, replica_groups=mesh['xh'=2,'z'=16,'chan'=16] {'xh','z'}, dimensions={0} | all-to-all | bytes 65536 | tf_op jit(solution)/shard_map/all_to_all | solution.py:254
  59.8 3.9 %all-to-all-start.2 = ((bf16[32,64,128]{2,1,0:T(8,128)(2,1)}), bf16[32,64,128]{2,1,0:T(8,128)(2,1)S(1)}, u32[]{:S(2)}, u32[]{:S(2)}) async-start(bf16[32,64,128]{2,1,0:T(8,128)(2,1)} %cot_ref.1), calls=%async_computation.2 | async-start | bytes 1048576 | tf_op jit(solution)/shard_map/all_to_all | solution.py:254
  63.7 16.9 %all-gather = bf16[2048,128]{1,0:T(8,128)(2,1)S(1)} all-gather(bf16[128,128]{1,0:T(8,128)(2,1)S(1)} %gather.1), channel_id=2, replica_groups=mesh['xh'=2,'z'=16,'chan'=16] {'chan'}, dimensions={0}, use_global_device_ids=true | all-gather | bytes 557056 | tf_op jit(solution)/shard_map/all_gather | solution.py:288
  80.6 14.5 %all-to-all-done.2.moved_ref.cot_ref = bf16[32,64,128]{2,1,0:T(8,128)(2,1)S(1)} async-done(((bf16[32,64,128]{2,1,0:T(8,128)(2,1)}), bf16[32,64,128]{2,1,0:T(8,128)(2,1)S(1)}, u32[]{:S(2)}, u32[]{:S(2)}) %all-to-all-start.2) | async-done | bytes 524320 | tf_op jit(solution)/shard_map/all_to_all | solution.py:254
  95.1 0.0 copy-done
  95.1 0.6 mix.1
  95.7 0.0 copy-start.4
  95.7 19.7 %all_to_all.79 = bf16[32,4,128]{2,1,0:T(4,128)(2,1)S(1)} all-to-all(bf16[32,4,128]{2,1,0:T(4,128)(2,1)S(1)} %bitcast.29), channel_id=1, replica_groups=mesh['xh'=2,'z'=16,'chan'=16] {'xh','z'}, dimensions={0} | all-to-all | bytes 65536 | tf_op jit(solution)/shard_map/all_to_all | solution.py:254
  115.4 0.0 copy-done.8
  115.4 0.1 broadcast_in_dim.2.bias_ref
  115.5 0.0 copy-done.3
  115.5 0.0 copy-done.6
  115.5 0.0 copy-start.1
  115.5 1.8 pointwise.1
  117.3 18.8 %all_to_all.80 = bf16[32,8,128]{2,1,0:T(8,128)(2,1)S(1)} all-to-all(bf16[32,8,128]{2,1,0:T(8,128)(2,1)S(1)} %bitcast.22), channel_id=1, replica_groups=mesh['xh'=2,'z'=16,'chan'=16] {'xh','z'}, dimensions={0} | all-to-all | bytes 131072 | tf_op jit(solution)/shard_map/all_to_all | solution.py:254
  136.1 0.6 back.1
  136.7 0.0 copy-done.4
  136.7 0.0 copy-start.5
  136.7 13.4 %all_to_all.81.got_ref = bf16[16,128,128]{2,1,0:T(8,128)(2,1)S(1)} all-to-all(bf16[16,128,128]{2,1,0:T(8,128)(2,1)S(1)} %get-tuple-element.13), channel_id=1, replica_groups=mesh['xh'=2,'z'=16,'chan'=16] {'chan'}, dimensions={0} | all-to-all | bytes 1048576 | tf_op jit(solution)/shard_map/all_to_all | solution.py:254
  150.1 0.1 collect.1
  150.1 18.2 %all_to_all.82 = bf16[32,4,128]{2,1,0:T(4,128)(2,1)S(1)} all-to-all(bf16[32,4,128]{2,1,0:T(4,128)(2,1)S(1)} %bitcast.27), channel_id=1, replica_groups=mesh['xh'=2,'z'=16,'chan'=16] {'xh','z'}, dimensions={0} | all-to-all | bytes 65536 | tf_op jit(solution)/shard_map/all_to_all | solution.py:254
  168.3 0.0 copy-start.7
  168.3 0.0 copy-done.1
  168.3 1.1 windows.1
  169.5 3.9 %all-to-all-start.7 = ((bf16[32,16,128]{2,1,0:T(8,128)(2,1)}), bf16[32,16,128]{2,1,0:T(8,128)(2,1)S(1)}, u32[]{:S(2)}, u32[]{:S(2)}) async-start(bf16[32,16,128]{2,1,0:T(8,128)(2,1)} %bitcast.12), calls=%async_computation.7 | async-start | bytes 262144 | tf_op jit(solution)/shard_map/all_to_all | solution.py:254
  173.3 0.0 copy-done.5
  173.3 1.8 weight.1
  175.1 0.5 slice_bitcast_fusion
  175.6 15.6 %all-to-all-done.7 = bf16[32,16,128]{2,1,0:T(8,128)(2,1)S(1)} async-done(((bf16[32,16,128]{2,1,0:T(8,128)(2,1)}), bf16[32,16,128]{2,1,0:T(8,128)(2,1)S(1)}, u32[]{:S(2)}, u32[]{:S(2)}) %all-to-all-start.7) | async-done | bytes 131104 | tf_op jit(solution)/shard_map/all_to_all | solution.py:254
  191.2 0.0 copy-done.7
  191.2 2.2 %finish.1 = bf16[32,64,128]{2,1,0:T(8,128)(2,1)} custom-call(bf16[512,128]{1,0:T(8,128)(2,1)S(1)} %bitcast.20, bf16[32,64,128]{2,1,0:T(8,128)(2,1)} %cot_ref.1, bf16[64,128]{1,0:T(8,128)(2,1)S(1)} %copy-done.7), custom_call_target="tpu_custom_call" | custom-call | bytes 1196032 | tf_op jit(solution)/shard_map/finish/pallas_call | solution.py:69
  (1 shorter events, 0.0 us)
Async XLA Ops:
  0.6 94.5 %copy-start = (bf16[4,2,64,1024]{3,2,1,0:T(8,128)(2,1)S(1)}, bf16[4,2,64,1024]{3,2,1,0:T(8,128)(2,1)}, u32[]{:S(2)}) copy-start(bf16[4,2,64,1024]{3,2,1,0:T(8,128)(2,1)} %param.11) | copy-start | bytes 3145732
  39.7 1.2 copy-start.2
  41.5 73.9 %copy-start.8 = (f32[64]{0:T(128)S(1)}, f32[64]{0:T(128)}, u32[]{:S(2)}) copy-start(f32[64]{0:T(128)} %param.12) | copy-start | bytes 772
  41.5 74.0 %copy-start.3 = (bf16[2,256,1024]{2,1,0:T(8,128)(2,1)S(1)}, bf16[2,256,1024]{2,1,0:T(8,128)(2,1)}, u32[]{:S(2)}) copy-start(bf16[2,256,1024]{2,1,0:T(8,128)(2,1)} %constant.13.clone.table_ref) | copy-start | bytes 3145732
  41.6 74.0 %copy-start.6 = (bf16[384,512]{1,0:T(8,128)(2,1)S(1)}, bf16[384,512]{1,0:T(8,128)(2,1)}, u32[]{:S(2)}) copy-start(bf16[384,512]{1,0:T(8,128)(2,1)} %constant.14.clone.e_ref) | copy-start | bytes 1179652
  59.8 35.3 %all-to-all-start.2 = ((bf16[32,64,128]{2,1,0:T(8,128)(2,1)}), bf16[32,64,128]{2,1,0:T(8,128)(2,1)S(1)}, u32[]{:S(2)}, u32[]{:S(2)}) async-start(bf16[32,64,128]{2,1,0:T(8,128)(2,1)} %cot_ref.1), calls=%async_computation.2 | async-start | bytes 1048576 | tf_op jit(solution)/shard_map/all_to_all | solution.py:254
  95.7 41.0 %copy-start.4 = (bf16[4,64,1024]{2,1,0:T(8,128)(2,1)}, bf16[4,64,1024]{2,1,0:T(8,128)(2,1)S(1)}, u32[]{:S(2)}) copy-start(bf16[4,64,1024]{2,1,0:T(8,128)(2,1)S(1)} %get-tuple-element.15.spec_ref) | copy-start | bytes 1572868
  115.5 52.8 %copy-start.1 = (bf16[1024,512]{1,0:T(8,128)(2,1)S(1)}, bf16[1024,512]{1,0:T(8,128)(2,1)}, u32[]{:S(2)}) copy-start(bf16[1024,512]{1,0:T(8,128)(2,1)} %constant.12.clone.u_ref) | copy-start | bytes 3145732
  136.7 36.6 %copy-start.5 = (bf16[4,64,1024]{2,1,0:T(8,128)(2,1)S(1)}, bf16[4,64,1024]{2,1,0:T(8,128)(2,1)}, u32[]{:S(2)}) copy-start(bf16[4,64,1024]{2,1,0:T(8,128)(2,1)} %copy-done.4) | copy-start | bytes 1572868
  168.3 22.9 %copy-start.7 = (bf16[64,128]{1,0:T(8,128)(2,1)S(1)}, bf16[64,128]{1,0:T(8,128)(2,1)}, u32[]{:S(2)}) copy-start(bf16[64,128]{1,0:T(8,128)(2,1)} %constant.10.clone.v_ref) | copy-start | bytes 49156
  169.5 21.7 %all-to-all-start.7 = ((bf16[32,16,128]{2,1,0:T(8,128)(2,1)}), bf16[32,16,128]{2,1,0:T(8,128)(2,1)S(1)}, u32[]{:S(2)}, u32[]{:S(2)}) async-start(bf16[32,16,128]{2,1,0:T(8,128)(2,1)} %bitcast.12), calls=%async_computation.7 | async-start | bytes 262144 | tf_op jit(solution)/shard_map/all_to_all | solution.py:254

commit v7 on v5

--- a/solution.py
+++ b/solution.py
@@ -18,7 +18,7 @@
 PITCH = XH * Z
 WIN = P_SIZE // PITCH
 KEPT = M // PITCH
-EARLY = 32
+BOTH = XH * KEPT
 R = 32
 PITCH_AXES = ("xh", "z")
 f32 = jnp.float32
@@ -50,11 +50,13 @@
     by_z = coef.reshape(2, XH, Z, KEPT, PITCH, 2, R // 2).transpose(5, 0, 2, 1, 3, 4, 6)
     gather = by_z.reshape(2, 2 * M, PITCH * R // 2)
     out["modes"] = np.stack(split_hi_lo(gather), axis=1).reshape(8 * M, PITCH * R // 2)
-    spread = coef.transpose(1, 3, 2, 0).reshape(PITCH * R // 2, 4 * M)
+    spread = by_z.transpose(5, 6, 0, 1, 2, 3, 4)
+    spread = spread.reshape(PITCH * R // 2, 4 * M)
     out["windows"] = np.concatenate(split_hi_lo(spread), axis=0)
-    scale = np.where(modes == 0, 1.0, 2.0).reshape(1, PITCH, KEPT, 1)
-    scaled = coef.reshape(2, PITCH, KEPT, PITCH * R) * scale
-    out["doubled"] = np.stack(split_hi_lo(scaled.transpose(0, 2, 1, 3).reshape(2 * M, PITCH * R)))
+    scale = np.where(modes == 0, 1.0, 2.0).reshape(1, XH, Z, KEPT, 1)
+    scaled = coef.reshape(2, XH, Z, KEPT, PITCH * R) * scale
+    scaled = scaled.transpose(0, 1, 3, 2, 4).reshape(2 * M, PITCH * R)
+    out["doubled"] = np.stack(split_hi_lo(scaled))
     high, low = split_hi_lo(np.kron(np.eye(4), basis))
     out["expand"] = np.concatenate([high, high, low], axis=0)
     return out
@@ -64,9 +66,10 @@
     return lax.dot_general(left, right, dims, preferred_element_type=f32)
 
 
-def run(kernel, out_shape, *args, scratch=(), flops=0, name=None, far=0, far_out=False, vmem=VMEM_LIMIT):
+def run(kernel, out_shape, *args, scratch=(), flops=0, name=None, far=0, far_out=False, vmem=VMEM_LIMIT, scalars=0):
     out_space = pltpu.HBM if far_out else pltpu.VMEM
-    near = [pl.BlockSpec(memory_space=pltpu.VMEM)] * (len(args) - far)
+    near = [pl.BlockSpec(memory_space=pltpu.SMEM)] * scalars
+    near += [pl.BlockSpec(memory_space=pltpu.VMEM)] * (len(args) - far - scalars)
     touched = sum(int(np.prod(a.shape)) * a.dtype.itemsize for a in list(args) + jax.tree.leaves(out_shape))
     return pl.pallas_call(
         kernel,
@@ -94,7 +97,7 @@
         part = slice(8 * i, 8 * i + 8)
         fields.append(pltpu.make_async_copy(x_ref.at[part], field.at[part], sems.at[i]))
         cots.append(
-            pltpu.make_async_copy(cot_ref.at[part, 0:EARLY, :], message.at[part, R // 2 :, :], sems.at[4 + i])
+            pltpu.make_async_copy(cot_ref.at[part], message.at[part, R // 2 :, :], sems.at[4 + i])
         )
         sends.append(pltpu.make_async_copy(message.at[part], out_ref.at[part], sems.at[8 + i]))
     table.start()
@@ -126,48 +129,35 @@
 
 def by_mode(scr, value, count):
     scr[...] = value
-    return [scr[pl.ds(k, PITCH, stride=count), :] for k in range(KEPT)]
+    return [scr[pl.ds(k, Z, stride=count), :] for k in range(BOTH)]
 
 
 def gather_kernel(got_ref, out_ref, scr):
-    scr[...] = got_ref[...].astype(f32)
-    each = out_ref.shape[0] // XH
-    for a in range(XH):
-        rows = [scr[pl.ds(a * KEPT + k, Z, stride=XH * KEPT), :] for k in range(KEPT)]
-        send = jnp.concatenate(rows, axis=0).astype(bf16)
-        for i in range(each):
-            out_ref[a * each + i] = send
-
-
-def mix_kernel(got_ref, weight_ref, cot_ref, out_ref, spec_ref, scr):
-    late = cot_ref.shape[1] - EARLY
-    scr[...] = jnp.zeros(scr.shape, f32)
-    out_ref[:, 0:late, :] = cot_ref[:, EARLY:, :]
-    for k in range(KEPT):
+    send = jnp.concatenate(by_mode(scr, got_ref[...].astype(f32), BOTH), axis=0).astype(bf16)
+    for i in range(out_ref.shape[0]):
+        out_ref[i] = send
+
+
+def mix_kernel(got_ref, weight_ref, out_ref, spec_ref, scr):
+    for k in range(BOTH):
         rows = slice(k * Z, (k + 1) * Z)
-        chan = got_ref.shape[0] // XH
         re, im = [], []
-        for q in range(chan // 2):
-            left, right = [
-                jnp.concatenate([got_ref[c, rows, :], got_ref[chan + c, rows, :]], axis=0) for c in (2 * q, 2 * q + 1)
-            ]
-            first, second = halves(left, right)
+        for q in range(got_ref.shape[0] // 2):
+            first, second = halves(got_ref[2 * q, rows, :], got_ref[2 * q + 1, rows, :])
             re.append(first)
             im.append(second)
         spec = jnp.concatenate([jnp.concatenate(re, axis=1), jnp.concatenate(im, axis=1)], axis=0)
         spec_ref[k] = spec
         out = dot(spec, weight_ref[k], NT)
-        real = out[:32, :64] - out[32:, 64:]
-        imag = out[:32, 64:] + out[32:, :64]
-        scr[pl.ds(k, PITCH, stride=8), :] = jnp.concatenate([real, imag], axis=1)
-    out_ref[:, late:, :] = scr[...].reshape(PITCH, 8, 128).astype(bf16)
-
-
-def pointwise_kernel(got_ref, early_ref, bias_ref, table_ref, e_ref, out_ref, scr, send):
+        real = out[:Z, :64] - out[Z:, 64:]
+        imag = out[:Z, 64:] + out[Z:, :64]
+        scr[pl.ds(k, Z, stride=BOTH), :] = jnp.concatenate([real, imag], axis=1)
+    out_ref[...] = scr[...].astype(bf16)
+
+
+def pointwise_kernel(got_ref, cot_ref, bias_ref, table_ref, e_ref, out_ref, scr, send):
     root = math.sqrt(2.0 / math.pi)
-    late = got_ref.shape[1] - 8
-    modes = got_ref[:, late:, :].astype(f32).reshape(8 * PITCH, 128)
-    mixed = jnp.concatenate(by_mode(scr, modes, 8), axis=0)
+    mixed = jnp.concatenate(by_mode(scr, got_ref[...].astype(f32), BOTH), axis=0)
     mixed = mixed.T
     mixed = jnp.concatenate([mixed[:64], mixed[64:]], axis=1).astype(bf16)
     bias = bias_ref[...]
@@ -190,8 +180,7 @@
                 square = v * v
                 th = jnp.tanh(root * (v + 0.044715 * (square * v)))
                 slope = 0.5 * (1.0 + th) + (0.5 * root) * v * (1.0 - th * th) * (1.0 + (3.0 * 0.044715) * square)
-                cot = [early_ref[4 * g + i, R // 2 :, :], got_ref[4 * g + i, 0:late, :]]
-                grad = slope * jnp.concatenate(cot, axis=0).astype(f32)
+                grad = slope * cot_ref[4 * g + i, R // 2 :, :].astype(f32)
                 total = total + grad
                 grads.append(grad.astype(bf16))
             blocks.append(jnp.concatenate(grads, axis=1))
@@ -209,43 +198,56 @@
     rounded = sums.astype(bf16).astype(f32)
     sums = jnp.concatenate([rounded, sums - rounded], axis=1)
     modes = jnp.concatenate([modes[:M], modes[M:]], axis=1)
-    for k in range(KEPT):
-        send[pl.ds(k, PITCH, stride=8), :] = modes[k * PITCH : (k + 1) * PITCH]
-    send[pl.ds(KEPT, PITCH, stride=8), :] = jnp.concatenate([sums] * (PITCH // 8), axis=0)
-    for k in range(KEPT + 1, 8):
-        send[pl.ds(k, PITCH, stride=8), :] = jnp.zeros((PITCH, 128), f32)
+    for k in range(BOTH):
+        send[pl.ds(k, Z, stride=2 * BOTH), :] = modes[k * Z : (k + 1) * Z]
+    send[pl.ds(BOTH, Z, stride=2 * BOTH), :] = jnp.concatenate([sums] * (Z // 8), axis=0)
+    for k in range(BOTH + 1, 2 * BOTH):
+        send[pl.ds(k, Z, stride=2 * BOTH), :] = jnp.zeros((Z, 128), f32)
     out_ref[...] = send[...].astype(bf16)
 
 
-def back_kernel(got_ref, weight_ref, out_ref, grad_ref, bias_ref, scr):
-    blocks = by_mode(scr, got_ref[...].astype(f32), 8)
-    sums = jnp.sum(scr[pl.ds(KEPT, PITCH, stride=8), :], axis=0, keepdims=True)
-    bias_ref[...] = jnp.broadcast_to(sums[:, :64] + sums[:, 64:], (8, 64))
-    for k in range(KEPT):
+def back_kernel(got_ref, weight_ref, spec_ref, out_ref, pack_ref, scr):
+    blocks = by_mode(scr, got_ref[...].astype(f32), 2 * BOTH)
+    inputs = spec_ref.shape[2]
+    sums = jnp.sum(scr[pl.ds(BOTH, Z, stride=2 * BOTH), :], axis=0, keepdims=True)
+    sums = sums[:, :64] + sums[:, 64:]
+    rounded = sums.astype(bf16).astype(f32)
+    sums = jnp.concatenate([rounded, sums - rounded], axis=1)
+    pack_ref[BOTH] = jnp.zeros(pack_ref.shape[1:], bf16)
+    pack_ref[BOTH, :, inputs:] = jnp.broadcast_to(sums, (2 * Z, 128)).astype(bf16)
+    for k in range(BOTH):
         top = blocks[k]
         low = jnp.concatenate([top[:, 64:], -top[:, :64]], axis=1)
         grad = jnp.concatenate([top, low], axis=0).astype(bf16)
-        grad_ref[k] = grad
+        pack_ref[k, :, 0:inputs] = spec_ref[k]
+        pack_ref[k, :, inputs:] = grad
         out = dot(grad, weight_ref[k], NN)
-        rows = slice(k * PITCH, (k + 1) * PITCH)
+        rows = slice(k * Z, (k + 1) * Z)
         for q in range(out_ref.shape[0] // 2):
             lanes = slice(q * 128, (q + 1) * 128)
-            first, second = halves(out[:32, lanes], out[32:, lanes])
+            first, second = halves(out[:Z, lanes], out[Z:, lanes])
             out_ref[2 * q, rows, :] = first.astype(bf16)
             out_ref[2 * q + 1, rows, :] = second.astype(bf16)
 
 
-def weight_kernel(grad_ref, spec_ref, out_ref):
+def weight_kernel(where_ref, pack_ref, out_ref, bias_ref):
+    inputs = pack_ref.shape[3] - 128
     for k in range(KEPT):
-        out_ref[k] = dot(grad_ref[k], spec_ref[k], TN)
+        mode = where_ref[0] * KEPT + k
+        both = [pack_ref[a, mode] for a in range(XH)]
+        grad = jnp.concatenate([block[:, inputs:] for block in both], axis=0)
+        spec = jnp.concatenate([block[:, :inputs] for block in both], axis=0)
+        out_ref[k] = dot(grad, spec, TN)
+    sums = pack_ref[0, BOTH, :, inputs:].astype(f32) + pack_ref[1, BOTH, :, inputs:].astype(f32)
+    bias_ref[...] = (sums[:, :64] + sums[:, 64:])[:8]
 
 
 def collect_kernel(got_ref, out_ref, scr):
     total = got_ref[0].astype(f32)
     for i in range(1, got_ref.shape[0]):
         total = total + got_ref[i].astype(f32)
-    for k in range(KEPT):
-        scr[pl.ds(k, PITCH, stride=KEPT), :] = total[k * PITCH : (k + 1) * PITCH]
+    for k in range(BOTH):
+        scr[pl.ds(k, Z, stride=BOTH), :] = total[k * Z : (k + 1) * Z]
     out_ref[...] = scr[...].astype(bf16)
 
 
@@ -265,7 +267,7 @@
     out_ref[...] = (out[:half] + out[half:]).astype(bf16)
 
 
-def finish_kernel(got_ref, cot_ref, v_ref, out_ref, field, sems):
+def finish_kernel(got_ref, cot_ref, v_ref, bias_ref, out_ref, field, sems):
     sends = []
     for t in range(16):
         low, high = halves(got_ref[t * 32 : t * 32 + 16, :], got_ref[t * 32 + 16 : t * 32 + 32, :])
@@ -302,14 +304,14 @@
 
     first = run(
         points_kernel,
-        shape((PITCH, R // 2 + EARLY, 128), bf16),
+        shape((PITCH, R // 2 + width, 128), bf16),
         const["points"],
         activation,
         cotangent,
         scratch=[
             pltpu.VMEM((2 * R, WIN), bf16),
             pltpu.VMEM(activation.shape, bf16),
-            pltpu.VMEM((PITCH, R // 2 + EARLY, 128), bf16),
+            pltpu.VMEM((PITCH, R // 2 + width, 128), bf16),
             pltpu.SemaphoreType.DMA((13,)),
         ],
         far=3,
@@ -318,21 +320,21 @@
         name="points",
     )
     first = exchange(first, PITCH_AXES)
+    weights = lax.all_gather(weight, "xh", axis=0, tiled=True)
     spectra = run(modes_kernel, small, first, const["modes"], name="modes")
     spectra = exchange(spectra, "z")
-    spectra = run(gather_kernel, shape((XH * chan, M // XH, 128), bf16), spectra, scratch=[square], name="gather")
-    spectra = exchange(spectra, ("xh", "chan"))
+    spectra = run(gather_kernel, across, spectra, scratch=[square], name="gather")
+    spectra = exchange(spectra, "chan")
     mixed, spec = run(
         mix_kernel,
-        (shape((PITCH, width - EARLY + 8, 128), bf16), shape((KEPT, 64, inputs), bf16)),
+        (small, shape((BOTH, 2 * Z, inputs), bf16)),
         spectra,
-        weight,
-        cotangent,
-        scratch=[tall],
+        weights,
+        scratch=[square],
         flops=mix_flops,
         name="mix",
     )
-    mixed = exchange(mixed, PITCH_AXES)
+    mixed = exchange(mixed, "z")
     grads = run(
         pointwise_kernel,
         shape((2 * M, 128), bf16),
@@ -341,25 +343,34 @@
         bias_wide,
         const["doubled"],
         const["expand"],
-        scratch=[tall, tall],
+        scratch=[square, tall],
         name="pointwise",
     )
-    grads = exchange(grads, PITCH_AXES)
-    back, grad, bias = run(
+    grads = exchange(grads, "z")
+    back, pack = run(
         back_kernel,
-        (across, shape((KEPT, 64, 128), bf16), shape((8, 64), f32)),
+        (across, shape((BOTH + 1, 2 * Z, inputs + 128), bf16)),
         grads,
-        weight,
+        weights,
+        spec,
         scratch=[tall],
         flops=mix_flops,
         name="back",
     )
+    pack = lax.all_gather(pack, "xh", axis=0, tiled=False)
     back = exchange(back, "chan")
-    grad_weight = run(
-        weight_kernel, shape((KEPT, 2 * width, inputs), f32), grad, spec, flops=mix_flops, name="weight"
+    where = jnp.reshape(lax.axis_index("xh"), (1,)).astype(jnp.int32)
+    grad_weight, bias = run(
+        weight_kernel,
+        (shape((KEPT, 2 * width, inputs), f32), shape((8, 64), f32)),
+        where,
+        pack,
+        scalars=1,
+        flops=mix_flops,
+        name="weight",
     )
     back = run(collect_kernel, small, back, scratch=[square], name="collect")
-    back = exchange(back, PITCH_AXES)
+    back = exchange(back, "z")
     coefs = run(windows_kernel, coefs_shape, back, const["windows"], name="windows")
     coefs = exchange(coefs, PITCH_AXES)
     grad_input = run(
@@ -368,6 +379,7 @@
         coefs,
         cotangent,
         const["points"],
+        bias,
         scratch=[pltpu.VMEM(activation.shape, bf16), pltpu.SemaphoreType.DMA((4,))],
         far_out=True,
         name="finish",

time: 190 us -> 199 us (1.047)
  blocking collectives: 157 us -> 79.9 us
  waiting for transfers between devices: 15.6 us -> 61.7 us
  starting transfers between devices: 3.86 us -> 26.6 us
  between operations: 0.73 us -> 14.2 us
  local copies, waits for them, and re-layouts: 0.62 us -> 3.53 us
  Pallas kernels: 10.6 us -> 12.6 us
    all_to_all x7 -> x5, blocking collectives: 157 us -> 79.9 us  [exchange(): return lax.all_to_all(blocks, axis, split_axis=0, concat_axis=0, tiled=True)]
    all_to_all x1 -> x3, waiting for transfers between devices: 15.6 us -> 61 us  [exchange(): return lax.all_to_all(blocks, axis, split_axis=0, concat_axis=0, tiled=True)]
    all_to_all x1 -> x3, starting transfers between devices: 3.86 us -> 26.5 us  [exchange(): return lax.all_to_all(blocks, axis, split_axis=0, concat_axis=0, tiled=True)]
    unnamed x16 -> x20, local copies, waits for them, and re-layouts: 0.04 us -> 2.94 us
    pallas_call x10, Pallas kernels: 10.6 us -> 12.6 us  [run(): pl.pallas_call(kernel, out_shape=out_shape, in_specs=near + [pl.BlockSpec...]
  transfers between devices with their start and end apart: 1 -> 5, of which waited for: 1 -> 3; matrix products, arithmetic and copies ran while one was open for 0% -> 0% of each run, Pallas kernels for 1% -> 2%
where the time goes in v7:
time: 199 us
  blocking collectives  79.9 us (40%)
  waiting for transfers between devices  61.7 us (31%)
  starting transfers between devices  26.6 us (13%)
  between operations  14.2 us (7%)
  Pallas kernels  12.6 us (6%)
  local copies, waits for them, and re-layouts  3.53 us (2%)
    all_to_all x5, blocking collectives, exchange(): return lax.all_to_all(blocks, axis, split_axis=0, concat_axis=0, tiled=True)  79.9 us
    all_to_all x3, waiting for transfers between devices, exchange(): return lax.all_to_all(blocks, axis, split_axis=0, concat_axis=0, tiled=True)  61 us
    all_to_all x3, starting transfers between devices, exchange(): return lax.all_to_all(blocks, axis, split_axis=0, concat_axis=0, tiled=True)  26.5 us
    pallas_call x10, Pallas kernels, run(): pl.pallas_call(kernel, out_shape=out_shape, in_specs=near + [pl.BlockSpec...  12.6 us
  transfers between devices with their start and end apart: 5, of which 3 were waited for; matrix products, arithmetic and copies ran while one was open for 0% of the time, Pallas kernels for 2%

profile of v7, /device:TPU:24, one launch (start us, length us, event | category | flops | bytes accessed | tf_op | source)
XLA Modules:
  0.0 198.5 jit_solution(11519012691922774304)
XLA Ops:
  7.2 0.0 copy-start.6
  7.2 2.9 %points.1 = bf16[32,80,128]{2,1,0:T(8,128)(2,1)} custom-call(bf16[64,128]{1,0:T(8,128)(2,1)} %constant.16.clone.v_ref, bf16[32,64,128]{2,1,0:T(8,128)(2,1)} %x_ref.1, bf16[32,64,128]{2,1,0:T(8,128)(2,1)} %cot_ref.3), custom_call_target="tpu_custom_call" | custom-call | bytes 1720320 | tf_op jit(solution)/shard_map/points/pallas_call | solution.py:74
  10.1 17.9 %all-to-all-start = ((bf16[32,80,128]{2,1,0:T(8,128)(2,1)}), bf16[32,80,128]{2,1,0:T(8,128)(2,1)S(1)}, u32[]{:S(2)}, u32[]{:S(2)}) async-start(bf16[32,80,128]{2,1,0:T(8,128)(2,1)} %points.1), calls=%async_computation | async-start | bytes 1310720 | tf_op jit(solution)/shard_map/all_to_all | solution.py:287
  28.0 0.0 all-gather.4.cloned.1.call-start
  28.1 0.7 all-gather.4.cloned.1.call-update
  28.8 36.7 %all-to-all-done.got_ref.cot_ref = bf16[32,80,128]{2,1,0:T(8,128)(2,1)S(1)} async-done(((bf16[32,80,128]{2,1,0:T(8,128)(2,1)}), bf16[32,80,128]{2,1,0:T(8,128)(2,1)S(1)}, u32[]{:S(2)}, u32[]{:S(2)}) %all-to-all-start) | async-done | bytes 655392 | tf_op jit(solution)/shard_map/all_to_all | solution.py:287
  65.5 0.0 copy-done.6
  65.5 0.6 modes.1
  66.1 18.1 %all_to_all.70 = bf16[16,8,128]{2,1,0:T(8,128)(2,1)S(1)} all-to-all(bf16[16,8,128]{2,1,0:T(8,128)(2,1)S(1)} %bitcast.22), channel_id=1, replica_groups=mesh['xh'=2,'z'=16,'chan'=16] {'z'}, dimensions={0} | all-to-all | bytes 65536 | tf_op jit(solution)/shard_map/all_to_all | solution.py:287
  84.2 0.0 copy-start.9
  84.2 0.0 copy-start.5
  84.2 0.0 copy-start.7
  84.2 0.9 gather.1
  85.1 4.7 %all-to-all-start.2 = ((bf16[16,128,128]{2,1,0:T(8,128)(2,1)}), bf16[16,128,128]{2,1,0:T(8,128)(2,1)S(1)}, u32[]{:S(2)}, u32[]{:S(2)}) async-start(bf16[16,128,128]{2,1,0:T(8,128)(2,1)} %gather.1), calls=%async_computation.2 | async-start | bytes 1048576 | tf_op jit(solution)/shard_map/all_to_all | solution.py:287
  89.8 0.0 all-gather.6.cloned.1.call-start
  89.8 0.0 all-gather.4.cloned.1.call-done.weight_ref
  89.9 8.6 %all-to-all-done.2.got_ref = bf16[16,128,128]{2,1,0:T(8,128)(2,1)S(1)} async-done(((bf16[16,128,128]{2,1,0:T(8,128)(2,1)}), bf16[16,128,128]{2,1,0:T(8,128)(2,1)S(1)}, u32[]{:S(2)}, u32[]{:S(2)}) %all-to-all-start.2) | async-done | bytes 524320 | tf_op jit(solution)/shard_map/all_to_all | solution.py:287
  98.5 0.0 copy-start
  98.5 1.6 copy-done
  100.1 0.0 copy-start.1
  100.1 0.9 mix.1
  101.0 15.1 %all_to_all.71 = bf16[16,8,128]{2,1,0:T(8,128)(2,1)S(1)} all-to-all(bf16[16,8,128]{2,1,0:T(8,128)(2,1)S(1)} %bitcast.25), channel_id=1, replica_groups=mesh['xh'=2,'z'=16,'chan'=16] {'z'}, dimensions={0} | all-to-all | bytes 65536 | tf_op jit(solution)/shard_map/all_to_all | solution.py:287
  116.2 0.0 copy-done.9
  116.2 0.1 broadcast_in_dim.2.bias_ref
  116.2 0.0 copy-done.5
  116.2 0.0 copy-done.7
  116.2 1.8 pointwise.1
  118.0 15.3 %all_to_all.72 = bf16[16,16,128]{2,1,0:T(8,128)(2,1)S(1)} all-to-all(bf16[16,16,128]{2,1,0:T(8,128)(2,1)S(1)} %bitcast.18), channel_id=1, replica_groups=mesh['xh'=2,'z'=16,'chan'=16] {'z'}, dimensions={0} | all-to-all | bytes 131072 | tf_op jit(solution)/shard_map/all_to_all | solution.py:287
  133.3 0.0 copy-done.1
  133.3 1.4 back.1
  134.7 0.0 all-gather.6.cloned.1.call-update
  134.7 0.0 copy-start.2
  134.7 0.0 copy-start.8
  134.7 16.3 %all_to_all.73.got_ref = bf16[16,128,128]{2,1,0:T(8,128)(2,1)S(1)} all-to-all(bf16[16,128,128]{2,1,0:T(8,128)(2,1)S(1)} %get-tuple-element.11), channel_id=1, replica_groups=mesh['xh'=2,'z'=16,'chan'=16] {'chan'}, dimensions={0} | all-to-all | bytes 1048576 | tf_op jit(solution)/shard_map/all_to_all | solution.py:287
  151.0 0.1 collect.1
  151.1 15.2 %all_to_all.74 = bf16[16,8,128]{2,1,0:T(8,128)(2,1)S(1)} all-to-all(bf16[16,8,128]{2,1,0:T(8,128)(2,1)S(1)} %bitcast.24), channel_id=1, replica_groups=mesh['xh'=2,'z'=16,'chan'=16] {'z'}, dimensions={0} | all-to-all | bytes 65536 | tf_op jit(solution)/shard_map/all_to_all | solution.py:287
  166.3 0.0 copy-done.4
  166.3 1.2 windows.1
  167.4 3.9 %all-to-all-start.7 = ((bf16[32,16,128]{2,1,0:T(8,128)(2,1)}), bf16[32,16,128]{2,1,0:T(8,128)(2,1)S(1)}, u32[]{:S(2)}, u32[]{:S(2)}) async-start(bf16[32,16,128]{2,1,0:T(8,128)(2,1)} %bitcast.9), calls=%async_computation.7 | async-start | bytes 262144 | tf_op jit(solution)/shard_map/all_to_all | solution.py:287
  171.3 0.0 all-gather.6.cloned.1.call-done
  171.3 0.0 copy-start.3
  171.3 1.3 copy-done.3
  172.6 1.8 weight.1
  174.4 0.5 slice_bitcast_fusion
  174.9 15.6 %all-to-all-done.7 = bf16[32,16,128]{2,1,0:T(8,128)(2,1)S(1)} async-done(((bf16[32,16,128]{2,1,0:T(8,128)(2,1)}), bf16[32,16,128]{2,1,0:T(8,128)(2,1)S(1)}, u32[]{:S(2)}, u32[]{:S(2)}) %all-to-all-start.7) | async-done | bytes 131104 | tf_op jit(solution)/shard_map/all_to_all | solution.py:287
  190.5 0.0 copy-done.2
  190.5 0.0 copy-done.8
  190.5 1.2 finish.1
  (1 shorter events, 0.0 us)
Async XLA Ops:
  7.2 58.3 %copy-start.6 = (bf16[1024,512]{1,0:T(8,128)(2,1)S(1)}, bf16[1024,512]{1,0:T(8,128)(2,1)}, u32[]{:S(2)}) copy-start(bf16[1024,512]{1,0:T(8,128)(2,1)} %constant.17.clone.g_ref) | copy-start | bytes 3145732
  10.1 55.4 %all-to-all-start = ((bf16[32,80,128]{2,1,0:T(8,128)(2,1)}), bf16[32,80,128]{2,1,0:T(8,128)(2,1)S(1)}, u32[]{:S(2)}, u32[]{:S(2)}) async-start(bf16[32,80,128]{2,1,0:T(8,128)(2,1)} %points.1), calls=%async_computation | async-start | bytes 1310720 | tf_op jit(solution)/shard_map/all_to_all | solution.py:287
  28.0 61.8 %all-gather.4.cloned.1.call-start = ((), (), s32[]{:S(2)}) async-start(), calls=%async_computation.8 | async-start | bytes 3145728 | tf_op jit(solution)/shard_map/all_gather | solution.py:323
  84.2 32.0 %copy-start.9 = (f32[64]{0:T(128)S(1)}, f32[64]{0:T(128)}, u32[]{:S(2)}) copy-start(f32[64]{0:T(128)} %param.12) | copy-start | bytes 772
  84.2 32.0 %copy-start.5 = (bf16[2,256,1024]{2,1,0:T(8,128)(2,1)S(1)}, bf16[2,256,1024]{2,1,0:T(8,128)(2,1)}, u32[]{:S(2)}) copy-start(bf16[2,256,1024]{2,1,0:T(8,128)(2,1)} %constant.19.clone.table_ref) | copy-start | bytes 3145732
  84.2 32.0 %copy-start.7 = (bf16[384,512]{1,0:T(8,128)(2,1)S(1)}, bf16[384,512]{1,0:T(8,128)(2,1)}, u32[]{:S(2)}) copy-start(bf16[384,512]{1,0:T(8,128)(2,1)} %constant.20.clone.e_ref) | copy-start | bytes 1179652
  85.1 13.4 %all-to-all-start.2 = ((bf16[16,128,128]{2,1,0:T(8,128)(2,1)}), bf16[16,128,128]{2,1,0:T(8,128)(2,1)S(1)}, u32[]{:S(2)}, u32[]{:S(2)}) async-start(bf16[16,128,128]{2,1,0:T(8,128)(2,1)} %gather.1), calls=%async_computation.2 | async-start | bytes 1048576 | tf_op jit(solution)/shard_map/all_to_all | solution.py:287
  89.8 81.5 %all-gather.6.cloned.1.call-start = ((), (), s32[]{:S(2)}) async-start(), calls=%async_computation.9 | async-start | bytes 1990656 | tf_op jit(solution)/shard_map/all_gather | solution.py:360
  98.5 1.6 copy-start
  100.1 33.2 %copy-start.1 = (bf16[8,128,1024]{2,1,0:T(8,128)(2,1)S(1)}, bf16[8,128,1024]{2,1,0:T(8,128)(2,1)}, u32[]{:S(2)}) copy-start(bf16[8,128,1024]{2,1,0:T(8,128)(2,1)} %all-gather.4.cloned.1.call-done.weight_ref) | copy-start | bytes 6291460
  133.3 33.0 %copy-start.4 = (bf16[1024,512]{1,0:T(8,128)(2,1)S(1)}, bf16[1024,512]{1,0:T(8,128)(2,1)}, u32[]{:S(2)}) copy-start(bf16[1024,512]{1,0:T(8,128)(2,1)} %constant.18.clone.u_ref) | copy-start | bytes 3145732
  134.7 55.8 %copy-start.2 = (bf16[32,64,128]{2,1,0:T(8,128)(2,1)S(1)}, bf16[32,64,128]{2,1,0:T(8,128)(2,1)}, u32[]{:S(2)}) copy-start(bf16[32,64,128]{2,1,0:T(8,128)(2,1)} %cot_ref.3) | copy-start | bytes 1572868
  134.7 55.8 %copy-start.8 = (bf16[64,128]{1,0:T(8,128)(2,1)S(1)}, bf16[64,128]{1,0:T(8,128)(2,1)}, u32[]{:S(2)}) copy-start(bf16[64,128]{1,0:T(8,128)(2,1)} %constant.16.clone.v_ref) | copy-start | bytes 49156
  167.4 23.1 %all-to-all-start.7 = ((bf16[32,16,128]{2,1,0:T(8,128)(2,1)}), bf16[32,16,128]{2,1,0:T(8,128)(2,1)S(1)}, u32[]{:S(2)}, u32[]{:S(2)}) async-start(bf16[32,16,128]{2,1,0:T(8,128)(2,1)} %bitcast.9), calls=%async_computation.7 | async-start | bytes 262144 | tf_op jit(solution)/shard_map/all_to_all | solution.py:287
  171.3 1.3 copy-start.3
Sparse Core Ops, SparseCore 0:
  31.0 47.5 all-gather.3
  134.8 27.3 all-gather.5

commit v8 on v7

--- a/solution.py
+++ b/solution.py
@@ -119,7 +119,7 @@
         sends[i].wait()
 
 
-def modes_kernel(got_ref, g_ref, out_ref):
+def modes_kernel(where_ref, got_ref, g_ref, out_ref):
     got = got_ref[:, 0 : R // 2, :].reshape(PITCH * R // 2, 128)
     part = dot(g_ref[...], got, NN)
     part = part[: 4 * M, :64] + part[4 * M :, 64:]
@@ -132,13 +132,22 @@
     return [scr[pl.ds(k, Z, stride=count), :] for k in range(BOTH)]
 
 
-def gather_kernel(got_ref, out_ref, scr):
+def gather_kernel(got_ref, arrived_ref, out_ref, scr):
     send = jnp.concatenate(by_mode(scr, got_ref[...].astype(f32), BOTH), axis=0).astype(bf16)
     for i in range(out_ref.shape[0]):
         out_ref[i] = send
 
 
-def mix_kernel(got_ref, weight_ref, out_ref, spec_ref, scr):
+def by_place(where_ref, own_ref, other_ref, step):
+    for place in range(XH):
+        refs = [own_ref, other_ref] if place == 0 else [other_ref, own_ref]
+
+        @pl.when(where_ref[0] == place)
+        def _(refs=refs):
+            step([refs[k // KEPT].at[k % KEPT] for k in range(BOTH)])
+
+
+def mix_kernel(where_ref, got_ref, own_ref, other_ref, out_ref, spec_ref, scr):
     for k in range(BOTH):
         rows = slice(k * Z, (k + 1) * Z)
         re, im = [], []
@@ -146,12 +155,16 @@
             first, second = halves(got_ref[2 * q, rows, :], got_ref[2 * q + 1, rows, :])
             re.append(first)
             im.append(second)
-        spec = jnp.concatenate([jnp.concatenate(re, axis=1), jnp.concatenate(im, axis=1)], axis=0)
-        spec_ref[k] = spec
-        out = dot(spec, weight_ref[k], NT)
-        real = out[:Z, :64] - out[Z:, 64:]
-        imag = out[:Z, 64:] + out[Z:, :64]
-        scr[pl.ds(k, Z, stride=BOTH), :] = jnp.concatenate([real, imag], axis=1)
+        spec_ref[k] = jnp.concatenate([jnp.concatenate(re, axis=1), jnp.concatenate(im, axis=1)], axis=0)
+
+    def step(weights):
+        for k in range(BOTH):
+            out = dot(spec_ref[k], weights[k][...], NT)
+            real = out[:Z, :64] - out[Z:, 64:]
+            imag = out[:Z, 64:] + out[Z:, :64]
+            scr[pl.ds(k, Z, stride=BOTH), :] = jnp.concatenate([real, imag], axis=1)
+
+    by_place(where_ref, own_ref, other_ref, step)
     out_ref[...] = scr[...].astype(bf16)
 
 
@@ -206,39 +219,46 @@
     out_ref[...] = send[...].astype(bf16)
 
 
-def back_kernel(got_ref, weight_ref, spec_ref, out_ref, pack_ref, scr):
+def back_kernel(where_ref, got_ref, own_ref, other_ref, spec_ref, out_ref, grad_ref, send_ref, scr):
     blocks = by_mode(scr, got_ref[...].astype(f32), 2 * BOTH)
     inputs = spec_ref.shape[2]
     sums = jnp.sum(scr[pl.ds(BOTH, Z, stride=2 * BOTH), :], axis=0, keepdims=True)
     sums = sums[:, :64] + sums[:, 64:]
     rounded = sums.astype(bf16).astype(f32)
     sums = jnp.concatenate([rounded, sums - rounded], axis=1)
-    pack_ref[BOTH] = jnp.zeros(pack_ref.shape[1:], bf16)
-    pack_ref[BOTH, :, inputs:] = jnp.broadcast_to(sums, (2 * Z, 128)).astype(bf16)
+    grad_ref[BOTH] = jnp.broadcast_to(sums, (2 * Z, 128)).astype(bf16)
     for k in range(BOTH):
         top = blocks[k]
         low = jnp.concatenate([top[:, 64:], -top[:, :64]], axis=1)
-        grad = jnp.concatenate([top, low], axis=0).astype(bf16)
-        pack_ref[k, :, 0:inputs] = spec_ref[k]
-        pack_ref[k, :, inputs:] = grad
-        out = dot(grad, weight_ref[k], NN)
-        rows = slice(k * Z, (k + 1) * Z)
-        for q in range(out_ref.shape[0] // 2):
-            lanes = slice(q * 128, (q + 1) * 128)
-            first, second = halves(out[:Z, lanes], out[Z:, lanes])
-            out_ref[2 * q, rows, :] = first.astype(bf16)
-            out_ref[2 * q + 1, rows, :] = second.astype(bf16)
-
-
-def weight_kernel(where_ref, pack_ref, out_ref, bias_ref):
-    inputs = pack_ref.shape[3] - 128
+        grad_ref[k] = jnp.concatenate([top, low], axis=0).astype(bf16)
+
+    def step(weights):
+        for k in range(BOTH):
+            out = dot(grad_ref[k], weights[k][...], NN)
+            rows = slice(k * Z, (k + 1) * Z)
+            for q in range(out_ref.shape[0] // 2):
+                lanes = slice(q * 128, (q + 1) * 128)
+                first, second = halves(out[:Z, lanes], out[Z:, lanes])
+                out_ref[2 * q, rows, :] = first.astype(bf16)
+                out_ref[2 * q + 1, rows, :] = second.astype(bf16)
+
+    by_place(where_ref, own_ref, other_ref, step)
+    for k in range(KEPT):
+        mode = (1 - where_ref[0]) * KEPT + k
+        send_ref[k, :, 0:inputs] = spec_ref[mode]
+        send_ref[k, :, inputs:] = grad_ref[mode]
+    send_ref[KEPT, :, 0:inputs] = jnp.zeros((2 * Z, inputs), bf16)
+    send_ref[KEPT, :, inputs:] = grad_ref[BOTH]
+
+
+def weight_kernel(where_ref, grad_ref, spec_ref, got_ref, out_ref, bias_ref):
+    inputs = spec_ref.shape[2]
     for k in range(KEPT):
         mode = where_ref[0] * KEPT + k
-        both = [pack_ref[a, mode] for a in range(XH)]
-        grad = jnp.concatenate([block[:, inputs:] for block in both], axis=0)
-        spec = jnp.concatenate([block[:, :inputs] for block in both], axis=0)
+        grad = jnp.concatenate([grad_ref[mode], got_ref[k, :, inputs:]], axis=0)
+        spec = jnp.concatenate([spec_ref[mode], got_ref[k, :, :inputs]], axis=0)
         out_ref[k] = dot(grad, spec, TN)
-    sums = pack_ref[0, BOTH, :, inputs:].astype(f32) + pack_ref[1, BOTH, :, inputs:].astype(f32)
+    sums = grad_ref[BOTH].astype(f32) + got_ref[KEPT, :, inputs:].astype(f32)
     bias_ref[...] = (sums[:, :64] + sums[:, 64:])[:8]
 
 
@@ -295,6 +315,9 @@
     inputs = spectral_weight.shape[3]
     weight = spectral_weight.reshape(KEPT, 2 * width, inputs)
     bias_wide = jnp.broadcast_to(out_bias[:, None], (width, WIN))
+    where = jnp.reshape(lax.axis_index("xh"), (1,)).astype(jnp.int32)
+    pairs = [(0, 1), (1, 0)]
+    partner = lax.ppermute(weight, "xh", pairs)
     square = pltpu.VMEM((M, 128), f32)
     tall = pltpu.VMEM((2 * M, 128), f32)
     small = shape((M, 128), bf16)
@@ -320,16 +343,18 @@
         name="points",
     )
     first = exchange(first, PITCH_AXES)
-    weights = lax.all_gather(weight, "xh", axis=0, tiled=True)
-    spectra = run(modes_kernel, small, first, const["modes"], name="modes")
+    spectra = run(modes_kernel, small, where, first, const["modes"], scalars=1, name="modes")
     spectra = exchange(spectra, "z")
-    spectra = run(gather_kernel, across, spectra, scratch=[square], name="gather")
+    spectra = run(gather_kernel, across, spectra, partner, scratch=[square], far=1, name="gather")
     spectra = exchange(spectra, "chan")
     mixed, spec = run(
         mix_kernel,
         (small, shape((BOTH, 2 * Z, inputs), bf16)),
+        where,
         spectra,
-        weights,
+        weight,
+        partner,
+        scalars=1,
         scratch=[square],
         flops=mix_flops,
         name="mix",
@@ -347,24 +372,32 @@
         name="pointwise",
     )
     grads = exchange(grads, "z")
-    back, pack = run(
+    back, grad, send = run(
         back_kernel,
-        (across, shape((BOTH + 1, 2 * Z, inputs + 128), bf16)),
+        (
+            across,
+            shape((BOTH + 1, 2 * Z, 128), bf16),
+            shape((KEPT + 1, 2 * Z, inputs + 128), bf16),
+        ),
+        where,
         grads,
-        weights,
+        weight,
+        partner,
         spec,
+        scalars=1,
         scratch=[tall],
         flops=mix_flops,
         name="back",
     )
-    pack = lax.all_gather(pack, "xh", axis=0, tiled=False)
+    received = lax.ppermute(send, "xh", pairs)
     back = exchange(back, "chan")
-    where = jnp.reshape(lax.axis_index("xh"), (1,)).astype(jnp.int32)
     grad_weight, bias = run(
         weight_kernel,
         (shape((KEPT, 2 * width, inputs), f32), shape((8, 64), f32)),
         where,
-        pack,
+        grad,
+        spec,
+        received,
         scalars=1,
         flops=mix_flops,
         name="weight",

time: 199 us -> 185 us (0.930)
  blocking collectives: 79.9 us -> 57.5 us
  starting transfers between devices: 26.6 us -> 40.1 us
  between operations: 14.2 us -> 0.8 us
  waiting for transfers between devices: 61.7 us -> 70.2 us
    all_to_all x5 -> x4, blocking collectives: 79.9 us -> 57.5 us  [exchange(): return lax.all_to_all(blocks, axis, split_axis=0, concat_axis=0, tiled=True)]
    all_to_all x3 -> x4, waiting for transfers between devices: 61 us -> 70.2 us  [exchange(): return lax.all_to_all(blocks, axis, split_axis=0, concat_axis=0, tiled=True)]
    ppermute x0 -> x2, starting transfers between devices: none -> 8.36 us  [the longest x1 5.21 us: body(): partner = lax.ppermute(weight, 'xh', pairs)]
    all_to_all x3 -> x4, starting transfers between devices: 26.5 us -> 31.8 us  [exchange(): return lax.all_to_all(blocks, axis, split_axis=0, concat_axis=0, tiled=True)]
  transfers between devices with their start and end apart: 5 -> 6, of which waited for: 3 -> 4; matrix products, arithmetic and copies ran while one was open for 0% -> 0% of each run, Pallas kernels for 2% -> 2%
where the time goes in v8:
time: 185 us; the launch traced here: 184 us
  waiting for transfers between devices  70.2 us (38%)
  blocking collectives  57.5 us (31%)
  starting transfers between devices  40.1 us (22%)
  Pallas kernels  12.3 us (7%)
  local copies, waits for them, and re-layouts  2.57 us (1%)
    all_to_all x4, waiting for transfers between devices, exchange(): return lax.all_to_all(blocks, axis, split_axis=0, concat_axis=0, tiled=True)  70.2 us
    all_to_all x4, blocking collectives, exchange(): return lax.all_to_all(blocks, axis, split_axis=0, concat_axis=0, tiled=True)  57.5 us
    all_to_all x4, starting transfers between devices, exchange(): return lax.all_to_all(blocks, axis, split_axis=0, concat_axis=0, tiled=True)  31.8 us
    pallas_call x10, Pallas kernels, run(): pl.pallas_call(kernel, out_shape=out_shape, in_specs=near + [pl.BlockSpec...  12.3 us
    ppermute x1, starting transfers between devices, body(): partner = lax.ppermute(weight, 'xh', pairs)  5.21 us
  transfers between devices with their start and end apart: 6, of which 4 were waited for; matrix products, arithmetic and copies ran while one was open for 0% of the time, Pallas kernels for 2%

profile of v8, /device:TPU:24, one launch (start us, length us, event | category | flops | bytes accessed | tf_op | source)
XLA Modules:
  0.0 183.5 jit_solution(15856682180109994243)
XLA Ops:
  0.6 0.0 copy-start
  0.6 2.9 %points.1 = bf16[32,80,128]{2,1,0:T(8,128)(2,1)} custom-call(bf16[64,128]{1,0:T(8,128)(2,1)} %constant.16.clone.v_ref, bf16[32,64,128]{2,1,0:T(8,128)(2,1)} %x_ref.1, bf16[32,64,128]{2,1,0:T(8,128)(2,1)} %cot_ref.3), custom_call_target="tpu_custom_call" | custom-call | bytes 1720320 | tf_op jit(solution)/shard_map/points/pallas_call | solution.py:74
  3.5 18.0 %all-to-all-start = ((bf16[32,80,128]{2,1,0:T(8,128)(2,1)}), bf16[32,80,128]{2,1,0:T(8,128)(2,1)S(1)}, u32[]{:S(2)}, u32[]{:S(2)}) async-start(bf16[32,80,128]{2,1,0:T(8,128)(2,1)} %points.1), calls=%async_computation | async-start | bytes 1310720 | tf_op jit(solution)/shard_map/all_to_all | solution.py:307
  21.5 0.0 copy-done
  21.5 5.2 %collective-permute-start = (bf16[4,128,1024]{2,1,0:T(8,128)(2,1)S(1)}, bf16[4,128,1024]{2,1,0:T(8,128)(2,1)S(1)}, u32[]{:S(2)}, u32[]{:S(2)}) collective-permute-start(bf16[4,128,1024]{2,1,0:T(8,128)(2,1)S(1)} %bitcast.15), channel_id=1, source_target_pairs={{0,256},{256,0},{1,257},{257,1},{2,258},{258,2},{3,259},{259,3},{4... | collective-permute-start | bytes 3145736 | tf_op jit(solution)/shard_map/ppermute | solution.py:320
  26.7 32.3 %all-to-all-done.got_ref.cot_ref = bf16[32,80,128]{2,1,0:T(8,128)(2,1)S(1)} async-done(((bf16[32,80,128]{2,1,0:T(8,128)(2,1)}), bf16[32,80,128]{2,1,0:T(8,128)(2,1)S(1)}, u32[]{:S(2)}, u32[]{:S(2)}) %all-to-all-start) | async-done | bytes 655392 | tf_op jit(solution)/shard_map/all_to_all | solution.py:307
  59.0 0.0 copy-start.2
  59.0 1.2 copy-done.2
  60.2 1.2 modes.1
  61.4 5.7 %all-to-all-start.1 = ((bf16[16,8,128]{2,1,0:T(8,128)(2,1)}), bf16[16,8,128]{2,1,0:T(8,128)(2,1)S(1)}, u32[]{:S(2)}, u32[]{:S(2)}) async-start(bf16[16,8,128]{2,1,0:T(8,128)(2,1)} %bitcast.1), calls=%async_computation.1 | async-start | bytes 65536 | tf_op jit(solution)/shard_map/all_to_all | solution.py:307
  67.1 0.0 collective-permute-done.arrived_ref.other_ref
  67.2 12.6 %all-to-all-done.1 = bf16[16,8,128]{2,1,0:T(8,128)(2,1)S(1)} async-done(((bf16[16,8,128]{2,1,0:T(8,128)(2,1)}), bf16[16,8,128]{2,1,0:T(8,128)(2,1)S(1)}, u32[]{:S(2)}, u32[]{:S(2)}) %all-to-all-start.1) | async-done | bytes 32800 | tf_op jit(solution)/shard_map/all_to_all | solution.py:307
  79.8 0.1 gather.1
  79.8 0.0 copy-start.8
  79.9 0.0 copy-start.4
  79.9 0.0 copy-start.5
  79.9 13.4 %all_to_all.70.got_ref = bf16[16,128,128]{2,1,0:T(8,128)(2,1)S(1)} all-to-all(bf16[16,128,128]{2,1,0:T(8,128)(2,1)S(1)} %gather.1), channel_id=1, replica_groups=mesh['xh'=2,'z'=16,'chan'=16] {'chan'}, dimensions={0} | all-to-all | bytes 1048576 | tf_op jit(solution)/shard_map/all_to_all | solution.py:307
  93.2 0.9 mix.1
  94.2 15.1 %all_to_all.71 = bf16[16,8,128]{2,1,0:T(8,128)(2,1)S(1)} all-to-all(bf16[16,8,128]{2,1,0:T(8,128)(2,1)S(1)} %bitcast.24), channel_id=1, replica_groups=mesh['xh'=2,'z'=16,'chan'=16] {'z'}, dimensions={0} | all-to-all | bytes 65536 | tf_op jit(solution)/shard_map/all_to_all | solution.py:307
  109.3 0.0 copy-done.8
  109.3 0.1 broadcast_in_dim.2.bias_ref
  109.4 0.0 copy-done.4
  109.4 0.0 copy-done.5
  109.4 1.8 pointwise.1
  111.2 15.3 %all_to_all.72 = bf16[16,16,128]{2,1,0:T(8,128)(2,1)S(1)} all-to-all(bf16[16,16,128]{2,1,0:T(8,128)(2,1)S(1)} %bitcast.20), channel_id=1, replica_groups=mesh['xh'=2,'z'=16,'chan'=16] {'z'}, dimensions={0} | all-to-all | bytes 131072 | tf_op jit(solution)/shard_map/all_to_all | solution.py:307
  126.5 0.7 back.1
  127.1 0.0 copy-start.7
  127.2 0.7 copy-done.7
  127.9 0.0 copy-start.3
  127.9 0.0 copy-start.1
  127.9 0.0 copy-start.6
  127.9 13.8 %all_to_all.73.got_ref = bf16[16,128,128]{2,1,0:T(8,128)(2,1)S(1)} all-to-all(bf16[16,128,128]{2,1,0:T(8,128)(2,1)S(1)} %get-tuple-element.12), channel_id=1, replica_groups=mesh['xh'=2,'z'=16,'chan'=16] {'chan'}, dimensions={0} | all-to-all | bytes 1048576 | tf_op jit(solution)/shard_map/all_to_all | solution.py:307
  141.7 0.7 collect.1
  142.4 3.5 %all-to-all-start.6 = ((bf16[16,8,128]{2,1,0:T(8,128)(2,1)}), bf16[16,8,128]{2,1,0:T(8,128)(2,1)S(1)}, u32[]{:S(2)}, u32[]{:S(2)}) async-start(bf16[16,8,128]{2,1,0:T(8,128)(2,1)} %bitcast.8), calls=%async_computation.6 | async-start | bytes 65536 | tf_op jit(solution)/shard_map/all_to_all | solution.py:307
  145.9 3.2 %collective-permute-start.1 = (bf16[5,32,1152]{2,1,0:T(8,128)(2,1)}, bf16[5,32,1152]{2,1,0:T(8,128)(2,1)S(1)}, u32[]{:S(2)}, u32[]{:S(2)}) collective-permute-start(bf16[5,32,1152]{2,1,0:T(8,128)(2,1)} %copy-done.7), channel_id=1, source_target_pairs={{0,256},{256,0},{1,257},{257,1},{2,258},{258,2},{3,259},{259,3},{4... | collective-permute-start | bytes 1105928 | tf_op jit(solution)/shard_map/ppermute | solution.py:392
  149.0 9.4 %all-to-all-done.6 = bf16[16,8,128]{2,1,0:T(8,128)(2,1)S(1)} async-done(((bf16[16,8,128]{2,1,0:T(8,128)(2,1)}), bf16[16,8,128]{2,1,0:T(8,128)(2,1)S(1)}, u32[]{:S(2)}, u32[]{:S(2)}) %all-to-all-start.6) | async-done | bytes 32800 | tf_op jit(solution)/shard_map/all_to_all | solution.py:307
  158.4 0.0 copy-done.3
  158.4 1.1 windows.1
  159.5 4.6 %all-to-all-start.7 = ((bf16[32,16,128]{2,1,0:T(8,128)(2,1)}), bf16[32,16,128]{2,1,0:T(8,128)(2,1)S(1)}, u32[]{:S(2)}, u32[]{:S(2)}) async-start(bf16[32,16,128]{2,1,0:T(8,128)(2,1)} %bitcast.10), calls=%async_computation.7 | async-start | bytes 262144 | tf_op jit(solution)/shard_map/all_to_all | solution.py:307
  164.1 0.0 collective-permute-done.1.got_ref
  164.1 1.8 weight.1
  165.9 0.5 slice_bitcast_fusion
  166.4 15.9 %all-to-all-done.7 = bf16[32,16,128]{2,1,0:T(8,128)(2,1)S(1)} async-done(((bf16[32,16,128]{2,1,0:T(8,128)(2,1)}), bf16[32,16,128]{2,1,0:T(8,128)(2,1)S(1)}, u32[]{:S(2)}, u32[]{:S(2)}) %all-to-all-start.7) | async-done | bytes 131104 | tf_op jit(solution)/shard_map/all_to_all | solution.py:307
  182.4 0.0 copy-done.1
  182.4 0.0 copy-done.6
  182.4 1.2 finish.1
Async XLA Ops:
  0.6 20.9 %copy-start = (bf16[4,2,64,1024]{3,2,1,0:T(8,128)(2,1)S(1)}, bf16[4,2,64,1024]{3,2,1,0:T(8,128)(2,1)}, u32[]{:S(2)}) copy-start(bf16[4,2,64,1024]{3,2,1,0:T(8,128)(2,1)} %param.11) | copy-start | bytes 3145732
  3.5 55.4 %all-to-all-start = ((bf16[32,80,128]{2,1,0:T(8,128)(2,1)}), bf16[32,80,128]{2,1,0:T(8,128)(2,1)S(1)}, u32[]{:S(2)}, u32[]{:S(2)}) async-start(bf16[32,80,128]{2,1,0:T(8,128)(2,1)} %points.1), calls=%async_computation | async-start | bytes 1310720 | tf_op jit(solution)/shard_map/all_to_all | solution.py:307
  21.5 45.6 %collective-permute-start = (bf16[4,128,1024]{2,1,0:T(8,128)(2,1)S(1)}, bf16[4,128,1024]{2,1,0:T(8,128)(2,1)S(1)}, u32[]{:S(2)}, u32[]{:S(2)}) collective-permute-start(bf16[4,128,1024]{2,1,0:T(8,128)(2,1)S(1)} %bitcast.15), channel_id=1, source_target_pairs={{0,256},{256,0},{1,257},{257,1},{2,258},{258,2},{3,259},{259,3},{4... | collective-permute-start | bytes 3145736 | tf_op jit(solution)/shard_map/ppermute | solution.py:320
  59.0 1.2 copy-start.2
  61.4 18.4 %all-to-all-start.1 = ((bf16[16,8,128]{2,1,0:T(8,128)(2,1)}), bf16[16,8,128]{2,1,0:T(8,128)(2,1)S(1)}, u32[]{:S(2)}, u32[]{:S(2)}) async-start(bf16[16,8,128]{2,1,0:T(8,128)(2,1)} %bitcast.1), calls=%async_computation.1 | async-start | bytes 65536 | tf_op jit(solution)/shard_map/all_to_all | solution.py:307
  79.8 29.5 %copy-start.8 = (f32[64]{0:T(128)S(1)}, f32[64]{0:T(128)}, u32[]{:S(2)}) copy-start(f32[64]{0:T(128)} %param.12) | copy-start | bytes 772
  79.9 29.6 %copy-start.4 = (bf16[2,256,1024]{2,1,0:T(8,128)(2,1)S(1)}, bf16[2,256,1024]{2,1,0:T(8,128)(2,1)}, u32[]{:S(2)}) copy-start(bf16[2,256,1024]{2,1,0:T(8,128)(2,1)} %constant.19.clone.table_ref) | copy-start | bytes 3145732
  79.9 29.6 %copy-start.5 = (bf16[384,512]{1,0:T(8,128)(2,1)S(1)}, bf16[384,512]{1,0:T(8,128)(2,1)}, u32[]{:S(2)}) copy-start(bf16[384,512]{1,0:T(8,128)(2,1)} %constant.20.clone.e_ref) | copy-start | bytes 1179652
  127.1 0.7 copy-start.7
  127.9 30.5 %copy-start.3 = (bf16[1024,512]{1,0:T(8,128)(2,1)S(1)}, bf16[1024,512]{1,0:T(8,128)(2,1)}, u32[]{:S(2)}) copy-start(bf16[1024,512]{1,0:T(8,128)(2,1)} %constant.18.clone.u_ref) | copy-start | bytes 3145732
  127.9 54.5 %copy-start.1 = (bf16[32,64,128]{2,1,0:T(8,128)(2,1)S(1)}, bf16[32,64,128]{2,1,0:T(8,128)(2,1)}, u32[]{:S(2)}) copy-start(bf16[32,64,128]{2,1,0:T(8,128)(2,1)} %cot_ref.3) | copy-start | bytes 1572868
  127.9 54.5 %copy-start.6 = (bf16[64,128]{1,0:T(8,128)(2,1)S(1)}, bf16[64,128]{1,0:T(8,128)(2,1)}, u32[]{:S(2)}) copy-start(bf16[64,128]{1,0:T(8,128)(2,1)} %constant.16.clone.v_ref) | copy-start | bytes 49156
  142.4 16.0 %all-to-all-start.6 = ((bf16[16,8,128]{2,1,0:T(8,128)(2,1)}), bf16[16,8,128]{2,1,0:T(8,128)(2,1)S(1)}, u32[]{:S(2)}, u32[]{:S(2)}) async-start(bf16[16,8,128]{2,1,0:T(8,128)(2,1)} %bitcast.8), calls=%async_computation.6 | async-start | bytes 65536 | tf_op jit(solution)/shard_map/all_to_all | solution.py:307
  145.9 18.3 %collective-permute-start.1 = (bf16[5,32,1152]{2,1,0:T(8,128)(2,1)}, bf16[5,32,1152]{2,1,0:T(8,128)(2,1)S(1)}, u32[]{:S(2)}, u32[]{:S(2)}) collective-permute-start(bf16[5,32,1152]{2,1,0:T(8,128)(2,1)} %copy-done.7), channel_id=1, source_target_pairs={{0,256},{256,0},{1,257},{257,1},{2,258},{258,2},{3,259},{259,3},{4... | collective-permute-start | bytes 1105928 | tf_op jit(solution)/shard_map/ppermute | solution.py:392
  159.5 22.9 %all-to-all-start.7 = ((bf16[32,16,128]{2,1,0:T(8,128)(2,1)}), bf16[32,16,128]{2,1,0:T(8,128)(2,1)S(1)}, u32[]{:S(2)}, u32[]{:S(2)}) async-start(bf16[32,16,128]{2,1,0:T(8,128)(2,1)} %bitcast.10), calls=%async_computation.7 | async-start | bytes 262144 | tf_op jit(solution)/shard_map/all_to_all | solution.py:307

commit v9 on v8

--- a/solution.py
+++ b/solution.py
@@ -119,7 +119,7 @@
         sends[i].wait()
 
 
-def modes_kernel(where_ref, got_ref, g_ref, out_ref):
+def modes_kernel(where_ref, got_ref, g_ref, arrived_ref, out_ref):
     got = got_ref[:, 0 : R // 2, :].reshape(PITCH * R // 2, 128)
     part = dot(g_ref[...], got, NN)
     part = part[: 4 * M, :64] + part[4 * M :, 64:]
@@ -132,7 +132,7 @@
     return [scr[pl.ds(k, Z, stride=count), :] for k in range(BOTH)]
 
 
-def gather_kernel(got_ref, arrived_ref, out_ref, scr):
+def gather_kernel(got_ref, out_ref, scr):
     send = jnp.concatenate(by_mode(scr, got_ref[...].astype(f32), BOTH), axis=0).astype(bf16)
     for i in range(out_ref.shape[0]):
         out_ref[i] = send
@@ -219,9 +219,8 @@
     out_ref[...] = send[...].astype(bf16)
 
 
-def back_kernel(where_ref, got_ref, own_ref, other_ref, spec_ref, out_ref, grad_ref, send_ref, scr):
+def back_kernel(where_ref, got_ref, own_ref, other_ref, spec_ref, out_ref, grad_ref, scr):
     blocks = by_mode(scr, got_ref[...].astype(f32), 2 * BOTH)
-    inputs = spec_ref.shape[2]
     sums = jnp.sum(scr[pl.ds(BOTH, Z, stride=2 * BOTH), :], axis=0, keepdims=True)
     sums = sums[:, :64] + sums[:, 64:]
     rounded = sums.astype(bf16).astype(f32)
@@ -243,6 +242,10 @@
                 out_ref[2 * q + 1, rows, :] = second.astype(bf16)
 
     by_place(where_ref, own_ref, other_ref, step)
+
+
+def pack_kernel(where_ref, grad_ref, spec_ref, before_ref, send_ref):
+    inputs = spec_ref.shape[2]
     for k in range(KEPT):
         mode = (1 - where_ref[0]) * KEPT + k
         send_ref[k, :, 0:inputs] = spec_ref[mode]
@@ -343,9 +346,9 @@
         name="points",
     )
     first = exchange(first, PITCH_AXES)
-    spectra = run(modes_kernel, small, where, first, const["modes"], scalars=1, name="modes")
+    spectra = run(modes_kernel, small, where, first, const["modes"], partner, scalars=1, far=1, name="modes")
     spectra = exchange(spectra, "z")
-    spectra = run(gather_kernel, across, spectra, partner, scratch=[square], far=1, name="gather")
+    spectra = run(gather_kernel, across, spectra, scratch=[square], name="gather")
     spectra = exchange(spectra, "chan")
     mixed, spec = run(
         mix_kernel,
@@ -372,12 +375,11 @@
         name="pointwise",
     )
     grads = exchange(grads, "z")
-    back, grad, send = run(
+    back, grad = run(
         back_kernel,
         (
             across,
             shape((BOTH + 1, 2 * Z, 128), bf16),
-            shape((KEPT + 1, 2 * Z, inputs + 128), bf16),
         ),
         where,
         grads,
@@ -389,8 +391,22 @@
         flops=mix_flops,
         name="back",
     )
+    back = exchange(back, "chan")
+    back = run(collect_kernel, small, back, scratch=[square], name="collect")
+    send = run(
+        pack_kernel,
+        shape((KEPT + 1, 2 * Z, inputs + 128), bf16),
+        where,
+        grad,
+        spec,
+        back,
+        scalars=1,
+        far=1,
+        name="pack",
+    )
+    back = exchange(back, "z")
+    coefs = run(windows_kernel, coefs_shape, back, const["windows"], name="windows")
     received = lax.ppermute(send, "xh", pairs)
-    back = exchange(back, "chan")
     grad_weight, bias = run(
         weight_kernel,
         (shape((KEPT, 2 * width, inputs), f32), shape((8, 64), f32)),
@@ -402,9 +418,6 @@
         flops=mix_flops,
         name="weight",
     )
-    back = run(collect_kernel, small, back, scratch=[square], name="collect")
-    back = exchange(back, "z")
-    coefs = run(windows_kernel, coefs_shape, back, const["windows"], name="windows")
     coefs = exchange(coefs, PITCH_AXES)
     grad_input = run(
         finish_kernel,

time: 185 us -> 186 us (level)
  blocking collectives: 57.5 us -> 78.2 us
  waiting for transfers between devices: 70.2 us -> 55.5 us
  starting transfers between devices: 40.1 us -> 37.3 us
    all_to_all x4 -> x3, waiting for transfers between devices: 70.2 us -> 26.5 us  [exchange(): return lax.all_to_all(blocks, axis, split_axis=0, concat_axis=0, tiled=True)]
    ppermute x1, waiting for transfers between devices: 0.01 us -> 28.9 us  [body(): partner = lax.ppermute(weight, 'xh', pairs)]
    all_to_all x4 -> x5, blocking collectives: 57.5 us -> 78.2 us  [exchange(): return lax.all_to_all(blocks, axis, split_axis=0, concat_axis=0, tiled=True)]
    all_to_all x4 -> x3, starting transfers between devices: 31.8 us -> 26.9 us  [exchange(): return lax.all_to_all(blocks, axis, split_axis=0, concat_axis=0, tiled=True)]
    ppermute x1, starting transfers between devices: 3.15 us -> 5.17 us  [body(): received = lax.ppermute(send, 'xh', pairs)]
    pallas_call x10 -> x11, Pallas kernels: 12.3 us -> 11.7 us  [run(): pl.pallas_call(kernel, out_shape=out_shape, in_specs=near + [pl.BlockSpec...]
  transfers between devices with their start and end apart: 6 -> 5, of which waited for: 4 -> 4; matrix products, arithmetic and copies ran while one was open for 0% -> 0% of each run, Pallas kernels for 2% -> 2%
where the time goes in v9:
time: 186 us; the launch traced here: 185 us
  blocking collectives  78.2 us (42%)
  waiting for transfers between devices  55.5 us (30%)
  starting transfers between devices  37.3 us (20%)
  Pallas kernels  11.7 us (6%)
    all_to_all x5, blocking collectives, exchange(): return lax.all_to_all(blocks, axis, split_axis=0, concat_axis=0, tiled=True)  78.2 us
    ppermute x1, waiting for transfers between devices, body(): partner = lax.ppermute(weight, 'xh', pairs)  28.9 us
    all_to_all x3, starting transfers between devices, exchange(): return lax.all_to_all(blocks, axis, split_axis=0, concat_axis=0, tiled=True)  26.9 us
    all_to_all x3, waiting for transfers between devices, exchange(): return lax.all_to_all(blocks, axis, split_axis=0, concat_axis=0, tiled=True)  26.5 us
    pallas_call x11, Pallas kernels, run(): pl.pallas_call(kernel, out_shape=out_shape, in_specs=near + [pl.BlockSpec...  11.7 us
    ppermute x1, starting transfers between devices, body(): partner = lax.ppermute(weight, 'xh', pairs)  5.21 us
    ppermute x1, starting transfers between devices, body(): received = lax.ppermute(send, 'xh', pairs)  5.17 us
  transfers between devices with their start and end apart: 5, of which 4 were waited for; matrix products, arithmetic and copies ran while one was open for 0% of the time, Pallas kernels for 2%

profile of v9, /device:TPU:24, one launch (start us, length us, event | category | flops | bytes accessed | tf_op | source)
XLA Modules:
  0.0 185.3 jit_solution(4263581964587351307)
XLA Ops:
  0.6 0.0 copy-start
  0.6 2.9 %points.1 = bf16[32,80,128]{2,1,0:T(8,128)(2,1)} custom-call(bf16[64,128]{1,0:T(8,128)(2,1)} %constant.16.clone.v_ref, bf16[32,64,128]{2,1,0:T(8,128)(2,1)} %x_ref.1, bf16[32,64,128]{2,1,0:T(8,128)(2,1)} %cot_ref.3), custom_call_target="tpu_custom_call" | custom-call | bytes 1720320 | tf_op jit(solution)/shard_map/points/pallas_call | solution.py:74
  3.5 18.0 %all-to-all-start = ((bf16[32,80,128]{2,1,0:T(8,128)(2,1)}), bf16[32,80,128]{2,1,0:T(8,128)(2,1)S(1)}, u32[]{:S(2)}, u32[]{:S(2)}) async-start(bf16[32,80,128]{2,1,0:T(8,128)(2,1)} %points.1), calls=%async_computation | async-start | bytes 1310720 | tf_op jit(solution)/shard_map/all_to_all | solution.py:310
  21.5 0.0 copy-done
  21.5 5.2 %collective-permute-start = (bf16[4,128,1024]{2,1,0:T(8,128)(2,1)S(1)}, bf16[4,128,1024]{2,1,0:T(8,128)(2,1)S(1)}, u32[]{:S(2)}, u32[]{:S(2)}) collective-permute-start(bf16[4,128,1024]{2,1,0:T(8,128)(2,1)S(1)} %bitcast.15), channel_id=1, source_target_pairs={{0,256},{256,0},{1,257},{257,1},{2,258},{258,2},{3,259},{259,3},{4... | collective-permute-start | bytes 3145736 | tf_op jit(solution)/shard_map/ppermute | solution.py:323
  26.7 28.9 %collective-permute-done.arrived_ref.other_ref = bf16[4,128,1024]{2,1,0:T(8,128)(2,1)S(1)} collective-permute-done((bf16[4,128,1024]{2,1,0:T(8,128)(2,1)S(1)}, bf16[4,128,1024]{2,1,0:T(8,128)(2,1)S(1)}, u32[]{:S(2)}, u32[]{:S(2)}) %collective-permute-start) | collective-permute-done | bytes 1048608 | tf_op jit(solution)/shard_map/ppermute | solution.py:323
  55.7 3.3 %all-to-all-done.got_ref.cot_ref = bf16[32,80,128]{2,1,0:T(8,128)(2,1)S(1)} async-done(((bf16[32,80,128]{2,1,0:T(8,128)(2,1)}), bf16[32,80,128]{2,1,0:T(8,128)(2,1)S(1)}, u32[]{:S(2)}, u32[]{:S(2)}) %all-to-all-start) | async-done | bytes 655392 | tf_op jit(solution)/shard_map/all_to_all | solution.py:310
  59.0 0.0 copy-start.4
  59.0 1.2 copy-done.4
  60.2 0.6 modes.1
  60.8 20.7 %all_to_all.70 = bf16[16,8,128]{2,1,0:T(8,128)(2,1)S(1)} all-to-all(bf16[16,8,128]{2,1,0:T(8,128)(2,1)S(1)} %bitcast.22), channel_id=1, replica_groups=mesh['xh'=2,'z'=16,'chan'=16] {'z'}, dimensions={0} | all-to-all | bytes 65536 | tf_op jit(solution)/shard_map/all_to_all | solution.py:310
  81.5 0.0 copy-start.7
  81.5 0.0 copy-start.3
  81.5 0.0 copy-start.5
  81.5 0.1 gather.1
  81.5 13.4 %all_to_all.71.got_ref = bf16[16,128,128]{2,1,0:T(8,128)(2,1)S(1)} all-to-all(bf16[16,128,128]{2,1,0:T(8,128)(2,1)S(1)} %gather.1), channel_id=1, replica_groups=mesh['xh'=2,'z'=16,'chan'=16] {'chan'}, dimensions={0} | all-to-all | bytes 1048576 | tf_op jit(solution)/shard_map/all_to_all | solution.py:310
  94.9 0.9 mix.1
  95.8 15.1 %all_to_all.72 = bf16[16,8,128]{2,1,0:T(8,128)(2,1)S(1)} all-to-all(bf16[16,8,128]{2,1,0:T(8,128)(2,1)S(1)} %bitcast.25), channel_id=1, replica_groups=mesh['xh'=2,'z'=16,'chan'=16] {'z'}, dimensions={0} | all-to-all | bytes 65536 | tf_op jit(solution)/shard_map/all_to_all | solution.py:310
  111.0 0.0 copy-done.7
  111.0 0.1 broadcast_in_dim.2.bias_ref
  111.1 0.0 copy-done.3
  111.1 0.0 copy-done.5
  111.1 1.8 pointwise.1
  112.8 15.3 %all_to_all.73 = bf16[16,16,128]{2,1,0:T(8,128)(2,1)S(1)} all-to-all(bf16[16,16,128]{2,1,0:T(8,128)(2,1)S(1)} %bitcast.19), channel_id=1, replica_groups=mesh['xh'=2,'z'=16,'chan'=16] {'z'}, dimensions={0} | all-to-all | bytes 131072 | tf_op jit(solution)/shard_map/all_to_all | solution.py:310
  128.1 0.7 back.1
  128.8 0.0 copy-start.2
  128.8 13.8 %all_to_all.74.got_ref = bf16[16,128,128]{2,1,0:T(8,128)(2,1)S(1)} all-to-all(bf16[16,128,128]{2,1,0:T(8,128)(2,1)S(1)} %get-tuple-element.11), channel_id=1, replica_groups=mesh['xh'=2,'z'=16,'chan'=16] {'chan'}, dimensions={0} | all-to-all | bytes 1048576 | tf_op jit(solution)/shard_map/all_to_all | solution.py:310
  142.6 0.0 copy-start.1
  142.6 0.0 copy-start.6
  142.6 0.7 collect.1.before_ref
  143.3 3.5 %all-to-all-start.6 = ((bf16[16,8,128]{2,1,0:T(8,128)(2,1)}), bf16[16,8,128]{2,1,0:T(8,128)(2,1)S(1)}, u32[]{:S(2)}, u32[]{:S(2)}) async-start(bf16[16,8,128]{2,1,0:T(8,128)(2,1)} %bitcast.8), calls=%async_computation.6 | async-start | bytes 65536 | tf_op jit(solution)/shard_map/all_to_all | solution.py:310
  146.8 5.2 %collective-permute-start.1 = (bf16[5,32,1152]{2,1,0:T(8,128)(2,1)S(1)}, bf16[5,32,1152]{2,1,0:T(8,128)(2,1)S(1)}, u32[]{:S(2)}, u32[]{:S(2)}) collective-permute-start(bf16[5,32,1152]{2,1,0:T(8,128)(2,1)S(1)} %pack.1), channel_id=1, source_target_pairs={{0,256},{256,0},{1,257},{257,1},{2,258},{258,2},{3,259},{259,3},{4... | collective-permute-start | bytes 1105928 | tf_op jit(solution)/shard_map/ppermute | solution.py:409
  152.0 7.3 %all-to-all-done.6 = bf16[16,8,128]{2,1,0:T(8,128)(2,1)S(1)} async-done(((bf16[16,8,128]{2,1,0:T(8,128)(2,1)}), bf16[16,8,128]{2,1,0:T(8,128)(2,1)S(1)}, u32[]{:S(2)}, u32[]{:S(2)}) %all-to-all-start.6) | async-done | bytes 32800 | tf_op jit(solution)/shard_map/all_to_all | solution.py:310
  159.3 0.0 copy-done.2
  159.3 1.2 windows.1
  160.5 5.4 %all-to-all-start.7 = ((bf16[32,16,128]{2,1,0:T(8,128)(2,1)}), bf16[32,16,128]{2,1,0:T(8,128)(2,1)S(1)}, u32[]{:S(2)}, u32[]{:S(2)}) async-start(bf16[32,16,128]{2,1,0:T(8,128)(2,1)} %bitcast.10), calls=%async_computation.7 | async-start | bytes 262144 | tf_op jit(solution)/shard_map/all_to_all | solution.py:310
  165.9 0.0 collective-permute-done.1.got_ref
  165.9 1.8 weight.1
  167.7 0.5 slice_bitcast_fusion
  168.2 15.9 %all-to-all-done.7 = bf16[32,16,128]{2,1,0:T(8,128)(2,1)S(1)} async-done(((bf16[32,16,128]{2,1,0:T(8,128)(2,1)}), bf16[32,16,128]{2,1,0:T(8,128)(2,1)S(1)}, u32[]{:S(2)}, u32[]{:S(2)}) %all-to-all-start.7) | async-done | bytes 131104 | tf_op jit(solution)/shard_map/all_to_all | solution.py:310
  184.1 0.0 copy-done.1
  184.1 0.0 copy-done.6
  184.1 1.2 finish.1
  (1 shorter events, 0.0 us)
Async XLA Ops:
  0.6 20.9 %copy-start = (bf16[4,2,64,1024]{3,2,1,0:T(8,128)(2,1)S(1)}, bf16[4,2,64,1024]{3,2,1,0:T(8,128)(2,1)}, u32[]{:S(2)}) copy-start(bf16[4,2,64,1024]{3,2,1,0:T(8,128)(2,1)} %param.11) | copy-start | bytes 3145732
  3.5 55.4 %all-to-all-start = ((bf16[32,80,128]{2,1,0:T(8,128)(2,1)}), bf16[32,80,128]{2,1,0:T(8,128)(2,1)S(1)}, u32[]{:S(2)}, u32[]{:S(2)}) async-start(bf16[32,80,128]{2,1,0:T(8,128)(2,1)} %points.1), calls=%async_computation | async-start | bytes 1310720 | tf_op jit(solution)/shard_map/all_to_all | solution.py:310
  21.5 34.2 %collective-permute-start = (bf16[4,128,1024]{2,1,0:T(8,128)(2,1)S(1)}, bf16[4,128,1024]{2,1,0:T(8,128)(2,1)S(1)}, u32[]{:S(2)}, u32[]{:S(2)}) collective-permute-start(bf16[4,128,1024]{2,1,0:T(8,128)(2,1)S(1)} %bitcast.15), channel_id=1, source_target_pairs={{0,256},{256,0},{1,257},{257,1},{2,258},{258,2},{3,259},{259,3},{4... | collective-permute-start | bytes 3145736 | tf_op jit(solution)/shard_map/ppermute | solution.py:323
  59.0 1.2 copy-start.4
  81.5 29.5 %copy-start.7 = (f32[64]{0:T(128)S(1)}, f32[64]{0:T(128)}, u32[]{:S(2)}) copy-start(f32[64]{0:T(128)} %param.12) | copy-start | bytes 772
  81.5 29.6 %copy-start.3 = (bf16[2,256,1024]{2,1,0:T(8,128)(2,1)S(1)}, bf16[2,256,1024]{2,1,0:T(8,128)(2,1)}, u32[]{:S(2)}) copy-start(bf16[2,256,1024]{2,1,0:T(8,128)(2,1)} %constant.19.clone.table_ref) | copy-start | bytes 3145732
  81.5 29.6 %copy-start.5 = (bf16[384,512]{1,0:T(8,128)(2,1)S(1)}, bf16[384,512]{1,0:T(8,128)(2,1)}, u32[]{:S(2)}) copy-start(bf16[384,512]{1,0:T(8,128)(2,1)} %constant.20.clone.e_ref) | copy-start | bytes 1179652
  128.8 30.5 %copy-start.2 = (bf16[1024,512]{1,0:T(8,128)(2,1)S(1)}, bf16[1024,512]{1,0:T(8,128)(2,1)}, u32[]{:S(2)}) copy-start(bf16[1024,512]{1,0:T(8,128)(2,1)} %constant.18.clone.u_ref) | copy-start | bytes 3145732
  142.6 41.5 %copy-start.1 = (bf16[32,64,128]{2,1,0:T(8,128)(2,1)S(1)}, bf16[32,64,128]{2,1,0:T(8,128)(2,1)}, u32[]{:S(2)}) copy-start(bf16[32,64,128]{2,1,0:T(8,128)(2,1)} %cot_ref.3) | copy-start | bytes 1572868
  142.6 41.5 %copy-start.6 = (bf16[64,128]{1,0:T(8,128)(2,1)S(1)}, bf16[64,128]{1,0:T(8,128)(2,1)}, u32[]{:S(2)}) copy-start(bf16[64,128]{1,0:T(8,128)(2,1)} %constant.16.clone.v_ref) | copy-start | bytes 49156
  143.3 16.0 %all-to-all-start.6 = ((bf16[16,8,128]{2,1,0:T(8,128)(2,1)}), bf16[16,8,128]{2,1,0:T(8,128)(2,1)S(1)}, u32[]{:S(2)}, u32[]{:S(2)}) async-start(bf16[16,8,128]{2,1,0:T(8,128)(2,1)} %bitcast.8), calls=%async_computation.6 | async-start | bytes 65536 | tf_op jit(solution)/shard_map/all_to_all | solution.py:310
  146.8 19.1 %collective-permute-start.1 = (bf16[5,32,1152]{2,1,0:T(8,128)(2,1)S(1)}, bf16[5,32,1152]{2,1,0:T(8,128)(2,1)S(1)}, u32[]{:S(2)}, u32[]{:S(2)}) collective-permute-start(bf16[5,32,1152]{2,1,0:T(8,128)(2,1)S(1)} %pack.1), channel_id=1, source_target_pairs={{0,256},{256,0},{1,257},{257,1},{2,258},{258,2},{3,259},{259,3},{4... | collective-permute-start | bytes 1105928 | tf_op jit(solution)/shard_map/ppermute | solution.py:409
  160.5 23.6 %all-to-all-start.7 = ((bf16[32,16,128]{2,1,0:T(8,128)(2,1)}), bf16[32,16,128]{2,1,0:T(8,128)(2,1)S(1)}, u32[]{:S(2)}, u32[]{:S(2)}) async-start(bf16[32,16,128]{2,1,0:T(8,128)(2,1)} %bitcast.10), calls=%async_computation.7 | async-start | bytes 262144 | tf_op jit(solution)/shard_map/all_to_all | solution.py:310

commit v10 on v8

--- a/solution.py
+++ b/solution.py
@@ -147,7 +147,7 @@
             step([refs[k // KEPT].at[k % KEPT] for k in range(BOTH)])
 
 
-def mix_kernel(where_ref, got_ref, own_ref, other_ref, out_ref, spec_ref, scr):
+def mix_kernel(where_ref, got_ref, own_ref, other_ref, out_ref, spec_ref, send_ref, scr):
     for k in range(BOTH):
         rows = slice(k * Z, (k + 1) * Z)
         re, im = [], []
@@ -166,6 +166,8 @@
 
     by_place(where_ref, own_ref, other_ref, step)
     out_ref[...] = scr[...].astype(bf16)
+    for k in range(KEPT):
+        send_ref[k] = spec_ref[(1 - where_ref[0]) * KEPT + k]
 
 
 def pointwise_kernel(got_ref, cot_ref, bias_ref, table_ref, e_ref, out_ref, scr, send):
@@ -219,9 +221,8 @@
     out_ref[...] = send[...].astype(bf16)
 
 
-def back_kernel(where_ref, got_ref, own_ref, other_ref, spec_ref, out_ref, grad_ref, send_ref, scr):
+def back_kernel(where_ref, got_ref, own_ref, other_ref, out_ref, grad_ref, send_ref, scr):
     blocks = by_mode(scr, got_ref[...].astype(f32), 2 * BOTH)
-    inputs = spec_ref.shape[2]
     sums = jnp.sum(scr[pl.ds(BOTH, Z, stride=2 * BOTH), :], axis=0, keepdims=True)
     sums = sums[:, :64] + sums[:, 64:]
     rounded = sums.astype(bf16).astype(f32)
@@ -244,21 +245,17 @@
 
     by_place(where_ref, own_ref, other_ref, step)
     for k in range(KEPT):
-        mode = (1 - where_ref[0]) * KEPT + k
-        send_ref[k, :, 0:inputs] = spec_ref[mode]
-        send_ref[k, :, inputs:] = grad_ref[mode]
-    send_ref[KEPT, :, 0:inputs] = jnp.zeros((2 * Z, inputs), bf16)
-    send_ref[KEPT, :, inputs:] = grad_ref[BOTH]
-
-
-def weight_kernel(where_ref, grad_ref, spec_ref, got_ref, out_ref, bias_ref):
-    inputs = spec_ref.shape[2]
+        send_ref[k] = grad_ref[(1 - where_ref[0]) * KEPT + k]
+    send_ref[KEPT] = grad_ref[BOTH]
+
+
+def weight_kernel(where_ref, grad_ref, spec_ref, other_grad_ref, other_spec_ref, out_ref, bias_ref):
     for k in range(KEPT):
         mode = where_ref[0] * KEPT + k
-        grad = jnp.concatenate([grad_ref[mode], got_ref[k, :, inputs:]], axis=0)
-        spec = jnp.concatenate([spec_ref[mode], got_ref[k, :, :inputs]], axis=0)
+        grad = jnp.concatenate([grad_ref[mode], other_grad_ref[k]], axis=0)
+        spec = jnp.concatenate([spec_ref[mode], other_spec_ref[k]], axis=0)
         out_ref[k] = dot(grad, spec, TN)
-    sums = grad_ref[BOTH].astype(f32) + got_ref[KEPT, :, inputs:].astype(f32)
+    sums = grad_ref[BOTH].astype(f32) + other_grad_ref[KEPT].astype(f32)
     bias_ref[...] = (sums[:, :64] + sums[:, 64:])[:8]
 
 
@@ -347,9 +344,9 @@
     spectra = exchange(spectra, "z")
     spectra = run(gather_kernel, across, spectra, partner, scratch=[square], far=1, name="gather")
     spectra = exchange(spectra, "chan")
-    mixed, spec = run(
+    mixed, spec, send = run(
         mix_kernel,
-        (small, shape((BOTH, 2 * Z, inputs), bf16)),
+        (small, shape((BOTH, 2 * Z, inputs), bf16), shape((KEPT, 2 * Z, inputs), bf16)),
         where,
         spectra,
         weight,
@@ -359,6 +356,7 @@
         flops=mix_flops,
         name="mix",
     )
+    other_spec = lax.ppermute(send, "xh", pairs)
     mixed = exchange(mixed, "z")
     grads = run(
         pointwise_kernel,
@@ -377,19 +375,18 @@
         (
             across,
             shape((BOTH + 1, 2 * Z, 128), bf16),
-            shape((KEPT + 1, 2 * Z, inputs + 128), bf16),
+            shape((KEPT + 1, 2 * Z, 128), bf16),
         ),
         where,
         grads,
         weight,
         partner,
-        spec,
         scalars=1,
         scratch=[tall],
         flops=mix_flops,
         name="back",
     )
-    received = lax.ppermute(send, "xh", pairs)
+    other_grad = lax.ppermute(send, "xh", pairs)
     back = exchange(back, "chan")
     grad_weight, bias = run(
         weight_kernel,
@@ -397,7 +394,8 @@
         where,
         grad,
         spec,
-        received,
+        other_grad,
+        other_spec,
         scalars=1,
         flops=mix_flops,
         name="weight",

time: 185 us -> 182 us (0.984)
  waiting for transfers between devices: 70.2 us -> 53.1 us
  blocking collectives: 57.5 us -> 72.9 us
    all_to_all x4 -> x3, waiting for transfers between devices: 70.2 us -> 47.8 us  [exchange(): return lax.all_to_all(blocks, axis, split_axis=0, concat_axis=0, tiled=True)]
    all_to_all x4 -> x5, blocking collectives: 57.5 us -> 72.9 us  [exchange(): return lax.all_to_all(blocks, axis, split_axis=0, concat_axis=0, tiled=True)]
    ppermute x1 -> x2, waiting for transfers between devices: 0.01 us -> 5.24 us  [the longest x1 4.69 us: body(): other_spec = lax.ppermute(send, 'xh', pairs)]
    all_to_all x4 -> x3, starting transfers between devices: 31.8 us -> 27.6 us  [exchange(): return lax.all_to_all(blocks, axis, split_axis=0, concat_axis=0, tiled=True)]
    ppermute x1 -> x2, starting transfers between devices: 3.15 us -> 7.35 us  [the longest x1 5.19 us: body(): other_spec = lax.ppermute(send, 'xh', pairs)]
  transfers between devices with their start and end apart: 6 -> 6, of which waited for: 4 -> 5; matrix products, arithmetic and copies ran while one was open for 0% -> 0% of each run, Pallas kernels for 2% -> 2%
where the time goes in v10:
time: 182 us; the launch traced here: 180 us
  blocking collectives  72.9 us (40%)
  waiting for transfers between devices  53.1 us (29%)
  starting transfers between devices  40.1 us (22%)
  Pallas kernels  11.7 us (6%)
  local copies, waits for them, and re-layouts  1.85 us (1%)
    all_to_all x5, blocking collectives, exchange(): return lax.all_to_all(blocks, axis, split_axis=0, concat_axis=0, tiled=True)  72.9 us
    all_to_all x3, waiting for transfers between devices, exchange(): return lax.all_to_all(blocks, axis, split_axis=0, concat_axis=0, tiled=True)  47.8 us
    all_to_all x3, starting transfers between devices, exchange(): return lax.all_to_all(blocks, axis, split_axis=0, concat_axis=0, tiled=True)  27.6 us
    pallas_call x10, Pallas kernels, run(): pl.pallas_call(kernel, out_shape=out_shape, in_specs=near + [pl.BlockSpec...  11.7 us
    ppermute x1, starting transfers between devices, body(): partner = lax.ppermute(weight, 'xh', pairs)  5.21 us
    ppermute x1, starting transfers between devices, body(): other_spec = lax.ppermute(send, 'xh', pairs)  5.19 us
    ppermute x1, waiting for transfers between devices, body(): other_spec = lax.ppermute(send, 'xh', pairs)  4.69 us
  transfers between devices with their start and end apart: 6, of which 5 were waited for; matrix products, arithmetic and copies ran while one was open for 0% of the time, Pallas kernels for 2%

profile of v10, /device:TPU:24, one launch (start us, length us, event | category | flops | bytes accessed | tf_op | source)
XLA Modules:
  0.0 180.4 jit_solution(4501287866129359235)
XLA Ops:
  0.6 0.0 copy-start
  0.6 2.9 %points.1 = bf16[32,80,128]{2,1,0:T(8,128)(2,1)} custom-call(bf16[64,128]{1,0:T(8,128)(2,1)} %constant.16.clone.v_ref, bf16[32,64,128]{2,1,0:T(8,128)(2,1)} %x_ref.1, bf16[32,64,128]{2,1,0:T(8,128)(2,1)} %cot_ref.3), custom_call_target="tpu_custom_call" | custom-call | bytes 1720320 | tf_op jit(solution)/shard_map/points/pallas_call | solution.py:74
  3.5 18.0 %all-to-all-start = ((bf16[32,80,128]{2,1,0:T(8,128)(2,1)}), bf16[32,80,128]{2,1,0:T(8,128)(2,1)S(1)}, u32[]{:S(2)}, u32[]{:S(2)}) async-start(bf16[32,80,128]{2,1,0:T(8,128)(2,1)} %points.1), calls=%async_computation | async-start | bytes 1310720 | tf_op jit(solution)/shard_map/all_to_all | solution.py:304
  21.5 0.0 copy-done
  21.5 5.2 %collective-permute-start = (bf16[4,128,1024]{2,1,0:T(8,128)(2,1)S(1)}, bf16[4,128,1024]{2,1,0:T(8,128)(2,1)S(1)}, u32[]{:S(2)}, u32[]{:S(2)}) collective-permute-start(bf16[4,128,1024]{2,1,0:T(8,128)(2,1)S(1)} %bitcast.15), channel_id=1, source_target_pairs={{0,256},{256,0},{1,257},{257,1},{2,258},{258,2},{3,259},{259,3},{4... | collective-permute-start | bytes 3145736 | tf_op jit(solution)/shard_map/ppermute | solution.py:317
  26.7 32.3 %all-to-all-done.got_ref.cot_ref = bf16[32,80,128]{2,1,0:T(8,128)(2,1)S(1)} async-done(((bf16[32,80,128]{2,1,0:T(8,128)(2,1)}), bf16[32,80,128]{2,1,0:T(8,128)(2,1)S(1)}, u32[]{:S(2)}, u32[]{:S(2)}) %all-to-all-start) | async-done | bytes 655392 | tf_op jit(solution)/shard_map/all_to_all | solution.py:304
  59.0 0.0 copy-start.2
  59.0 1.2 copy-done.2
  60.2 1.2 modes.1
  61.4 5.7 %all-to-all-start.1 = ((bf16[16,8,128]{2,1,0:T(8,128)(2,1)}), bf16[16,8,128]{2,1,0:T(8,128)(2,1)S(1)}, u32[]{:S(2)}, u32[]{:S(2)}) async-start(bf16[16,8,128]{2,1,0:T(8,128)(2,1)} %bitcast.1), calls=%async_computation.1 | async-start | bytes 65536 | tf_op jit(solution)/shard_map/all_to_all | solution.py:304
  67.1 0.0 collective-permute-done.arrived_ref.other_ref
  67.2 12.6 %all-to-all-done.1 = bf16[16,8,128]{2,1,0:T(8,128)(2,1)S(1)} async-done(((bf16[16,8,128]{2,1,0:T(8,128)(2,1)}), bf16[16,8,128]{2,1,0:T(8,128)(2,1)S(1)}, u32[]{:S(2)}, u32[]{:S(2)}) %all-to-all-start.1) | async-done | bytes 32800 | tf_op jit(solution)/shard_map/all_to_all | solution.py:304
  79.8 0.1 gather.1
  79.8 0.0 copy-start.7
  79.9 0.0 copy-start.4
  79.9 0.0 copy-start.5
  79.9 13.4 %all_to_all.70.got_ref = bf16[16,128,128]{2,1,0:T(8,128)(2,1)S(1)} all-to-all(bf16[16,128,128]{2,1,0:T(8,128)(2,1)S(1)} %gather.1), channel_id=1, replica_groups=mesh['xh'=2,'z'=16,'chan'=16] {'chan'}, dimensions={0} | all-to-all | bytes 1048576 | tf_op jit(solution)/shard_map/all_to_all | solution.py:304
  93.2 1.0 mix.1
  94.2 15.1 %all_to_all.71 = bf16[16,8,128]{2,1,0:T(8,128)(2,1)S(1)} all-to-all(bf16[16,8,128]{2,1,0:T(8,128)(2,1)S(1)} %bitcast.25), channel_id=1, replica_groups=mesh['xh'=2,'z'=16,'chan'=16] {'z'}, dimensions={0} | all-to-all | bytes 65536 | tf_op jit(solution)/shard_map/all_to_all | solution.py:304
  109.4 0.0 copy-done.7
  109.4 0.1 broadcast_in_dim.2.bias_ref
  109.4 0.0 copy-done.4
  109.4 0.0 copy-done.5
  109.4 1.8 pointwise.1
  111.2 0.0 copy-start.3
  111.2 15.4 %all_to_all.72 = bf16[16,16,128]{2,1,0:T(8,128)(2,1)S(1)} all-to-all(bf16[16,16,128]{2,1,0:T(8,128)(2,1)S(1)} %bitcast.19), channel_id=1, replica_groups=mesh['xh'=2,'z'=16,'chan'=16] {'z'}, dimensions={0} | all-to-all | bytes 131072 | tf_op jit(solution)/shard_map/all_to_all | solution.py:304
  126.6 0.7 back.1
  127.3 0.0 copy-start.1
  127.3 0.0 copy-start.6
  127.3 13.8 %all_to_all.73.got_ref = bf16[16,128,128]{2,1,0:T(8,128)(2,1)S(1)} all-to-all(bf16[16,128,128]{2,1,0:T(8,128)(2,1)S(1)} %get-tuple-element.12), channel_id=1, replica_groups=mesh['xh'=2,'z'=16,'chan'=16] {'chan'}, dimensions={0} | all-to-all | bytes 1048576 | tf_op jit(solution)/shard_map/all_to_all | solution.py:304
  141.1 0.1 collect.1
  141.2 15.2 %all_to_all.74 = bf16[16,8,128]{2,1,0:T(8,128)(2,1)S(1)} all-to-all(bf16[16,8,128]{2,1,0:T(8,128)(2,1)S(1)} %bitcast.24), channel_id=1, replica_groups=mesh['xh'=2,'z'=16,'chan'=16] {'z'}, dimensions={0} | all-to-all | bytes 65536 | tf_op jit(solution)/shard_map/all_to_all | solution.py:304
  156.4 0.0 copy-done.3
  156.4 1.2 windows.1
  157.5 3.9 %all-to-all-start.7 = ((bf16[32,16,128]{2,1,0:T(8,128)(2,1)}), bf16[32,16,128]{2,1,0:T(8,128)(2,1)S(1)}, u32[]{:S(2)}, u32[]{:S(2)}) async-start(bf16[32,16,128]{2,1,0:T(8,128)(2,1)} %bitcast.10), calls=%async_computation.7 | async-start | bytes 262144 | tf_op jit(solution)/shard_map/all_to_all | solution.py:304
  161.4 5.2 %collective-permute-start.2 = (bf16[4,32,1024]{2,1,0:T(8,128)(2,1)S(1)}, bf16[4,32,1024]{2,1,0:T(8,128)(2,1)S(1)}, u32[]{:S(2)}, u32[]{:S(2)}) collective-permute-start(bf16[4,32,1024]{2,1,0:T(8,128)(2,1)S(1)} %get-tuple-element.16), channel_id=1, source_target_pairs={{0,256},{256,0},{1,257},{257,1},{2,258},{258,2},{3,259},{259,3},{4... | collective-permute-start | bytes 786440 | tf_op jit(solution)/shard_map/ppermute | solution.py:359
  166.6 2.2 %collective-permute-start.1 = (bf16[5,32,128]{2,1,0:T(8,128)(2,1)S(1)}, bf16[5,32,128]{2,1,0:T(8,128)(2,1)S(1)}, u32[]{:S(2)}, u32[]{:S(2)}) collective-permute-start(bf16[5,32,128]{2,1,0:T(8,128)(2,1)S(1)} %get-tuple-element.15), channel_id=1, source_target_pairs={{0,256},{256,0},{1,257},{257,1},{2,258},{258,2},{3,259},{259,3},{4... | collective-permute-start | bytes 122888 | tf_op jit(solution)/shard_map/ppermute | solution.py:389
  168.8 4.7 %collective-permute-done.2.other_spec_ref = bf16[4,32,1024]{2,1,0:T(8,128)(2,1)S(1)} collective-permute-done((bf16[4,32,1024]{2,1,0:T(8,128)(2,1)S(1)}, bf16[4,32,1024]{2,1,0:T(8,128)(2,1)S(1)}, u32[]{:S(2)}, u32[]{:S(2)}) %collective-permute-start.2) | collective-permute-done | bytes 262176 | tf_op jit(solution)/shard_map/ppermute | solution.py:359
  173.5 0.5 collective-permute-done.1.other_grad_ref
  174.0 1.8 weight.1
  175.8 0.5 slice_bitcast_fusion
  176.3 3.0 %all-to-all-done.7 = bf16[32,16,128]{2,1,0:T(8,128)(2,1)S(1)} async-done(((bf16[32,16,128]{2,1,0:T(8,128)(2,1)}), bf16[32,16,128]{2,1,0:T(8,128)(2,1)S(1)}, u32[]{:S(2)}, u32[]{:S(2)}) %all-to-all-start.7) | async-done | bytes 131104 | tf_op jit(solution)/shard_map/all_to_all | solution.py:304
  179.3 0.0 copy-done.1
  179.3 0.0 copy-done.6
  179.3 1.2 finish.1
Async XLA Ops:
  0.6 20.9 %copy-start = (bf16[4,2,64,1024]{3,2,1,0:T(8,128)(2,1)S(1)}, bf16[4,2,64,1024]{3,2,1,0:T(8,128)(2,1)}, u32[]{:S(2)}) copy-start(bf16[4,2,64,1024]{3,2,1,0:T(8,128)(2,1)} %param.11) | copy-start | bytes 3145732
  3.5 55.4 %all-to-all-start = ((bf16[32,80,128]{2,1,0:T(8,128)(2,1)}), bf16[32,80,128]{2,1,0:T(8,128)(2,1)S(1)}, u32[]{:S(2)}, u32[]{:S(2)}) async-start(bf16[32,80,128]{2,1,0:T(8,128)(2,1)} %points.1), calls=%async_computation | async-start | bytes 1310720 | tf_op jit(solution)/shard_map/all_to_all | solution.py:304
  21.5 45.6 %collective-permute-start = (bf16[4,128,1024]{2,1,0:T(8,128)(2,1)S(1)}, bf16[4,128,1024]{2,1,0:T(8,128)(2,1)S(1)}, u32[]{:S(2)}, u32[]{:S(2)}) collective-permute-start(bf16[4,128,1024]{2,1,0:T(8,128)(2,1)S(1)} %bitcast.15), channel_id=1, source_target_pairs={{0,256},{256,0},{1,257},{257,1},{2,258},{258,2},{3,259},{259,3},{4... | collective-permute-start | bytes 3145736 | tf_op jit(solution)/shard_map/ppermute | solution.py:317
  59.0 1.2 copy-start.2
  61.4 18.4 %all-to-all-start.1 = ((bf16[16,8,128]{2,1,0:T(8,128)(2,1)}), bf16[16,8,128]{2,1,0:T(8,128)(2,1)S(1)}, u32[]{:S(2)}, u32[]{:S(2)}) async-start(bf16[16,8,128]{2,1,0:T(8,128)(2,1)} %bitcast.1), calls=%async_computation.1 | async-start | bytes 65536 | tf_op jit(solution)/shard_map/all_to_all | solution.py:304
  79.8 29.5 %copy-start.7 = (f32[64]{0:T(128)S(1)}, f32[64]{0:T(128)}, u32[]{:S(2)}) copy-start(f32[64]{0:T(128)} %param.12) | copy-start | bytes 772
  79.9 29.6 %copy-start.4 = (bf16[2,256,1024]{2,1,0:T(8,128)(2,1)S(1)}, bf16[2,256,1024]{2,1,0:T(8,128)(2,1)}, u32[]{:S(2)}) copy-start(bf16[2,256,1024]{2,1,0:T(8,128)(2,1)} %constant.19.clone.table_ref) | copy-start | bytes 3145732
  79.9 29.6 %copy-start.5 = (bf16[384,512]{1,0:T(8,128)(2,1)S(1)}, bf16[384,512]{1,0:T(8,128)(2,1)}, u32[]{:S(2)}) copy-start(bf16[384,512]{1,0:T(8,128)(2,1)} %constant.20.clone.e_ref) | copy-start | bytes 1179652
  111.2 45.2 %copy-start.3 = (bf16[1024,512]{1,0:T(8,128)(2,1)S(1)}, bf16[1024,512]{1,0:T(8,128)(2,1)}, u32[]{:S(2)}) copy-start(bf16[1024,512]{1,0:T(8,128)(2,1)} %constant.18.clone.u_ref) | copy-start | bytes 3145732
  127.3 52.0 %copy-start.1 = (bf16[32,64,128]{2,1,0:T(8,128)(2,1)S(1)}, bf16[32,64,128]{2,1,0:T(8,128)(2,1)}, u32[]{:S(2)}) copy-start(bf16[32,64,128]{2,1,0:T(8,128)(2,1)} %cot_ref.3) | copy-start | bytes 1572868
  127.3 52.0 %copy-start.6 = (bf16[64,128]{1,0:T(8,128)(2,1)S(1)}, bf16[64,128]{1,0:T(8,128)(2,1)}, u32[]{:S(2)}) copy-start(bf16[64,128]{1,0:T(8,128)(2,1)} %constant.16.clone.v_ref) | copy-start | bytes 49156
  157.5 21.7 %all-to-all-start.7 = ((bf16[32,16,128]{2,1,0:T(8,128)(2,1)}), bf16[32,16,128]{2,1,0:T(8,128)(2,1)S(1)}, u32[]{:S(2)}, u32[]{:S(2)}) async-start(bf16[32,16,128]{2,1,0:T(8,128)(2,1)} %bitcast.10), calls=%async_computation.7 | async-start | bytes 262144 | tf_op jit(solution)/shard_map/all_to_all | solution.py:304
  161.4 12.1 %collective-permute-start.2 = (bf16[4,32,1024]{2,1,0:T(8,128)(2,1)S(1)}, bf16[4,32,1024]{2,1,0:T(8,128)(2,1)S(1)}, u32[]{:S(2)}, u32[]{:S(2)}) collective-permute-start(bf16[4,32,1024]{2,1,0:T(8,128)(2,1)S(1)} %get-tuple-element.16), channel_id=1, source_target_pairs={{0,256},{256,0},{1,257},{257,1},{2,258},{258,2},{3,259},{259,3},{4... | collective-permute-start | bytes 786440 | tf_op jit(solution)/shard_map/ppermute | solution.py:359
  166.6 7.4 %collective-permute-start.1 = (bf16[5,32,128]{2,1,0:T(8,128)(2,1)S(1)}, bf16[5,32,128]{2,1,0:T(8,128)(2,1)S(1)}, u32[]{:S(2)}, u32[]{:S(2)}) collective-permute-start(bf16[5,32,128]{2,1,0:T(8,128)(2,1)S(1)} %get-tuple-element.15), channel_id=1, source_target_pairs={{0,256},{256,0},{1,257},{257,1},{2,258},{258,2},{3,259},{259,3},{4... | collective-permute-start | bytes 122888 | tf_op jit(solution)/shard_map/ppermute | solution.py:389

commit v11 on v10

--- a/solution.py
+++ b/solution.py
@@ -28,6 +28,7 @@
 TN = (((0,), (0,)), ((), ()))
 VMEM_LIMIT = 32 * 1024 * 1024
 FIRST_LIMIT = 60 * 1024 * 1024
+MODES_LIMIT = 53 * 1024 * 1024
 
 
 def split_hi_lo(table):
@@ -119,11 +120,18 @@
         sends[i].wait()
 
 
-def modes_kernel(where_ref, got_ref, g_ref, out_ref):
+def modes_kernel(where_ref, got_ref, g_ref, out_ref, table, sems):
+    copies = []
+    for i in range(4):
+        rows = slice(i * 2 * M, (i + 1) * 2 * M)
+        copies.append(pltpu.make_async_copy(g_ref.at[rows], table.at[rows], sems.at[i]))
+        copies[i].start()
     got = got_ref[:, 0 : R // 2, :].reshape(PITCH * R // 2, 128)
-    part = dot(g_ref[...], got, NN)
-    part = part[: 4 * M, :64] + part[4 * M :, 64:]
-    part = part[: 2 * M] + part[2 * M :]
+    parts = []
+    for i in range(4):
+        copies[i].wait()
+        parts.append(dot(table[i * 2 * M : (i + 1) * 2 * M, :], got, NN))
+    part = (parts[0] + parts[1])[:, :64] + (parts[2] + parts[3])[:, 64:]
     out_ref[...] = jnp.concatenate([part[:M], part[M:]], axis=1).astype(bf16)
 
 
@@ -340,7 +348,18 @@
         name="points",
     )
     first = exchange(first, PITCH_AXES)
-    spectra = run(modes_kernel, small, where, first, const["modes"], scalars=1, name="modes")
+    spectra = run(
+        modes_kernel,
+        small,
+        where,
+        first,
+        const["modes"],
+        scalars=1,
+        far=1,
+        scratch=[pltpu.VMEM((8 * M, PITCH * R // 2), bf16), pltpu.SemaphoreType.DMA((4,))],
+        vmem=MODES_LIMIT,
+        name="modes",
+    )
     spectra = exchange(spectra, "z")
     spectra = run(gather_kernel, across, spectra, partner, scratch=[square], far=1, name="gather")
     spectra = exchange(spectra, "chan")

time: 182 us -> 182 us (level)
  no operation moved by 1% of the time
where the time goes in v11:
time: 182 us; the launch traced here: 180 us
  blocking collectives  72.9 us (40%)
  waiting for transfers between devices  53.1 us (29%)
  starting transfers between devices  40.1 us (22%)
  Pallas kernels  12.9 us (7%)
    all_to_all x5, blocking collectives, exchange(): return lax.all_to_all(blocks, axis, split_axis=0, concat_axis=0, tiled=True)  72.9 us
    all_to_all x3, waiting for transfers between devices, exchange(): return lax.all_to_all(blocks, axis, split_axis=0, concat_axis=0, tiled=True)  47.8 us
    all_to_all x3, starting transfers between devices, exchange(): return lax.all_to_all(blocks, axis, split_axis=0, concat_axis=0, tiled=True)  27.6 us
    pallas_call x10, Pallas kernels, run(): pl.pallas_call(kernel, out_shape=out_shape, in_specs=near + [pl.BlockSpec...  12.9 us
    ppermute x1, starting transfers between devices, body(): partner = lax.ppermute(weight, 'xh', pairs)  5.21 us
    ppermute x1, starting transfers between devices, body(): other_spec = lax.ppermute(send, 'xh', pairs)  5.19 us
    ppermute x1, waiting for transfers between devices, body(): other_spec = lax.ppermute(send, 'xh', pairs)  4.7 us
  transfers between devices with their start and end apart: 6, of which 5 were waited for; matrix products, arithmetic and copies ran while one was open for 0% of the time, Pallas kernels for 2%

profile of v11, /device:TPU:24, one launch (start us, length us, event | category | flops | bytes accessed | tf_op | source)
XLA Modules:
  0.0 180.4 jit_solution(8396365903148632371)
XLA Ops:
  0.6 0.0 copy-start
  0.6 2.9 %points.1 = bf16[32,80,128]{2,1,0:T(8,128)(2,1)} custom-call(bf16[64,128]{1,0:T(8,128)(2,1)} %constant.16.clone.v_ref, bf16[32,64,128]{2,1,0:T(8,128)(2,1)} %x_ref.1, bf16[32,64,128]{2,1,0:T(8,128)(2,1)} %cot_ref.3), custom_call_target="tpu_custom_call" | custom-call | bytes 1720320 | tf_op jit(solution)/shard_map/points/pallas_call | solution.py:75
  3.5 18.0 %all-to-all-start = ((bf16[32,80,128]{2,1,0:T(8,128)(2,1)}), bf16[32,80,128]{2,1,0:T(8,128)(2,1)S(1)}, u32[]{:S(2)}, u32[]{:S(2)}) async-start(bf16[32,80,128]{2,1,0:T(8,128)(2,1)} %points.1), calls=%async_computation | async-start | bytes 1310720 | tf_op jit(solution)/shard_map/all_to_all | solution.py:312
  21.5 0.0 copy-done
  21.5 5.2 %collective-permute-start = (bf16[4,128,1024]{2,1,0:T(8,128)(2,1)S(1)}, bf16[4,128,1024]{2,1,0:T(8,128)(2,1)S(1)}, u32[]{:S(2)}, u32[]{:S(2)}) collective-permute-start(bf16[4,128,1024]{2,1,0:T(8,128)(2,1)S(1)} %bitcast.15), channel_id=1, source_target_pairs={{0,256},{256,0},{1,257},{257,1},{2,258},{258,2},{3,259},{259,3},{4... | collective-permute-start | bytes 3145736 | tf_op jit(solution)/shard_map/ppermute | solution.py:325
  26.7 32.3 %all-to-all-done.got_ref.cot_ref = bf16[32,80,128]{2,1,0:T(8,128)(2,1)S(1)} async-done(((bf16[32,80,128]{2,1,0:T(8,128)(2,1)}), bf16[32,80,128]{2,1,0:T(8,128)(2,1)S(1)}, u32[]{:S(2)}, u32[]{:S(2)}) %all-to-all-start) | async-done | bytes 655392 | tf_op jit(solution)/shard_map/all_to_all | solution.py:312
  59.0 2.4 %modes.1 = bf16[128,128]{1,0:T(8,128)(2,1)} custom-call(s32[1]{0:T(128)} %bitcast.where_ref, bf16[32,80,128]{2,1,0:T(8,128)(2,1)S(1)} %all-to-all-done.got_ref.cot_ref, bf16[1024,512]{1,0:T(8,128)(2,1)} %constant.17.clone.g_ref), custom_call_target="tpu_custom_call" | custom-call | bytes 1736708 | tf_op jit(solution)/shard_map/modes/pallas_call | solution.py:75
  61.4 5.8 %all-to-all-start.1 = ((bf16[16,8,128]{2,1,0:T(8,128)(2,1)}), bf16[16,8,128]{2,1,0:T(8,128)(2,1)S(1)}, u32[]{:S(2)}, u32[]{:S(2)}) async-start(bf16[16,8,128]{2,1,0:T(8,128)(2,1)} %bitcast.1), calls=%async_computation.1 | async-start | bytes 65536 | tf_op jit(solution)/shard_map/all_to_all | solution.py:312
  67.2 0.0 collective-permute-done.arrived_ref.other_ref
  67.2 12.6 %all-to-all-done.1 = bf16[16,8,128]{2,1,0:T(8,128)(2,1)S(1)} async-done(((bf16[16,8,128]{2,1,0:T(8,128)(2,1)}), bf16[16,8,128]{2,1,0:T(8,128)(2,1)S(1)}, u32[]{:S(2)}, u32[]{:S(2)}) %all-to-all-start.1) | async-done | bytes 32800 | tf_op jit(solution)/shard_map/all_to_all | solution.py:312
  79.8 0.1 gather.1
  79.8 0.0 copy-start.6
  79.8 0.0 copy-start.3
  79.8 0.0 copy-start.4
  79.8 13.4 %all_to_all.70.got_ref = bf16[16,128,128]{2,1,0:T(8,128)(2,1)S(1)} all-to-all(bf16[16,128,128]{2,1,0:T(8,128)(2,1)S(1)} %gather.1), channel_id=1, replica_groups=mesh['xh'=2,'z'=16,'chan'=16] {'chan'}, dimensions={0} | all-to-all | bytes 1048576 | tf_op jit(solution)/shard_map/all_to_all | solution.py:312
  93.2 1.0 mix.1
  94.2 15.1 %all_to_all.71 = bf16[16,8,128]{2,1,0:T(8,128)(2,1)S(1)} all-to-all(bf16[16,8,128]{2,1,0:T(8,128)(2,1)S(1)} %bitcast.25), channel_id=1, replica_groups=mesh['xh'=2,'z'=16,'chan'=16] {'z'}, dimensions={0} | all-to-all | bytes 65536 | tf_op jit(solution)/shard_map/all_to_all | solution.py:312
  109.4 0.0 copy-done.6
  109.4 0.1 broadcast_in_dim.2.bias_ref
  109.4 0.0 copy-done.3
  109.4 0.0 copy-done.4
  109.4 1.8 pointwise.1
  111.2 0.0 copy-start.2
  111.2 15.4 %all_to_all.72 = bf16[16,16,128]{2,1,0:T(8,128)(2,1)S(1)} all-to-all(bf16[16,16,128]{2,1,0:T(8,128)(2,1)S(1)} %bitcast.19), channel_id=1, replica_groups=mesh['xh'=2,'z'=16,'chan'=16] {'z'}, dimensions={0} | all-to-all | bytes 131072 | tf_op jit(solution)/shard_map/all_to_all | solution.py:312
  126.6 0.7 back.1
  127.3 0.0 copy-start.1
  127.3 0.0 copy-start.5
  127.3 13.8 %all_to_all.73.got_ref = bf16[16,128,128]{2,1,0:T(8,128)(2,1)S(1)} all-to-all(bf16[16,128,128]{2,1,0:T(8,128)(2,1)S(1)} %get-tuple-element.12), channel_id=1, replica_groups=mesh['xh'=2,'z'=16,'chan'=16] {'chan'}, dimensions={0} | all-to-all | bytes 1048576 | tf_op jit(solution)/shard_map/all_to_all | solution.py:312
  141.1 0.1 collect.1
  141.2 15.2 %all_to_all.74 = bf16[16,8,128]{2,1,0:T(8,128)(2,1)S(1)} all-to-all(bf16[16,8,128]{2,1,0:T(8,128)(2,1)S(1)} %bitcast.24), channel_id=1, replica_groups=mesh['xh'=2,'z'=16,'chan'=16] {'z'}, dimensions={0} | all-to-all | bytes 65536 | tf_op jit(solution)/shard_map/all_to_all | solution.py:312
  156.4 0.0 copy-done.2
  156.4 1.2 windows.1
  157.5 3.9 %all-to-all-start.7 = ((bf16[32,16,128]{2,1,0:T(8,128)(2,1)}), bf16[32,16,128]{2,1,0:T(8,128)(2,1)S(1)}, u32[]{:S(2)}, u32[]{:S(2)}) async-start(bf16[32,16,128]{2,1,0:T(8,128)(2,1)} %bitcast.10), calls=%async_computation.7 | async-start | bytes 262144 | tf_op jit(solution)/shard_map/all_to_all | solution.py:312
  161.4 5.2 %collective-permute-start.2 = (bf16[4,32,1024]{2,1,0:T(8,128)(2,1)S(1)}, bf16[4,32,1024]{2,1,0:T(8,128)(2,1)S(1)}, u32[]{:S(2)}, u32[]{:S(2)}) collective-permute-start(bf16[4,32,1024]{2,1,0:T(8,128)(2,1)S(1)} %get-tuple-element.16), channel_id=1, source_target_pairs={{0,256},{256,0},{1,257},{257,1},{2,258},{258,2},{3,259},{259,3},{4... | collective-permute-start | bytes 786440 | tf_op jit(solution)/shard_map/ppermute | solution.py:378
  166.6 2.2 %collective-permute-start.1 = (bf16[5,32,128]{2,1,0:T(8,128)(2,1)S(1)}, bf16[5,32,128]{2,1,0:T(8,128)(2,1)S(1)}, u32[]{:S(2)}, u32[]{:S(2)}) collective-permute-start(bf16[5,32,128]{2,1,0:T(8,128)(2,1)S(1)} %get-tuple-element.15), channel_id=1, source_target_pairs={{0,256},{256,0},{1,257},{257,1},{2,258},{258,2},{3,259},{259,3},{4... | collective-permute-start | bytes 122888 | tf_op jit(solution)/shard_map/ppermute | solution.py:408
  168.8 4.7 %collective-permute-done.2.other_spec_ref = bf16[4,32,1024]{2,1,0:T(8,128)(2,1)S(1)} collective-permute-done((bf16[4,32,1024]{2,1,0:T(8,128)(2,1)S(1)}, bf16[4,32,1024]{2,1,0:T(8,128)(2,1)S(1)}, u32[]{:S(2)}, u32[]{:S(2)}) %collective-permute-start.2) | collective-permute-done | bytes 262176 | tf_op jit(solution)/shard_map/ppermute | solution.py:378
  173.5 0.5 collective-permute-done.1.other_grad_ref
  174.0 1.8 weight.1
  175.8 0.5 slice_bitcast_fusion
  176.3 3.0 %all-to-all-done.7 = bf16[32,16,128]{2,1,0:T(8,128)(2,1)S(1)} async-done(((bf16[32,16,128]{2,1,0:T(8,128)(2,1)}), bf16[32,16,128]{2,1,0:T(8,128)(2,1)S(1)}, u32[]{:S(2)}, u32[]{:S(2)}) %all-to-all-start.7) | async-done | bytes 131104 | tf_op jit(solution)/shard_map/all_to_all | solution.py:312
  179.3 0.0 copy-done.1
  179.3 0.0 copy-done.5
  179.3 1.2 finish.1
Async XLA Ops:
  0.6 20.9 %copy-start = (bf16[4,2,64,1024]{3,2,1,0:T(8,128)(2,1)S(1)}, bf16[4,2,64,1024]{3,2,1,0:T(8,128)(2,1)}, u32[]{:S(2)}) copy-start(bf16[4,2,64,1024]{3,2,1,0:T(8,128)(2,1)} %param.11) | copy-start | bytes 3145732
  3.5 55.4 %all-to-all-start = ((bf16[32,80,128]{2,1,0:T(8,128)(2,1)}), bf16[32,80,128]{2,1,0:T(8,128)(2,1)S(1)}, u32[]{:S(2)}, u32[]{:S(2)}) async-start(bf16[32,80,128]{2,1,0:T(8,128)(2,1)} %points.1), calls=%async_computation | async-start | bytes 1310720 | tf_op jit(solution)/shard_map/all_to_all | solution.py:312
  21.5 45.7 %collective-permute-start = (bf16[4,128,1024]{2,1,0:T(8,128)(2,1)S(1)}, bf16[4,128,1024]{2,1,0:T(8,128)(2,1)S(1)}, u32[]{:S(2)}, u32[]{:S(2)}) collective-permute-start(bf16[4,128,1024]{2,1,0:T(8,128)(2,1)S(1)} %bitcast.15), channel_id=1, source_target_pairs={{0,256},{256,0},{1,257},{257,1},{2,258},{258,2},{3,259},{259,3},{4... | collective-permute-start | bytes 3145736 | tf_op jit(solution)/shard_map/ppermute | solution.py:325
  61.4 18.4 %all-to-all-start.1 = ((bf16[16,8,128]{2,1,0:T(8,128)(2,1)}), bf16[16,8,128]{2,1,0:T(8,128)(2,1)S(1)}, u32[]{:S(2)}, u32[]{:S(2)}) async-start(bf16[16,8,128]{2,1,0:T(8,128)(2,1)} %bitcast.1), calls=%async_computation.1 | async-start | bytes 65536 | tf_op jit(solution)/shard_map/all_to_all | solution.py:312
  79.8 29.5 %copy-start.6 = (f32[64]{0:T(128)S(1)}, f32[64]{0:T(128)}, u32[]{:S(2)}) copy-start(f32[64]{0:T(128)} %param.12) | copy-start | bytes 772
  79.8 29.6 %copy-start.3 = (bf16[2,256,1024]{2,1,0:T(8,128)(2,1)S(1)}, bf16[2,256,1024]{2,1,0:T(8,128)(2,1)}, u32[]{:S(2)}) copy-start(bf16[2,256,1024]{2,1,0:T(8,128)(2,1)} %constant.19.clone.table_ref) | copy-start | bytes 3145732
  79.8 29.6 %copy-start.4 = (bf16[384,512]{1,0:T(8,128)(2,1)S(1)}, bf16[384,512]{1,0:T(8,128)(2,1)}, u32[]{:S(2)}) copy-start(bf16[384,512]{1,0:T(8,128)(2,1)} %constant.20.clone.e_ref) | copy-start | bytes 1179652
  111.2 45.2 %copy-start.2 = (bf16[1024,512]{1,0:T(8,128)(2,1)S(1)}, bf16[1024,512]{1,0:T(8,128)(2,1)}, u32[]{:S(2)}) copy-start(bf16[1024,512]{1,0:T(8,128)(2,1)} %constant.18.clone.u_ref) | copy-start | bytes 3145732
  127.3 52.0 %copy-start.1 = (bf16[32,64,128]{2,1,0:T(8,128)(2,1)S(1)}, bf16[32,64,128]{2,1,0:T(8,128)(2,1)}, u32[]{:S(2)}) copy-start(bf16[32,64,128]{2,1,0:T(8,128)(2,1)} %cot_ref.3) | copy-start | bytes 1572868
  127.3 52.0 %copy-start.5 = (bf16[64,128]{1,0:T(8,128)(2,1)S(1)}, bf16[64,128]{1,0:T(8,128)(2,1)}, u32[]{:S(2)}) copy-start(bf16[64,128]{1,0:T(8,128)(2,1)} %constant.16.clone.v_ref) | copy-start | bytes 49156
  157.5 21.7 %all-to-all-start.7 = ((bf16[32,16,128]{2,1,0:T(8,128)(2,1)}), bf16[32,16,128]{2,1,0:T(8,128)(2,1)S(1)}, u32[]{:S(2)}, u32[]{:S(2)}) async-start(bf16[32,16,128]{2,1,0:T(8,128)(2,1)} %bitcast.10), calls=%async_computation.7 | async-start | bytes 262144 | tf_op jit(solution)/shard_map/all_to_all | solution.py:312
  161.4 12.1 %collective-permute-start.2 = (bf16[4,32,1024]{2,1,0:T(8,128)(2,1)S(1)}, bf16[4,32,1024]{2,1,0:T(8,128)(2,1)S(1)}, u32[]{:S(2)}, u32[]{:S(2)}) collective-permute-start(bf16[4,32,1024]{2,1,0:T(8,128)(2,1)S(1)} %get-tuple-element.16), channel_id=1, source_target_pairs={{0,256},{256,0},{1,257},{257,1},{2,258},{258,2},{3,259},{259,3},{4... | collective-permute-start | bytes 786440 | tf_op jit(solution)/shard_map/ppermute | solution.py:378
  166.6 7.4 %collective-permute-start.1 = (bf16[5,32,128]{2,1,0:T(8,128)(2,1)S(1)}, bf16[5,32,128]{2,1,0:T(8,128)(2,1)S(1)}, u32[]{:S(2)}, u32[]{:S(2)}) collective-permute-start(bf16[5,32,128]{2,1,0:T(8,128)(2,1)S(1)} %get-tuple-element.15), channel_id=1, source_target_pairs={{0,256},{256,0},{1,257},{257,1},{2,258},{258,2},{3,259},{259,3},{4... | collective-permute-start | bytes 122888 | tf_op jit(solution)/shard_map/ppermute | solution.py:408

commit v12 on v10

--- a/solution.py
+++ b/solution.py
@@ -49,7 +49,7 @@
     out["points"] = np.concatenate([hi, lo], axis=0)
     by_z = coef.reshape(2, XH, Z, KEPT, PITCH, 2, R // 2).transpose(5, 0, 2, 1, 3, 4, 6)
     gather = by_z.reshape(2, 2 * M, PITCH * R // 2)
-    out["modes"] = np.stack(split_hi_lo(gather), axis=1).reshape(8 * M, PITCH * R // 2)
+    out["modes"] = gather.astype(ml_dtypes.bfloat16).reshape(4 * M, PITCH * R // 2)
     spread = by_z.transpose(5, 6, 0, 1, 2, 3, 4)
     spread = spread.reshape(PITCH * R // 2, 4 * M)
     out["windows"] = np.concatenate(split_hi_lo(spread), axis=0)
@@ -122,8 +122,7 @@
 def modes_kernel(where_ref, got_ref, g_ref, out_ref):
     got = got_ref[:, 0 : R // 2, :].reshape(PITCH * R // 2, 128)
     part = dot(g_ref[...], got, NN)
-    part = part[: 4 * M, :64] + part[4 * M :, 64:]
-    part = part[: 2 * M] + part[2 * M :]
+    part = part[: 2 * M, :64] + part[2 * M :, 64:]
     out_ref[...] = jnp.concatenate([part[:M], part[M:]], axis=1).astype(bf16)
 
 

time: 182 us -> 181 us (level)
  no operation moved by 1% of the time
where the time goes in v12:
time: 181 us; the launch traced here: 179 us
  blocking collectives  72.9 us (40%)
  waiting for transfers between devices  53.1 us (29%)
  starting transfers between devices  40.1 us (22%)
  Pallas kernels  11.6 us (6%)
    all_to_all x5, blocking collectives, exchange(): return lax.all_to_all(blocks, axis, split_axis=0, concat_axis=0, tiled=True)  72.9 us
    all_to_all x3, waiting for transfers between devices, exchange(): return lax.all_to_all(blocks, axis, split_axis=0, concat_axis=0, tiled=True)  47.8 us
    all_to_all x3, starting transfers between devices, exchange(): return lax.all_to_all(blocks, axis, split_axis=0, concat_axis=0, tiled=True)  27.6 us
    pallas_call x10, Pallas kernels, run(): pl.pallas_call(kernel, out_shape=out_shape, in_specs=near + [pl.BlockSpec...  11.6 us
    ppermute x1, starting transfers between devices, body(): partner = lax.ppermute(weight, 'xh', pairs)  5.21 us
    ppermute x1, starting transfers between devices, body(): other_spec = lax.ppermute(send, 'xh', pairs)  5.19 us
    ppermute x1, waiting for transfers between devices, body(): other_spec = lax.ppermute(send, 'xh', pairs)  4.7 us
  transfers between devices with their start and end apart: 6, of which 5 were waited for; matrix products, arithmetic and copies ran while one was open for 0% of the time, Pallas kernels for 2%

profile of v12, /device:TPU:24, one launch (start us, length us, event | category | flops | bytes accessed | tf_op | source)
XLA Modules:
  0.0 179.1 jit_solution(5508179239801422302)
XLA Ops:
  0.6 0.0 copy-start.4
  0.6 0.0 copy-start
  0.7 2.9 %points.1 = bf16[32,80,128]{2,1,0:T(8,128)(2,1)} custom-call(bf16[64,128]{1,0:T(8,128)(2,1)} %constant.16.clone.v_ref, bf16[32,64,128]{2,1,0:T(8,128)(2,1)} %x_ref.1, bf16[32,64,128]{2,1,0:T(8,128)(2,1)} %cot_ref.3), custom_call_target="tpu_custom_call" | custom-call | bytes 1720320 | tf_op jit(solution)/shard_map/points/pallas_call | solution.py:74
  3.6 17.9 %all-to-all-start = ((bf16[32,80,128]{2,1,0:T(8,128)(2,1)}), bf16[32,80,128]{2,1,0:T(8,128)(2,1)S(1)}, u32[]{:S(2)}, u32[]{:S(2)}) async-start(bf16[32,80,128]{2,1,0:T(8,128)(2,1)} %points.1), calls=%async_computation | async-start | bytes 1310720 | tf_op jit(solution)/shard_map/all_to_all | solution.py:303
  21.5 0.0 copy-done
  21.5 5.2 %collective-permute-start = (bf16[4,128,1024]{2,1,0:T(8,128)(2,1)S(1)}, bf16[4,128,1024]{2,1,0:T(8,128)(2,1)S(1)}, u32[]{:S(2)}, u32[]{:S(2)}) collective-permute-start(bf16[4,128,1024]{2,1,0:T(8,128)(2,1)S(1)} %bitcast.15), channel_id=1, source_target_pairs={{0,256},{256,0},{1,257},{257,1},{2,258},{258,2},{3,259},{259,3},{4... | collective-permute-start | bytes 3145736 | tf_op jit(solution)/shard_map/ppermute | solution.py:316
  26.8 32.2 %all-to-all-done.got_ref.cot_ref = bf16[32,80,128]{2,1,0:T(8,128)(2,1)S(1)} async-done(((bf16[32,80,128]{2,1,0:T(8,128)(2,1)}), bf16[32,80,128]{2,1,0:T(8,128)(2,1)S(1)}, u32[]{:S(2)}, u32[]{:S(2)}) %all-to-all-start) | async-done | bytes 655392 | tf_op jit(solution)/shard_map/all_to_all | solution.py:303
  59.0 0.0 copy-done.4
  59.0 1.1 modes.1
  60.1 5.8 %all-to-all-start.1 = ((bf16[16,8,128]{2,1,0:T(8,128)(2,1)}), bf16[16,8,128]{2,1,0:T(8,128)(2,1)S(1)}, u32[]{:S(2)}, u32[]{:S(2)}) async-start(bf16[16,8,128]{2,1,0:T(8,128)(2,1)} %bitcast.1), calls=%async_computation.1 | async-start | bytes 65536 | tf_op jit(solution)/shard_map/all_to_all | solution.py:303
  65.8 0.0 collective-permute-done.arrived_ref.other_ref
  65.8 12.6 %all-to-all-done.1 = bf16[16,8,128]{2,1,0:T(8,128)(2,1)S(1)} async-done(((bf16[16,8,128]{2,1,0:T(8,128)(2,1)}), bf16[16,8,128]{2,1,0:T(8,128)(2,1)S(1)}, u32[]{:S(2)}, u32[]{:S(2)}) %all-to-all-start.1) | async-done | bytes 32800 | tf_op jit(solution)/shard_map/all_to_all | solution.py:303
  78.5 0.1 gather.1
  78.5 0.0 copy-start.7
  78.5 0.0 copy-start.3
  78.5 0.0 copy-start.5
  78.6 13.4 %all_to_all.70.got_ref = bf16[16,128,128]{2,1,0:T(8,128)(2,1)S(1)} all-to-all(bf16[16,128,128]{2,1,0:T(8,128)(2,1)S(1)} %gather.1), channel_id=1, replica_groups=mesh['xh'=2,'z'=16,'chan'=16] {'chan'}, dimensions={0} | all-to-all | bytes 1048576 | tf_op jit(solution)/shard_map/all_to_all | solution.py:303
  91.9 1.0 mix.1
  92.9 15.1 %all_to_all.71 = bf16[16,8,128]{2,1,0:T(8,128)(2,1)S(1)} all-to-all(bf16[16,8,128]{2,1,0:T(8,128)(2,1)S(1)} %bitcast.25), channel_id=1, replica_groups=mesh['xh'=2,'z'=16,'chan'=16] {'z'}, dimensions={0} | all-to-all | bytes 65536 | tf_op jit(solution)/shard_map/all_to_all | solution.py:303
  108.0 0.0 copy-done.7
  108.0 0.1 broadcast_in_dim.2.bias_ref
  108.1 0.0 copy-done.3
  108.1 0.0 copy-done.5
  108.1 1.8 pointwise.1
  109.9 0.0 copy-start.2
  109.9 15.4 %all_to_all.72 = bf16[16,16,128]{2,1,0:T(8,128)(2,1)S(1)} all-to-all(bf16[16,16,128]{2,1,0:T(8,128)(2,1)S(1)} %bitcast.19), channel_id=1, replica_groups=mesh['xh'=2,'z'=16,'chan'=16] {'z'}, dimensions={0} | all-to-all | bytes 131072 | tf_op jit(solution)/shard_map/all_to_all | solution.py:303
  125.3 0.7 back.1
  126.0 0.0 copy-start.1
  126.0 0.0 copy-start.6
  126.0 13.8 %all_to_all.73.got_ref = bf16[16,128,128]{2,1,0:T(8,128)(2,1)S(1)} all-to-all(bf16[16,128,128]{2,1,0:T(8,128)(2,1)S(1)} %get-tuple-element.12), channel_id=1, replica_groups=mesh['xh'=2,'z'=16,'chan'=16] {'chan'}, dimensions={0} | all-to-all | bytes 1048576 | tf_op jit(solution)/shard_map/all_to_all | solution.py:303
  139.8 0.1 collect.1
  139.9 15.2 %all_to_all.74 = bf16[16,8,128]{2,1,0:T(8,128)(2,1)S(1)} all-to-all(bf16[16,8,128]{2,1,0:T(8,128)(2,1)S(1)} %bitcast.24), channel_id=1, replica_groups=mesh['xh'=2,'z'=16,'chan'=16] {'z'}, dimensions={0} | all-to-all | bytes 65536 | tf_op jit(solution)/shard_map/all_to_all | solution.py:303
  155.1 0.0 copy-done.2
  155.1 1.2 windows.1
  156.2 3.9 %all-to-all-start.7 = ((bf16[32,16,128]{2,1,0:T(8,128)(2,1)}), bf16[32,16,128]{2,1,0:T(8,128)(2,1)S(1)}, u32[]{:S(2)}, u32[]{:S(2)}) async-start(bf16[32,16,128]{2,1,0:T(8,128)(2,1)} %bitcast.10), calls=%async_computation.7 | async-start | bytes 262144 | tf_op jit(solution)/shard_map/all_to_all | solution.py:303
  160.1 5.2 %collective-permute-start.2 = (bf16[4,32,1024]{2,1,0:T(8,128)(2,1)S(1)}, bf16[4,32,1024]{2,1,0:T(8,128)(2,1)S(1)}, u32[]{:S(2)}, u32[]{:S(2)}) collective-permute-start(bf16[4,32,1024]{2,1,0:T(8,128)(2,1)S(1)} %get-tuple-element.16), channel_id=1, source_target_pairs={{0,256},{256,0},{1,257},{257,1},{2,258},{258,2},{3,259},{259,3},{4... | collective-permute-start | bytes 786440 | tf_op jit(solution)/shard_map/ppermute | solution.py:358
  165.3 2.2 %collective-permute-start.1 = (bf16[5,32,128]{2,1,0:T(8,128)(2,1)S(1)}, bf16[5,32,128]{2,1,0:T(8,128)(2,1)S(1)}, u32[]{:S(2)}, u32[]{:S(2)}) collective-permute-start(bf16[5,32,128]{2,1,0:T(8,128)(2,1)S(1)} %get-tuple-element.15), channel_id=1, source_target_pairs={{0,256},{256,0},{1,257},{257,1},{2,258},{258,2},{3,259},{259,3},{4... | collective-permute-start | bytes 122888 | tf_op jit(solution)/shard_map/ppermute | solution.py:388
  167.4 4.7 %collective-permute-done.2.other_spec_ref = bf16[4,32,1024]{2,1,0:T(8,128)(2,1)S(1)} collective-permute-done((bf16[4,32,1024]{2,1,0:T(8,128)(2,1)S(1)}, bf16[4,32,1024]{2,1,0:T(8,128)(2,1)S(1)}, u32[]{:S(2)}, u32[]{:S(2)}) %collective-permute-start.2) | collective-permute-done | bytes 262176 | tf_op jit(solution)/shard_map/ppermute | solution.py:358
  172.1 0.5 collective-permute-done.1.other_grad_ref
  172.7 1.8 weight.1
  174.5 0.5 slice_bitcast_fusion
  175.0 3.0 %all-to-all-done.7 = bf16[32,16,128]{2,1,0:T(8,128)(2,1)S(1)} async-done(((bf16[32,16,128]{2,1,0:T(8,128)(2,1)}), bf16[32,16,128]{2,1,0:T(8,128)(2,1)S(1)}, u32[]{:S(2)}, u32[]{:S(2)}) %all-to-all-start.7) | async-done | bytes 131104 | tf_op jit(solution)/shard_map/all_to_all | solution.py:303
  177.9 0.0 copy-done.1
  178.0 0.0 copy-done.6
  178.0 1.2 finish.1
Async XLA Ops:
  0.6 58.4 %copy-start.4 = (bf16[512,512]{1,0:T(8,128)(2,1)S(1)}, bf16[512,512]{1,0:T(8,128)(2,1)}, u32[]{:S(2)}) copy-start(bf16[512,512]{1,0:T(8,128)(2,1)} %constant.17.clone.g_ref) | copy-start | bytes 1572868
  0.6 20.9 %copy-start = (bf16[4,2,64,1024]{3,2,1,0:T(8,128)(2,1)S(1)}, bf16[4,2,64,1024]{3,2,1,0:T(8,128)(2,1)}, u32[]{:S(2)}) copy-start(bf16[4,2,64,1024]{3,2,1,0:T(8,128)(2,1)} %param.11) | copy-start | bytes 3145732
  3.6 55.4 %all-to-all-start = ((bf16[32,80,128]{2,1,0:T(8,128)(2,1)}), bf16[32,80,128]{2,1,0:T(8,128)(2,1)S(1)}, u32[]{:S(2)}, u32[]{:S(2)}) async-start(bf16[32,80,128]{2,1,0:T(8,128)(2,1)} %points.1), calls=%async_computation | async-start | bytes 1310720 | tf_op jit(solution)/shard_map/all_to_all | solution.py:303
  21.5 44.3 %collective-permute-start = (bf16[4,128,1024]{2,1,0:T(8,128)(2,1)S(1)}, bf16[4,128,1024]{2,1,0:T(8,128)(2,1)S(1)}, u32[]{:S(2)}, u32[]{:S(2)}) collective-permute-start(bf16[4,128,1024]{2,1,0:T(8,128)(2,1)S(1)} %bitcast.15), channel_id=1, source_target_pairs={{0,256},{256,0},{1,257},{257,1},{2,258},{258,2},{3,259},{259,3},{4... | collective-permute-start | bytes 3145736 | tf_op jit(solution)/shard_map/ppermute | solution.py:316
  60.1 18.4 %all-to-all-start.1 = ((bf16[16,8,128]{2,1,0:T(8,128)(2,1)}), bf16[16,8,128]{2,1,0:T(8,128)(2,1)S(1)}, u32[]{:S(2)}, u32[]{:S(2)}) async-start(bf16[16,8,128]{2,1,0:T(8,128)(2,1)} %bitcast.1), calls=%async_computation.1 | async-start | bytes 65536 | tf_op jit(solution)/shard_map/all_to_all | solution.py:303
  78.5 29.5 %copy-start.7 = (f32[64]{0:T(128)S(1)}, f32[64]{0:T(128)}, u32[]{:S(2)}) copy-start(f32[64]{0:T(128)} %param.12) | copy-start | bytes 772
  78.5 29.6 %copy-start.3 = (bf16[2,256,1024]{2,1,0:T(8,128)(2,1)S(1)}, bf16[2,256,1024]{2,1,0:T(8,128)(2,1)}, u32[]{:S(2)}) copy-start(bf16[2,256,1024]{2,1,0:T(8,128)(2,1)} %constant.19.clone.table_ref) | copy-start | bytes 3145732
  78.5 29.6 %copy-start.5 = (bf16[384,512]{1,0:T(8,128)(2,1)S(1)}, bf16[384,512]{1,0:T(8,128)(2,1)}, u32[]{:S(2)}) copy-start(bf16[384,512]{1,0:T(8,128)(2,1)} %constant.20.clone.e_ref) | copy-start | bytes 1179652
  109.9 45.2 %copy-start.2 = (bf16[1024,512]{1,0:T(8,128)(2,1)S(1)}, bf16[1024,512]{1,0:T(8,128)(2,1)}, u32[]{:S(2)}) copy-start(bf16[1024,512]{1,0:T(8,128)(2,1)} %constant.18.clone.u_ref) | copy-start | bytes 3145732
  126.0 52.0 %copy-start.1 = (bf16[32,64,128]{2,1,0:T(8,128)(2,1)S(1)}, bf16[32,64,128]{2,1,0:T(8,128)(2,1)}, u32[]{:S(2)}) copy-start(bf16[32,64,128]{2,1,0:T(8,128)(2,1)} %cot_ref.3) | copy-start | bytes 1572868
  126.0 52.0 %copy-start.6 = (bf16[64,128]{1,0:T(8,128)(2,1)S(1)}, bf16[64,128]{1,0:T(8,128)(2,1)}, u32[]{:S(2)}) copy-start(bf16[64,128]{1,0:T(8,128)(2,1)} %constant.16.clone.v_ref) | copy-start | bytes 49156
  156.2 21.7 %all-to-all-start.7 = ((bf16[32,16,128]{2,1,0:T(8,128)(2,1)}), bf16[32,16,128]{2,1,0:T(8,128)(2,1)S(1)}, u32[]{:S(2)}, u32[]{:S(2)}) async-start(bf16[32,16,128]{2,1,0:T(8,128)(2,1)} %bitcast.10), calls=%async_computation.7 | async-start | bytes 262144 | tf_op jit(solution)/shard_map/all_to_all | solution.py:303
  160.1 12.1 %collective-permute-start.2 = (bf16[4,32,1024]{2,1,0:T(8,128)(2,1)S(1)}, bf16[4,32,1024]{2,1,0:T(8,128)(2,1)S(1)}, u32[]{:S(2)}, u32[]{:S(2)}) collective-permute-start(bf16[4,32,1024]{2,1,0:T(8,128)(2,1)S(1)} %get-tuple-element.16), channel_id=1, source_target_pairs={{0,256},{256,0},{1,257},{257,1},{2,258},{258,2},{3,259},{259,3},{4... | collective-permute-start | bytes 786440 | tf_op jit(solution)/shard_map/ppermute | solution.py:358
  165.3 7.4 %collective-permute-start.1 = (bf16[5,32,128]{2,1,0:T(8,128)(2,1)S(1)}, bf16[5,32,128]{2,1,0:T(8,128)(2,1)S(1)}, u32[]{:S(2)}, u32[]{:S(2)}) collective-permute-start(bf16[5,32,128]{2,1,0:T(8,128)(2,1)S(1)} %get-tuple-element.15), channel_id=1, source_target_pairs={{0,256},{256,0},{1,257},{257,1},{2,258},{258,2},{3,259},{259,3},{4... | collective-permute-start | bytes 122888 | tf_op jit(solution)/shard_map/ppermute | solution.py:388

commit v13 on v12

--- a/solution.py
+++ b/solution.py
@@ -91,23 +91,23 @@
 
 
 def points_kernel(v_ref, x_ref, cot_ref, out_ref, basis, field, message, sems):
-    table = pltpu.make_async_copy(v_ref, basis, sems.at[12])
+    table = pltpu.make_async_copy(v_ref, basis, sems.at[24])
     fields, cots, sends = [], [], []
-    for i in range(4):
-        part = slice(8 * i, 8 * i + 8)
+    for i in range(8):
+        part = slice(4 * i, 4 * i + 4)
         fields.append(pltpu.make_async_copy(x_ref.at[part], field.at[part], sems.at[i]))
         cots.append(
-            pltpu.make_async_copy(cot_ref.at[part], message.at[part, R // 2 :, :], sems.at[4 + i])
+            pltpu.make_async_copy(cot_ref.at[part], message.at[part, R // 2 :, :], sems.at[8 + i])
         )
-        sends.append(pltpu.make_async_copy(message.at[part], out_ref.at[part], sems.at[8 + i]))
+        sends.append(pltpu.make_async_copy(message.at[part], out_ref.at[part], sems.at[16 + i]))
     table.start()
-    for i in range(4):
+    for i in range(8):
         fields[i].start()
         cots[i].start()
     table.wait()
-    for i in range(4):
+    for i in range(8):
         fields[i].wait()
-        for t in range(4 * i, 4 * i + 4):
+        for t in range(2 * i, 2 * i + 2):
             y = dot(basis[...], field[2 * t : 2 * t + 2].reshape(128, WIN), NT)
             y = y[:R] + y[R:]
             first, second = halves(y[:16], y[16:])
@@ -115,7 +115,7 @@
             message[2 * t + 1, 0:16, :] = second.astype(bf16)
         cots[i].wait()
         sends[i].start()
-    for i in range(4):
+    for i in range(8):
         sends[i].wait()
 
 
@@ -331,7 +331,7 @@
             pltpu.VMEM((2 * R, WIN), bf16),
             pltpu.VMEM(activation.shape, bf16),
             pltpu.VMEM((PITCH, R // 2 + width, 128), bf16),
-            pltpu.SemaphoreType.DMA((13,)),
+            pltpu.SemaphoreType.DMA((25,)),
         ],
         far=3,
         far_out=True,

time: 181 us -> 181 us (level)
  no operation moved by 1% of the time
where the time goes in v13:
time: 181 us; the launch traced here: 180 us
  blocking collectives  72.9 us (40%)
  waiting for transfers between devices  53.1 us (29%)
  starting transfers between devices  40.1 us (22%)
  Pallas kernels  12.4 us (7%)
    all_to_all x5, blocking collectives, exchange(): return lax.all_to_all(blocks, axis, split_axis=0, concat_axis=0, tiled=True)  72.9 us
    all_to_all x3, waiting for transfers between devices, exchange(): return lax.all_to_all(blocks, axis, split_axis=0, concat_axis=0, tiled=True)  47.8 us
    all_to_all x3, starting transfers between devices, exchange(): return lax.all_to_all(blocks, axis, split_axis=0, concat_axis=0, tiled=True)  27.6 us
    pallas_call x10, Pallas kernels, run(): pl.pallas_call(kernel, out_shape=out_shape, in_specs=near + [pl.BlockSpec...  12.4 us
    ppermute x1, starting transfers between devices, body(): partner = lax.ppermute(weight, 'xh', pairs)  5.21 us
    ppermute x1, starting transfers between devices, body(): other_spec = lax.ppermute(send, 'xh', pairs)  5.19 us
    ppermute x1, waiting for transfers between devices, body(): other_spec = lax.ppermute(send, 'xh', pairs)  4.68 us
  transfers between devices with their start and end apart: 6, of which 5 were waited for; matrix products, arithmetic and copies ran while one was open for 0% of the time, Pallas kernels for 2%

profile of v13, /device:TPU:24, one launch (start us, length us, event | category | flops | bytes accessed | tf_op | source)
XLA Modules:
  0.0 179.9 jit_solution(3996503888828603969)
XLA Ops:
  0.6 0.0 copy-start.4
  0.6 0.0 copy-start
  0.7 3.7 %points.1 = bf16[32,80,128]{2,1,0:T(8,128)(2,1)} custom-call(bf16[64,128]{1,0:T(8,128)(2,1)} %constant.16.clone.v_ref, bf16[32,64,128]{2,1,0:T(8,128)(2,1)} %x_ref.1, bf16[32,64,128]{2,1,0:T(8,128)(2,1)} %cot_ref.3), custom_call_target="tpu_custom_call" | custom-call | bytes 1720320 | tf_op jit(solution)/shard_map/points/pallas_call | solution.py:74
  4.3 18.0 %all-to-all-start = ((bf16[32,80,128]{2,1,0:T(8,128)(2,1)}), bf16[32,80,128]{2,1,0:T(8,128)(2,1)S(1)}, u32[]{:S(2)}, u32[]{:S(2)}) async-start(bf16[32,80,128]{2,1,0:T(8,128)(2,1)} %points.1), calls=%async_computation | async-start | bytes 1310720 | tf_op jit(solution)/shard_map/all_to_all | solution.py:303
  22.3 0.0 copy-done
  22.3 5.2 %collective-permute-start = (bf16[4,128,1024]{2,1,0:T(8,128)(2,1)S(1)}, bf16[4,128,1024]{2,1,0:T(8,128)(2,1)S(1)}, u32[]{:S(2)}, u32[]{:S(2)}) collective-permute-start(bf16[4,128,1024]{2,1,0:T(8,128)(2,1)S(1)} %bitcast.15), channel_id=1, source_target_pairs={{0,256},{256,0},{1,257},{257,1},{2,258},{258,2},{3,259},{259,3},{4... | collective-permute-start | bytes 3145736 | tf_op jit(solution)/shard_map/ppermute | solution.py:316
  27.5 32.3 %all-to-all-done.got_ref.cot_ref = bf16[32,80,128]{2,1,0:T(8,128)(2,1)S(1)} async-done(((bf16[32,80,128]{2,1,0:T(8,128)(2,1)}), bf16[32,80,128]{2,1,0:T(8,128)(2,1)S(1)}, u32[]{:S(2)}, u32[]{:S(2)}) %all-to-all-start) | async-done | bytes 655392 | tf_op jit(solution)/shard_map/all_to_all | solution.py:303
  59.8 0.0 copy-done.4
  59.8 1.1 modes.1
  60.8 5.8 %all-to-all-start.1 = ((bf16[16,8,128]{2,1,0:T(8,128)(2,1)}), bf16[16,8,128]{2,1,0:T(8,128)(2,1)S(1)}, u32[]{:S(2)}, u32[]{:S(2)}) async-start(bf16[16,8,128]{2,1,0:T(8,128)(2,1)} %bitcast.1), calls=%async_computation.1 | async-start | bytes 65536 | tf_op jit(solution)/shard_map/all_to_all | solution.py:303
  66.6 0.0 collective-permute-done.arrived_ref.other_ref
  66.6 12.6 %all-to-all-done.1 = bf16[16,8,128]{2,1,0:T(8,128)(2,1)S(1)} async-done(((bf16[16,8,128]{2,1,0:T(8,128)(2,1)}), bf16[16,8,128]{2,1,0:T(8,128)(2,1)S(1)}, u32[]{:S(2)}, u32[]{:S(2)}) %all-to-all-start.1) | async-done | bytes 32800 | tf_op jit(solution)/shard_map/all_to_all | solution.py:303
  79.2 0.1 gather.1
  79.3 0.0 copy-start.7
  79.3 0.0 copy-start.3
  79.3 0.0 copy-start.5
  79.3 13.4 %all_to_all.70.got_ref = bf16[16,128,128]{2,1,0:T(8,128)(2,1)S(1)} all-to-all(bf16[16,128,128]{2,1,0:T(8,128)(2,1)S(1)} %gather.1), channel_id=1, replica_groups=mesh['xh'=2,'z'=16,'chan'=16] {'chan'}, dimensions={0} | all-to-all | bytes 1048576 | tf_op jit(solution)/shard_map/all_to_all | solution.py:303
  92.7 1.0 mix.1
  93.7 15.1 %all_to_all.71 = bf16[16,8,128]{2,1,0:T(8,128)(2,1)S(1)} all-to-all(bf16[16,8,128]{2,1,0:T(8,128)(2,1)S(1)} %bitcast.25), channel_id=1, replica_groups=mesh['xh'=2,'z'=16,'chan'=16] {'z'}, dimensions={0} | all-to-all | bytes 65536 | tf_op jit(solution)/shard_map/all_to_all | solution.py:303
  108.8 0.0 copy-done.7
  108.8 0.1 broadcast_in_dim.2.bias_ref
  108.9 0.0 copy-done.3
  108.9 0.0 copy-done.5
  108.9 1.8 pointwise.1
  110.7 0.0 copy-start.2
  110.7 15.4 %all_to_all.72 = bf16[16,16,128]{2,1,0:T(8,128)(2,1)S(1)} all-to-all(bf16[16,16,128]{2,1,0:T(8,128)(2,1)S(1)} %bitcast.19), channel_id=1, replica_groups=mesh['xh'=2,'z'=16,'chan'=16] {'z'}, dimensions={0} | all-to-all | bytes 131072 | tf_op jit(solution)/shard_map/all_to_all | solution.py:303
  126.1 0.7 back.1
  126.8 0.0 copy-start.1
  126.8 0.0 copy-start.6
  126.8 13.8 %all_to_all.73.got_ref = bf16[16,128,128]{2,1,0:T(8,128)(2,1)S(1)} all-to-all(bf16[16,128,128]{2,1,0:T(8,128)(2,1)S(1)} %get-tuple-element.12), channel_id=1, replica_groups=mesh['xh'=2,'z'=16,'chan'=16] {'chan'}, dimensions={0} | all-to-all | bytes 1048576 | tf_op jit(solution)/shard_map/all_to_all | solution.py:303
  140.6 0.1 collect.1
  140.6 15.2 %all_to_all.74 = bf16[16,8,128]{2,1,0:T(8,128)(2,1)S(1)} all-to-all(bf16[16,8,128]{2,1,0:T(8,128)(2,1)S(1)} %bitcast.24), channel_id=1, replica_groups=mesh['xh'=2,'z'=16,'chan'=16] {'z'}, dimensions={0} | all-to-all | bytes 65536 | tf_op jit(solution)/shard_map/all_to_all | solution.py:303
  155.8 0.0 copy-done.2
  155.8 1.2 windows.1
  157.0 3.9 %all-to-all-start.7 = ((bf16[32,16,128]{2,1,0:T(8,128)(2,1)}), bf16[32,16,128]{2,1,0:T(8,128)(2,1)S(1)}, u32[]{:S(2)}, u32[]{:S(2)}) async-start(bf16[32,16,128]{2,1,0:T(8,128)(2,1)} %bitcast.10), calls=%async_computation.7 | async-start | bytes 262144 | tf_op jit(solution)/shard_map/all_to_all | solution.py:303
  160.9 5.2 %collective-permute-start.2 = (bf16[4,32,1024]{2,1,0:T(8,128)(2,1)S(1)}, bf16[4,32,1024]{2,1,0:T(8,128)(2,1)S(1)}, u32[]{:S(2)}, u32[]{:S(2)}) collective-permute-start(bf16[4,32,1024]{2,1,0:T(8,128)(2,1)S(1)} %get-tuple-element.16), channel_id=1, source_target_pairs={{0,256},{256,0},{1,257},{257,1},{2,258},{258,2},{3,259},{259,3},{4... | collective-permute-start | bytes 786440 | tf_op jit(solution)/shard_map/ppermute | solution.py:358
  166.1 2.2 %collective-permute-start.1 = (bf16[5,32,128]{2,1,0:T(8,128)(2,1)S(1)}, bf16[5,32,128]{2,1,0:T(8,128)(2,1)S(1)}, u32[]{:S(2)}, u32[]{:S(2)}) collective-permute-start(bf16[5,32,128]{2,1,0:T(8,128)(2,1)S(1)} %get-tuple-element.15), channel_id=1, source_target_pairs={{0,256},{256,0},{1,257},{257,1},{2,258},{258,2},{3,259},{259,3},{4... | collective-permute-start | bytes 122888 | tf_op jit(solution)/shard_map/ppermute | solution.py:388
  168.2 4.7 %collective-permute-done.2.other_spec_ref = bf16[4,32,1024]{2,1,0:T(8,128)(2,1)S(1)} collective-permute-done((bf16[4,32,1024]{2,1,0:T(8,128)(2,1)S(1)}, bf16[4,32,1024]{2,1,0:T(8,128)(2,1)S(1)}, u32[]{:S(2)}, u32[]{:S(2)}) %collective-permute-start.2) | collective-permute-done | bytes 262176 | tf_op jit(solution)/shard_map/ppermute | solution.py:358
  172.9 0.6 collective-permute-done.1.other_grad_ref
  173.5 1.8 weight.1
  175.3 0.5 slice_bitcast_fusion
  175.8 2.9 %all-to-all-done.7 = bf16[32,16,128]{2,1,0:T(8,128)(2,1)S(1)} async-done(((bf16[32,16,128]{2,1,0:T(8,128)(2,1)}), bf16[32,16,128]{2,1,0:T(8,128)(2,1)S(1)}, u32[]{:S(2)}, u32[]{:S(2)}) %all-to-all-start.7) | async-done | bytes 131104 | tf_op jit(solution)/shard_map/all_to_all | solution.py:303
  178.7 0.0 copy-done.1
  178.7 0.0 copy-done.6
  178.7 1.2 finish.1
Async XLA Ops:
  0.6 59.2 %copy-start.4 = (bf16[512,512]{1,0:T(8,128)(2,1)S(1)}, bf16[512,512]{1,0:T(8,128)(2,1)}, u32[]{:S(2)}) copy-start(bf16[512,512]{1,0:T(8,128)(2,1)} %constant.17.clone.g_ref) | copy-start | bytes 1572868
  0.6 21.7 %copy-start = (bf16[4,2,64,1024]{3,2,1,0:T(8,128)(2,1)S(1)}, bf16[4,2,64,1024]{3,2,1,0:T(8,128)(2,1)}, u32[]{:S(2)}) copy-start(bf16[4,2,64,1024]{3,2,1,0:T(8,128)(2,1)} %param.11) | copy-start | bytes 3145732
  4.3 55.4 %all-to-all-start = ((bf16[32,80,128]{2,1,0:T(8,128)(2,1)}), bf16[32,80,128]{2,1,0:T(8,128)(2,1)S(1)}, u32[]{:S(2)}, u32[]{:S(2)}) async-start(bf16[32,80,128]{2,1,0:T(8,128)(2,1)} %points.1), calls=%async_computation | async-start | bytes 1310720 | tf_op jit(solution)/shard_map/all_to_all | solution.py:303
  22.3 44.3 %collective-permute-start = (bf16[4,128,1024]{2,1,0:T(8,128)(2,1)S(1)}, bf16[4,128,1024]{2,1,0:T(8,128)(2,1)S(1)}, u32[]{:S(2)}, u32[]{:S(2)}) collective-permute-start(bf16[4,128,1024]{2,1,0:T(8,128)(2,1)S(1)} %bitcast.15), channel_id=1, source_target_pairs={{0,256},{256,0},{1,257},{257,1},{2,258},{258,2},{3,259},{259,3},{4... | collective-permute-start | bytes 3145736 | tf_op jit(solution)/shard_map/ppermute | solution.py:316
  60.8 18.4 %all-to-all-start.1 = ((bf16[16,8,128]{2,1,0:T(8,128)(2,1)}), bf16[16,8,128]{2,1,0:T(8,128)(2,1)S(1)}, u32[]{:S(2)}, u32[]{:S(2)}) async-start(bf16[16,8,128]{2,1,0:T(8,128)(2,1)} %bitcast.1), calls=%async_computation.1 | async-start | bytes 65536 | tf_op jit(solution)/shard_map/all_to_all | solution.py:303
  79.3 29.5 %copy-start.7 = (f32[64]{0:T(128)S(1)}, f32[64]{0:T(128)}, u32[]{:S(2)}) copy-start(f32[64]{0:T(128)} %param.12) | copy-start | bytes 772
  79.3 29.6 %copy-start.3 = (bf16[2,256,1024]{2,1,0:T(8,128)(2,1)S(1)}, bf16[2,256,1024]{2,1,0:T(8,128)(2,1)}, u32[]{:S(2)}) copy-start(bf16[2,256,1024]{2,1,0:T(8,128)(2,1)} %constant.19.clone.table_ref) | copy-start | bytes 3145732
  79.3 29.6 %copy-start.5 = (bf16[384,512]{1,0:T(8,128)(2,1)S(1)}, bf16[384,512]{1,0:T(8,128)(2,1)}, u32[]{:S(2)}) copy-start(bf16[384,512]{1,0:T(8,128)(2,1)} %constant.20.clone.e_ref) | copy-start | bytes 1179652
  110.7 45.2 %copy-start.2 = (bf16[1024,512]{1,0:T(8,128)(2,1)S(1)}, bf16[1024,512]{1,0:T(8,128)(2,1)}, u32[]{:S(2)}) copy-start(bf16[1024,512]{1,0:T(8,128)(2,1)} %constant.18.clone.u_ref) | copy-start | bytes 3145732
  126.8 52.0 %copy-start.1 = (bf16[32,64,128]{2,1,0:T(8,128)(2,1)S(1)}, bf16[32,64,128]{2,1,0:T(8,128)(2,1)}, u32[]{:S(2)}) copy-start(bf16[32,64,128]{2,1,0:T(8,128)(2,1)} %cot_ref.3) | copy-start | bytes 1572868
  126.8 52.0 %copy-start.6 = (bf16[64,128]{1,0:T(8,128)(2,1)S(1)}, bf16[64,128]{1,0:T(8,128)(2,1)}, u32[]{:S(2)}) copy-start(bf16[64,128]{1,0:T(8,128)(2,1)} %constant.16.clone.v_ref) | copy-start | bytes 49156
  157.0 21.7 %all-to-all-start.7 = ((bf16[32,16,128]{2,1,0:T(8,128)(2,1)}), bf16[32,16,128]{2,1,0:T(8,128)(2,1)S(1)}, u32[]{:S(2)}, u32[]{:S(2)}) async-start(bf16[32,16,128]{2,1,0:T(8,128)(2,1)} %bitcast.10), calls=%async_computation.7 | async-start | bytes 262144 | tf_op jit(solution)/shard_map/all_to_all | solution.py:303
  160.9 12.0 %collective-permute-start.2 = (bf16[4,32,1024]{2,1,0:T(8,128)(2,1)S(1)}, bf16[4,32,1024]{2,1,0:T(8,128)(2,1)S(1)}, u32[]{:S(2)}, u32[]{:S(2)}) collective-permute-start(bf16[4,32,1024]{2,1,0:T(8,128)(2,1)S(1)} %get-tuple-element.16), channel_id=1, source_target_pairs={{0,256},{256,0},{1,257},{257,1},{2,258},{258,2},{3,259},{259,3},{4... | collective-permute-start | bytes 786440 | tf_op jit(solution)/shard_map/ppermute | solution.py:358
  166.1 7.4 %collective-permute-start.1 = (bf16[5,32,128]{2,1,0:T(8,128)(2,1)S(1)}, bf16[5,32,128]{2,1,0:T(8,128)(2,1)S(1)}, u32[]{:S(2)}, u32[]{:S(2)}) collective-permute-start(bf16[5,32,128]{2,1,0:T(8,128)(2,1)S(1)} %get-tuple-element.15), channel_id=1, source_target_pairs={{0,256},{256,0},{1,257},{257,1},{2,258},{258,2},{3,259},{259,3},{4... | collective-permute-start | bytes 122888 | tf_op jit(solution)/shard_map/ppermute | solution.py:388
